TPU v7x, 32 devices: a whole 2x2x4 slice. The times are simulated.
32 devices in a mesh: orient: 8 (over y, x, core), slab: 4 (over z).
Axes of the slice: x: 2, y: 2, z: 4, core: 2. Of those that a mesh axis runs over, the one named last changes fastest.
Arguments:
- images: bfloat16 [12288, 8192], P(('orient', 'slab')), may hold values from -20 to 20
- bucket: int32 [12288, 1], P(('orient', 'slab')), may hold values from 0 to 7; in each aligned block of 384 rows (0 to 383, 384 to 767, ...) at most 96 rows name the same one
- panels: bfloat16 [8, 512, 8192], P('orient'), may hold values from -6 to 6
- tile_slab: int32 [8, 64], replicated, may hold values from 0 to 3, as said below
- tile_row: int32 [8, 64], replicated, may hold values from 0 to 248
Outputs:
- volume: float32 [1024, 8192], P('slab', 'orient')
- loglik: float32 [12288], P(('orient', 'slab'))
Inputs may be any that keep to these rules, and one draw needn't show every extreme that they name: Among the rows of one device, at most 96 particles name one bucket, a bound that some block reaches. `tile_slab`: for every bucket, at most 24 of its tiles name one slab, and some slab is named by exactly 24 of them.
All inputs are finite; a program needn't handle non-finite values.
Results may differ from a plain program's by a relative error of at most 0.0038.
Values may be sent and summed in bfloat16 or wider, within the bound.
No kernel may reach another device: no remote copies, remote signals or barrier semaphores. Data moves between devices by JAX's collectives and lax.ppermute only.
A program may use at most 128 MiB of HBM per device.

v0:
```python
import math

import jax
import jax.numpy as jnp
from jax import lax
from jax.sharding import PartitionSpec as P

G = 8
SLAB_ROWS = 256


BETA = 2.0


def slot_table(labels, groups, capacity):
    total_rows = labels.shape[0]
    onehot = (labels[:, None] == jnp.arange(groups, dtype=jnp.int32)[None, :]).astype(jnp.int32)
    ordinal = jnp.sum((jnp.cumsum(onehot, axis=0) - 1) * onehot, axis=1)
    matches = onehot[:, :, None] * (
        ordinal[:, None, None] == jnp.arange(capacity, dtype=jnp.int32)[None, None, :]
    ).astype(jnp.int32)
    sources = jnp.sum(matches * jnp.arange(total_rows, dtype=jnp.int32)[:, None, None], axis=0)
    filled = jnp.sum(matches, axis=0)
    return (sources, filled, matches)


def body(images, bucket, panels, tile_slab, tile_row):
    orient_count = lax.axis_size("orient")
    slab_count = lax.axis_size("slab")
    per_device = images.shape[0]
    window = images.shape[1]
    capacity = 2 * per_device // orient_count
    sources, filled, matches = slot_table(bucket[:, 0], orient_count, capacity)
    outgoing = jnp.where(filled[:, :, None] > 0, images[sources], jnp.zeros((), jnp.bfloat16))
    panel_rows = panels[0]
    orient_total = panel_rows.shape[0]
    score_scale = BETA / math.sqrt(window)
    arrived = lax.all_to_all(outgoing, "orient", split_axis=0, concat_axis=0, tiled=True)
    groups_in = arrived.shape[0]
    item_count = arrived.shape[1]
    flattened = arrived.reshape(groups_in * item_count, window)
    scores = (
        lax.dot_general(
            flattened, panel_rows, (((1,), (1,)), ((), ())), preferred_element_type=jnp.float32
        )
        * score_scale
    )
    largest = jnp.max(scores, axis=1, keepdims=True)
    exponent = jnp.exp(scores - largest)
    totals = jnp.sum(exponent, axis=1, keepdims=True)
    weights = (exponent / totals).astype(jnp.bfloat16)
    logsum = (largest + jnp.log(totals)).reshape(groups_in, item_count)
    returned = lax.all_to_all(logsum, "orient", split_axis=0, concat_axis=0, tiled=True)
    arrived, weights, returned = (
        arrived,
        weights.reshape(groups_in, item_count, orient_total),
        returned,
    )
    loglik = jnp.sum(matches.astype(jnp.float32) * returned[None, :, :], axis=(1, 2))
    partial_value = lax.dot_general(
        weights.reshape(-1, orient_total),
        arrived.reshape(-1, window),
        (((0,), (0,)), ((), ())),
        preferred_element_type=jnp.float32,
    ).astype(jnp.bfloat16)
    tiles_total = orient_total // G
    tile_block = partial_value.reshape(tiles_total, G, window)
    my_bucket = lax.axis_index("orient")
    here_slab = lax.axis_index("slab")
    my_slabs = tile_slab[my_bucket]
    tile_cap = tiles_total // slab_count + tiles_total // (2 * slab_count)
    tile_source, tile_filled, tile_matches = slot_table(my_slabs, slab_count, tile_cap)
    packed = jnp.where(
        tile_filled[:, :, None, None] > 0, tile_block[tile_source], jnp.zeros((), jnp.bfloat16)
    )
    offsets = jnp.arange(G, dtype=jnp.int32)
    landed = lax.all_to_all(packed, "slab", split_axis=0, concat_axis=0, tiled=True)
    merged = jnp.sum(landed, axis=0, dtype=jnp.float32)
    slot_tiles = jnp.take(tile_source, here_slab, axis=0)
    starts = jnp.take(tile_row[my_bucket], slot_tiles)
    targets = starts[:, None] + offsets
    local_volume = (
        jnp.zeros((SLAB_ROWS, window), jnp.float32)
        .at[targets.reshape(-1)]
        .add(merged.reshape(-1, window))
    )
    volume = lax.psum_scatter(local_volume, "orient", scatter_dimension=1, tiled=True)
    return (volume, loglik)


def solution(mesh):
    in_specs = (
        P(("orient", "slab"), None),
        P(("orient", "slab"), None),
        P("orient", None, None),
        P(),
        P(),
    )
    out_specs = (P("slab", "orient"), P(("orient", "slab")))
    return jax.shard_map(body, mesh=mesh, in_specs=in_specs, out_specs=out_specs, check_vma=False)
```

profile of v0, /device:TPU:2, one launch (start us, length us, event | category | flops | bytes accessed | tf_op | source)
XLA Modules:
  0.0 616.2 jit_solution(7700728576357316190)
XLA Ops:
  7.2 0.7 reduce
  7.9 0.9 reduce-window.6
  8.8 0.2 slice_reduce_fusion
  9.0 0.1 fusion.18
  9.1 0.4 multiply_reduce_fusion
  9.6 25.6 %gather_fusion.1 = bf16[768,8192]{1,0:T(8,128)(2,1)} fusion(bf16[384,8192]{1,0:T(8,128)(2,1)} %param.5, s32[1024]{0:T(1024)S(1)} %pad_clamp_fusion.1), kind=kCustom, calls=%fused_computation.1 | custom fusion | bytes 25168896 | tf_op jit(solution)/shard_map/gather | solution.py:34
  35.2 10.7 %broadcast_select_fusion = bf16[8,96,8192]{2,1,0:T(8,128)(2,1)} fusion(bf16[8,96,8192]{2,1,0:T(8,128)(2,1)} %bitcast.46, pred[8,96]{1,0:T(8,128)(4,1)S(1)} %broadcast_compare_fusion), kind=kLoop, calls=%fused_computation.5 | loop fusion | flops 6291456 | bytes 25166592 | tf_op jit(solution)/shard_map/jit(_where)/select_n | solution.py:34
  45.8 5.5 all-to-all-start
  51.3 0.7 fusion.22
  52.0 0.1 fusion.17
  52.1 0.1 copy.9
  52.2 0.1 reduce_window_sum.24
  52.3 0.2 select_reduce_fusion
  52.5 0.2 multiply_reduce_fusion.1
  52.7 0.1 reshape.311
  52.8 135.8 %all-to-all-done = bf16[8,96,8192]{2,1,0:T(8,128)(2,1)} async-done(((bf16[8,96,8192]{2,1,0:T(8,128)(2,1)}), bf16[8,96,8192]{2,1,0:T(8,128)(2,1)}, u32[]{:S(2)}, u32[]{:S(2)}) %all-to-all-start) | async-done | bytes 12582944 | tf_op jit(solution)/shard_map/all_to_all | solution.py:38
  188.6 12.0 %fusion.25 = (f32[768]{0:T(1024)S(1)}, f32[768,512]{0,1:T(8,128)S(1)}) fusion(bf16[768,8192]{1,0:T(8,128)(2,1)} %bitcast.10, bf16[1,512,8192]{2,1,0:T(8,128)(2,1)} %param.7), kind=kOutput, calls=%fused_computation.63 | convolution fusion | flops 6443236352 | bytes 22547456 | tf_op jit(solution)/shard_map/dot_general | solution.py:43
  200.6 0.3 fusion.9
  200.9 13.4 %fusion = bf16[64,8,8192]{2,1,0:T(8,128)(2,1)} fusion(bf16[768,8192]{1,0:T(8,128)(2,1)} %bitcast.10, f32[768,512]{0,1:T(8,128)S(1)} %get-tuple-element.18, f32[768]{0:T(1024)S(1)} %fusion.9, f32[768]{0:T(1024)S(1)} %get-tuple-element.17), kind=kOutput, calls=%fused_computation.8 | convolution fusion | flops 6447824896 | bytes 22550528 | tf_op jit(solution)/shard_map/dot_general | solution.py:60
  214.3 10.2 %gather_fusion.2 = bf16[96,8,8192]{2,1,0:T(8,128)(2,1)} fusion(bf16[64,8,8192]{2,1,0:T(8,128)(2,1)} %fusion, s32[1024]{0:T(1024)S(1)} %pad_clamp_fusion), kind=kCustom, calls=%fused_computation.2 | custom fusion | bytes 25166208 | tf_op jit(solution)/shard_map/gather | solution.py:74
  224.5 10.7 %broadcast_select_fusion.1 = bf16[4,24,8,8192]{3,2,1,0:T(8,128)(2,1)} fusion(bf16[4,24,8,8192]{3,2,1,0:T(8,128)(2,1)} %bitcast.45, pred[4,24]{1,0:T(4,128)(4,1)S(1)} %broadcast_compare_fusion.1), kind=kLoop, calls=%fused_computation.6 | loop fusion | flops 6291456 | bytes 25165920 | tf_op jit(solution)/shard_map/jit(_where)/select_n | solution.py:73
  235.2 6.3 %all-to-all-start.1 = ((bf16[4,24,8,8192]{3,2,1,0:T(8,128)(2,1)}), bf16[4,24,8,8192]{3,2,1,0:T(8,128)(2,1)}, u32[]{:S(2)}, u32[]{:S(2)}) async-start(bf16[4,24,8,8192]{3,2,1,0:T(8,128)(2,1)} %broadcast_select_fusion.1), calls=%async_computation.1 | async-start | bytes 25165824 | tf_op jit(solution)/shard_map/all_to_all | solution.py:77
  241.6 0.3 reduce-scatter.2.cloned.1.call-start
  241.9 0.7 gather_fusion
  242.7 0.1 add.120
  242.8 272.9 %all-to-all-done.1 = bf16[4,24,8,8192]{3,2,1,0:T(8,128)(2,1)} async-done(((bf16[4,24,8,8192]{3,2,1,0:T(8,128)(2,1)}), bf16[4,24,8,8192]{3,2,1,0:T(8,128)(2,1)}, u32[]{:S(2)}, u32[]{:S(2)}) %all-to-all-start.1) | async-done | bytes 12582944 | tf_op jit(solution)/shard_map/all_to_all | solution.py:77
  515.7 10.2 %convert_reduce_fusion = f32[24,8,8192]{2,1,0:T(8,128)} fusion(bf16[4,24,8,8192]{3,2,1,0:T(8,128)(2,1)} %all-to-all-done.1), kind=kLoop, calls=%fused_computation.4 | loop fusion | flops 11010048 | bytes 18874368 | tf_op jit(solution)/shard_map/reduce_sum | solution.py:78
  525.9 14.1 %scatter_custom_fusion = f32[256,8192]{1,0:T(8,128)} fusion(s32[192]{0:T(256)S(1)} %bitcast.50, f32[24,8,8192]{2,1,0:T(8,128)} %convert_reduce_fusion, f32[]{:T(128)} %constant.25.clone.1), kind=kCustom, calls=%fused_computation.11 | custom fusion | flops 1572864 | bytes 14680068 | tf_op jit(solution)/shard_map/scatter-add | solution.py:85
  540.0 0.1 add.128
  540.1 6.3 %all_to_all.16 = f32[8,1,96]{2,1,0:T(1,128)S(1)} all-to-all(f32[8,1,96]{2,1,0:T(1,128)S(1)} %add.128), channel_id=1, replica_groups=mesh['orient'=8,'slab'=4] {'orient'}, dimensions={0} | all-to-all | bytes 6144 | tf_op jit(solution)/shard_map/all_to_all | solution.py:53
  546.4 0.8 fusion.12
  547.2 62.2 %reduce-scatter.2.cloned.1.call-done = f32[256,1024]{1,0:T(8,128)} async-done(((f32[256,8192]{1,0:T(8,128)}), f32[256,1024]{1,0:T(8,128)}) %reduce-scatter.2.cloned.1.call-update) | async-done | bytes 1048592 | tf_op jit(solution)/shard_map/reduce_scatter | solution.py:87
  (19 shorter events, 0.3 us)
Async XLA Ops:
  45.8 142.7 %all-to-all-start = ((bf16[8,96,8192]{2,1,0:T(8,128)(2,1)}), bf16[8,96,8192]{2,1,0:T(8,128)(2,1)}, u32[]{:S(2)}, u32[]{:S(2)}) async-start(bf16[8,96,8192]{2,1,0:T(8,128)(2,1)} %broadcast_select_fusion), calls=%async_computation | async-start | bytes 25165824 | tf_op jit(solution)/shard_map/all_to_all | solution.py:38
  235.2 280.4 %all-to-all-start.1 = ((bf16[4,24,8,8192]{3,2,1,0:T(8,128)(2,1)}), bf16[4,24,8,8192]{3,2,1,0:T(8,128)(2,1)}, u32[]{:S(2)}, u32[]{:S(2)}) async-start(bf16[4,24,8,8192]{3,2,1,0:T(8,128)(2,1)} %broadcast_select_fusion.1), calls=%async_computation.1 | async-start | bytes 25165824 | tf_op jit(solution)/shard_map/all_to_all | solution.py:77
  241.6 367.8 %reduce-scatter.2.cloned.1.call-start = ((), (), s32[]{:S(2)}) async-start(), calls=%async_computation.4 | async-start | bytes 9437184 | tf_op jit(solution)/shard_map/reduce_scatter | solution.py:87
Sparse Core Ops, SparseCore 0:
  540.1 69.1 reduce-scatter.1
where the time goes:
time: 618 us; the launch traced here: 616 us
  waiting for transfers between devices  471 us (76%)
  other arithmetic  49.6 us (8%)
  local copies, waits for them, and re-layouts  37.8 us (6%)
  matrix products  25.4 us (4%)
  between operations  14.2 us (2%)
  starting transfers between devices  12 us (2%)
  blocking collectives  6.29 us (1%)
    all_to_all x1, waiting for transfers between devices, body(): lax.all_to_all(packed, 'slab', split_axis=0, concat_axis=0, tiled=True)  273 us
    all_to_all x1, waiting for transfers between devices, body(): lax.all_to_all(outgoing, 'orient', split_axis=0, concat_axis=0, tiled=True)  136 us
    reduce_scatter x1, waiting for transfers between devices, body(): lax.psum_scatter(local_volume, 'orient', scatter_dimension=1, tiled=True)  62.2 us
    gather x1, local copies, waits for them, and re-layouts, body(): images[sources]  25.6 us
    scatter-add x1, other arithmetic, body(): local_volume = jnp.zeros((SLAB_ROWS, window), jnp.float32).at[targets.res...  14.1 us
    dot_general x1, matrix products, body(): lax.dot_general(weights.reshape(-1, orient_total), arrived.reshape(-1, wi...  13.4 us
  transfers between devices with their start and end apart: 3, of which 3 were waited for; matrix products, arithmetic and copies ran while one was open for 1% of the time, Pallas kernels for 0%

commit v1 on v0

v1 whole, which is shorter than its diff:
```python
import math

import jax
import jax.numpy as jnp
from jax import lax
from jax.sharding import PartitionSpec as P

G = 8
SLAB_ROWS = 256
BETA = 2.0
CHUNKS = 4


def slots(labels, groups, capacity):
    onehot = (labels[:, None] == jnp.arange(groups, dtype=jnp.int32)[None, :]).astype(jnp.int32)
    ordinal = jnp.sum((jnp.cumsum(onehot, axis=0) - 1) * onehot, axis=1)
    return labels * capacity + ordinal


def body(images, bucket, panels, tile_slab, tile_row):
    orient_count = lax.axis_size("orient")
    slab_count = lax.axis_size("slab")
    per_device, window = images.shape
    capacity = 2 * per_device // orient_count
    slot_total = orient_count * capacity
    panel = panels[0]
    orient_total = panel.shape[0]
    score_scale = BETA / math.sqrt(window)
    owned = window // orient_count
    piece = owned // CHUNKS
    width = window // CHUNKS

    slot_of = slots(bucket[:, 0], orient_count, capacity)
    place = (slot_of[None, :] == jnp.arange(slot_total, dtype=jnp.int32)[:, None])
    select = place.astype(jnp.bfloat16)

    scores = jnp.zeros((slot_total, orient_total), jnp.float32)
    arrived = []
    for j in range(CHUNKS):
        cols = slice(j * width, (j + 1) * width)
        outgoing = jnp.dot(select, images[:, cols], preferred_element_type=jnp.float32)
        outgoing = outgoing.astype(jnp.bfloat16).reshape(orient_count, capacity, width)
        got = lax.all_to_all(outgoing, "orient", split_axis=0, concat_axis=0, tiled=True)
        got = got.reshape(slot_total, width)
        arrived.append(got)
        scores = scores + lax.dot_general(
            got, panel[:, cols], (((1,), (1,)), ((), ())), preferred_element_type=jnp.float32
        )
    scores = scores * score_scale
    largest = jnp.max(scores, axis=1, keepdims=True)
    exponent = jnp.exp(scores - largest)
    totals = jnp.sum(exponent, axis=1, keepdims=True)
    weights = (exponent / totals).astype(jnp.bfloat16)
    logsum = (largest + jnp.log(totals)).reshape(orient_count, capacity)

    within = jnp.arange(G, dtype=jnp.int32)
    rows_total = slab_count * SLAB_ROWS
    targets = (tile_slab * SLAB_ROWS + tile_row)[:, :, None] + within
    targets = targets.reshape(-1)
    spread = (targets[None, :] == jnp.arange(rows_total, dtype=jnp.int32)[:, None]).astype(jnp.bfloat16)

    out = []
    for j in range(CHUNKS):
        parts = []
        for c in range(orient_count):
            begin = c * owned + j * piece
            block = arrived[begin // width][:, begin % width : begin % width + piece]
            parts.append(
                lax.dot_general(
                    weights, block, (((0,), (0,)), ((), ())), preferred_element_type=jnp.float32
                ).astype(jnp.bfloat16)
            )
        partial = jnp.stack(parts)
        landed = lax.all_to_all(partial, "orient", split_axis=0, concat_axis=0, tiled=True)
        landed = landed.reshape(orient_count * orient_total, piece)
        summed = jnp.dot(spread, landed, preferred_element_type=jnp.float32).astype(jnp.bfloat16)
        summed = summed.reshape(slab_count, SLAB_ROWS, piece)
        mine = lax.all_to_all(summed, "slab", split_axis=0, concat_axis=0, tiled=True)
        out.append(jnp.sum(mine, axis=0, dtype=jnp.float32))
    volume = jnp.concatenate(out, axis=1)

    returned = lax.all_to_all(logsum, "orient", split_axis=0, concat_axis=0, tiled=True)
    flat = returned.reshape(-1)
    loglik = jnp.sum(jnp.where(place, flat[:, None], 0.0), axis=0)
    return (volume, loglik)


def solution(mesh):
    in_specs = (
        P(("orient", "slab"), None),
        P(("orient", "slab"), None),
        P("orient", None, None),
        P(),
        P(),
    )
    out_specs = (P("slab", "orient"), P(("orient", "slab")))
    return jax.shard_map(body, mesh=mesh, in_specs=in_specs, out_specs=out_specs, check_vma=False)
```

time: 618 us -> 409 us (0.66); the launches traced: 616 us -> 401 us
  waiting for transfers between devices: 471 us -> 206 us
  matrix products: 25.4 us -> 121 us
  starting transfers between devices: 12 us -> 65.4 us
  other arithmetic: 49.6 us -> 6.25 us
  local copies, waits for them, and re-layouts: 37.8 us -> 1.65 us
  between operations: 14.2 us -> 1.22 us
  blocking collectives: 6.29 us -> 0 us
    all_to_all x1 -> x9, waiting for transfers between devices: 273 us -> 90.3 us  [the longest x4 49.9 us: body(): lax.all_to_all(partial, 'orient', split_axis=0, concat_axis=0, tiled=True)]
    dot_general x2 -> x44, matrix products: 25.4 us -> 121 us  [the longest x32 60.7 us: body(): lax.dot_general(weights, block, (((0,), (0,)), ((), ())), preferred_eleme...]
    reduce_scatter x1 -> x0, waiting for transfers between devices: 62.2 us -> none  [body(): lax.psum_scatter(local_volume, 'orient', scatter_dimension=1, tiled=True)]
    all_to_all x1 -> x9, starting transfers between devices: 6.33 us -> 43.4 us  [the longest x4 22.4 us: body(): lax.all_to_all(partial, 'orient', split_axis=0, concat_axis=0, tiled=True)]
    gather x3 -> x0, local copies, waits for them, and re-layouts: 36.5 us -> none  [the longest x1 25.6 us: body(): images[sources]]
    select_n x7 -> x0, other arithmetic: 21.4 us -> none  [the longest x1 10.7 us: body(): jnp.where(tile_filled[:, :, None, None] > 0, tile_block[tile_source], jnp...]
    all_to_all x1 -> x4, waiting for transfers between devices: 136 us -> 116 us  [body(): lax.all_to_all(outgoing, 'orient', split_axis=0, concat_axis=0, tiled=True)]
    all_to_all x1 -> x4, starting transfers between devices: 5.45 us -> 22 us  [body(): lax.all_to_all(outgoing, 'orient', split_axis=0, concat_axis=0, tiled=True)]
  transfers between devices with their start and end apart: 3 -> 13, of which waited for: 3 -> 13; matrix products, arithmetic and copies ran while one was open for 1% -> 25% of each run, Pallas kernels for 0% -> 0%
where the time goes in v1:
time: 409 us; the launch traced here: 401 us
  waiting for transfers between devices  206 us (50%)
  matrix products  121 us (30%)
  starting transfers between devices  65.4 us (16%)
  other arithmetic  6.25 us (2%)
    all_to_all x4, waiting for transfers between devices, body(): lax.all_to_all(outgoing, 'orient', split_axis=0, concat_axis=0, tiled=True)  116 us
    dot_general x32, matrix products, body(): lax.dot_general(weights, block, (((0,), (0,)), ((), ())), preferred_eleme...  60.7 us
    all_to_all x4, waiting for transfers between devices, body(): lax.all_to_all(partial, 'orient', split_axis=0, concat_axis=0, tiled=True)  49.9 us
    all_to_all x4, waiting for transfers between devices, body(): lax.all_to_all(summed, 'slab', split_axis=0, concat_axis=0, tiled=True)  39.5 us
    all_to_all x4, starting transfers between devices, body(): lax.all_to_all(partial, 'orient', split_axis=0, concat_axis=0, tiled=True)  22.4 us
    all_to_all x4, starting transfers between devices, body(): lax.all_to_all(outgoing, 'orient', split_axis=0, concat_axis=0, tiled=True)  22 us
    dot_general x4, matrix products, body(): lax.dot_general(got, panel[:, cols], (((1,), (1,)), ((), ())), preferred_...  21.4 us
    dot_general x4, matrix products, body(): jnp.dot(select, images[:, cols], preferred_element_type=jnp.float32)  19.5 us
  transfers between devices with their start and end apart: 13, of which 13 were waited for; matrix products, arithmetic and copies ran while one was open for 25% of the time, Pallas kernels for 0%

profile of v1, /device:TPU:2, one launch (start us, length us, event | category | flops | bytes accessed | tf_op | source)
XLA Modules:
  0.0 401.0 jit_solution(4893155789295694824)
XLA Ops:
  2.6 4.9 %convolution_convert_fusion.1 = bf16[768,2048]{1,0:T(8,128)(2,1)} fusion(bf16[384,8192]{1,0:T(8,128)(2,1)} %param.5, s32[384]{0:T(512)S(1)} %multiply_add_fusion.1), kind=kOutput, calls=%fused_computation.10 | convolution fusion | flops 1209827328 | bytes 4720128 | tf_op jit(solution)/shard_map/dot_general | solution.py:41
  11.7 4.9 %convolution_convert_fusion.2 = bf16[768,2048]{1,0:T(8,128)(2,1)} fusion(bf16[384,8192]{1,0:T(8,128)(2,1)} %param.5, s32[384]{0:T(512)S(1)} %multiply_add_fusion.1), kind=kOutput, calls=%fused_computation.11 | convolution fusion | flops 1209827328 | bytes 4720128 | tf_op jit(solution)/shard_map/dot_general | solution.py:41
  16.6 31.5 %all-to-all-done.2 = bf16[8,96,2048]{2,1,0:T(8,128)(2,1)S(1)} async-done(((bf16[8,96,2048]{2,1,0:T(8,128)(2,1)}), bf16[8,96,2048]{2,1,0:T(8,128)(2,1)S(1)}, u32[]{:S(2)}, u32[]{:S(2)}) %all-to-all-start.2) | async-done | bytes 3145760 | tf_op jit(solution)/shard_map/all_to_all | solution.py:43
  48.1 5.8 %all-to-all-start.1 = ((bf16[8,96,2048]{2,1,0:T(8,128)(2,1)}), bf16[8,96,2048]{2,1,0:T(8,128)(2,1)}, u32[]{:S(2)}, u32[]{:S(2)}) async-start(bf16[8,96,2048]{2,1,0:T(8,128)(2,1)} %bitcast.203), calls=%async_computation.1 | async-start | bytes 6291456 | tf_op jit(solution)/shard_map/all_to_all | solution.py:43
  53.9 4.9 %convolution_convert_fusion = bf16[768,2048]{1,0:T(8,128)(2,1)} fusion(bf16[384,8192]{1,0:T(8,128)(2,1)} %param.5, s32[384]{0:T(512)S(1)} %multiply_add_fusion.1), kind=kOutput, calls=%fused_computation.9 | convolution fusion | flops 1209827328 | bytes 4720128 | tf_op jit(solution)/shard_map/dot_general | solution.py:41
  58.8 31.6 %all-to-all-done.1 = bf16[8,96,2048]{2,1,0:T(8,128)(2,1)} async-done(((bf16[8,96,2048]{2,1,0:T(8,128)(2,1)}), bf16[8,96,2048]{2,1,0:T(8,128)(2,1)}, u32[]{:S(2)}, u32[]{:S(2)}) %all-to-all-start.1) | async-done | bytes 3145760 | tf_op jit(solution)/shard_map/all_to_all | solution.py:43
  90.4 5.8 %all-to-all-start.3 = ((bf16[8,96,2048]{2,1,0:T(8,128)(2,1)}), bf16[8,96,2048]{2,1,0:T(8,128)(2,1)}, u32[]{:S(2)}, u32[]{:S(2)}) async-start(bf16[8,96,2048]{2,1,0:T(8,128)(2,1)} %bitcast.204), calls=%async_computation.3 | async-start | bytes 6291456 | tf_op jit(solution)/shard_map/all_to_all | solution.py:43
  96.3 4.8 %convolution_convert_fusion.3 = bf16[768,2048]{1,0:T(8,128)(2,1)} fusion(bf16[384,8192]{1,0:T(8,128)(2,1)} %param.5, s32[384]{0:T(512)S(1)} %multiply_add_fusion.1), kind=kOutput, calls=%fused_computation.12 | convolution fusion | flops 1209827328 | bytes 4720128 | tf_op jit(solution)/shard_map/dot_general | solution.py:41
  101.1 31.7 %all-to-all-done.3 = bf16[8,96,2048]{2,1,0:T(8,128)(2,1)} async-done(((bf16[8,96,2048]{2,1,0:T(8,128)(2,1)}), bf16[8,96,2048]{2,1,0:T(8,128)(2,1)}, u32[]{:S(2)}, u32[]{:S(2)}) %all-to-all-start.3) | async-done | bytes 3145760 | tf_op jit(solution)/shard_map/all_to_all | solution.py:43
  132.8 6.1 %all-to-all-start = ((bf16[8,96,2048]{2,1,0:T(8,128)(2,1)}), bf16[8,96,2048]{2,1,0:T(8,128)(2,1)}, u32[]{:S(2)}, u32[]{:S(2)}) async-start(bf16[8,96,2048]{2,1,0:T(8,128)(2,1)} %bitcast.202), calls=%async_computation | async-start | bytes 6291456 | tf_op jit(solution)/shard_map/all_to_all | solution.py:43
  138.9 4.6 %fusion.10 = f32[768,512]{0,1:T(8,128)} fusion(bf16[768,2048]{1,0:T(8,128)(2,1)S(1)} %bitcast.193, bf16[512,8192]{1,0:T(8,128)(2,1)} %bitcast.212), kind=kOutput, calls=%fused_computation.15 | convolution fusion | flops 1610612736 | bytes 6815744 | tf_op jit(solution)/shard_map/dot_general | solution.py:46
  143.4 5.5 %fusion.12 = f32[768,512]{0,1:T(8,128)} fusion(bf16[768,2048]{1,0:T(8,128)(2,1)} %bitcast.6, bf16[512,8192]{1,0:T(8,128)(2,1)} %bitcast.213), kind=kOutput, calls=%fused_computation.17 | convolution fusion | flops 1610612736 | bytes 6815744 | tf_op jit(solution)/shard_map/dot_general | solution.py:46
  149.0 5.6 %fusion.8 = f32[768,512]{0,1:T(8,128)} fusion(bf16[768,2048]{1,0:T(8,128)(2,1)} %bitcast.10, bf16[512,8192]{1,0:T(8,128)(2,1)} %bitcast.214), kind=kOutput, calls=%fused_computation.13 | convolution fusion | flops 1610612736 | bytes 6815744 | tf_op jit(solution)/shard_map/dot_general | solution.py:46
  154.5 20.8 %all-to-all-done = bf16[8,96,2048]{2,1,0:T(8,128)(2,1)} async-done(((bf16[8,96,2048]{2,1,0:T(8,128)(2,1)}), bf16[8,96,2048]{2,1,0:T(8,128)(2,1)}, u32[]{:S(2)}, u32[]{:S(2)}) %all-to-all-start) | async-done | bytes 3145760 | tf_op jit(solution)/shard_map/all_to_all | solution.py:43
  175.3 5.7 %fusion.129 = (f32[768]{0:T(1024)S(1)}, f32[768,512]{0,1:T(8,128)S(1)}) fusion(f32[768,512]{0,1:T(8,128)} %fusion.8, f32[768,512]{0,1:T(8,128)} %fusion.10, f32[768,512]{0,1:T(8,128)} %fusion.12, bf16[768,2048]{1,0:T(8,128)(2,1)} %bitcast.3, bf16[512,8192]{1,0:T(8,128)(2,1)} %bitcast.215), kind=kOutput, calls=%fused_computation.182 | convolution fusion | flops 1612578048 | bytes 11537408 | tf_op jit(solution)/shard_map/dot_general | solution.py:46
  195.1 4.7 %all-to-all-start.12 = ((f32[8,1,96]{2,1,0:T(1,128)}), f32[8,1,96]{2,1,0:T(1,128)S(1)}, u32[]{:S(2)}, u32[]{:S(2)}) async-start(f32[8,1,96]{2,1,0:T(1,128)} %add.68), calls=%async_computation.12 | async-start | bytes 8192 | tf_op jit(solution)/shard_map/all_to_all | solution.py:82
  203.1 5.7 %all-to-all-start.4 = ((bf16[8,512,256]{2,1,0:T(8,128)(2,1)}), bf16[8,512,256]{2,1,0:T(8,128)(2,1)}, u32[]{:S(2)}, u32[]{:S(2)}) async-start(bf16[8,512,256]{2,1,0:T(8,128)(2,1)} %fusion.42), calls=%async_computation.4 | async-start | bytes 4194304 | tf_op jit(solution)/shard_map/all_to_all | solution.py:74
  223.9 10.1 %all-to-all-done.4 = bf16[8,512,256]{2,1,0:T(8,128)(2,1)} async-done(((bf16[8,512,256]{2,1,0:T(8,128)(2,1)}), bf16[8,512,256]{2,1,0:T(8,128)(2,1)}, u32[]{:S(2)}, u32[]{:S(2)}) %all-to-all-start.4) | async-done | bytes 2097184 | tf_op jit(solution)/shard_map/all_to_all | solution.py:74
  234.0 6.0 %all-to-all-start.6 = ((bf16[8,512,256]{2,1,0:T(8,128)(2,1)}), bf16[8,512,256]{2,1,0:T(8,128)(2,1)}, u32[]{:S(2)}, u32[]{:S(2)}) async-start(bf16[8,512,256]{2,1,0:T(8,128)(2,1)} %fusion.58), calls=%async_computation.6 | async-start | bytes 4194304 | tf_op jit(solution)/shard_map/all_to_all | solution.py:74
  255.3 10.0 %all-to-all-done.6 = bf16[8,512,256]{2,1,0:T(8,128)(2,1)} async-done(((bf16[8,512,256]{2,1,0:T(8,128)(2,1)}), bf16[8,512,256]{2,1,0:T(8,128)(2,1)}, u32[]{:S(2)}, u32[]{:S(2)}) %all-to-all-start.6) | async-done | bytes 2097184 | tf_op jit(solution)/shard_map/all_to_all | solution.py:74
  265.3 5.7 %all-to-all-start.8 = ((bf16[8,512,256]{2,1,0:T(8,128)(2,1)}), bf16[8,512,256]{2,1,0:T(8,128)(2,1)}, u32[]{:S(2)}, u32[]{:S(2)}) async-start(bf16[8,512,256]{2,1,0:T(8,128)(2,1)} %fusion.74), calls=%async_computation.8 | async-start | bytes 4194304 | tf_op jit(solution)/shard_map/all_to_all | solution.py:74
  286.2 10.1 %all-to-all-done.8 = bf16[8,512,256]{2,1,0:T(8,128)(2,1)} async-done(((bf16[8,512,256]{2,1,0:T(8,128)(2,1)}), bf16[8,512,256]{2,1,0:T(8,128)(2,1)}, u32[]{:S(2)}, u32[]{:S(2)}) %all-to-all-start.8) | async-done | bytes 2097184 | tf_op jit(solution)/shard_map/all_to_all | solution.py:74
  296.3 5.0 %all-to-all-start.10 = ((bf16[8,512,256]{2,1,0:T(8,128)(2,1)}), bf16[8,512,256]{2,1,0:T(8,128)(2,1)S(1)}, u32[]{:S(2)}, u32[]{:S(2)}) async-start(bf16[8,512,256]{2,1,0:T(8,128)(2,1)} %fusion.90), calls=%async_computation.10 | async-start | bytes 4194304 | tf_op jit(solution)/shard_map/all_to_all | solution.py:74
  301.6 5.1 %fusion.23 = bf16[1024,256]{1,0:T(8,128)(2,1)} fusion(bf16[4096,256]{1,0:T(8,128)(2,1)} %bitcast.19, s32[4096]{0:T(1024)S(1)} %add.62), kind=kOutput, calls=%fused_computation.29 | convolution fusion | flops 2151940096 | bytes 2637824 | tf_op jit(solution)/shard_map/dot_general | solution.py:76
  306.7 19.7 %all-to-all-done.10 = bf16[8,512,256]{2,1,0:T(8,128)(2,1)S(1)} async-done(((bf16[8,512,256]{2,1,0:T(8,128)(2,1)}), bf16[8,512,256]{2,1,0:T(8,128)(2,1)S(1)}, u32[]{:S(2)}, u32[]{:S(2)}) %all-to-all-start.10) | async-done | bytes 2097184 | tf_op jit(solution)/shard_map/all_to_all | solution.py:74
  326.4 4.9 %all-to-all-start.5 = ((bf16[4,256,256]{2,1,0:T(8,128)(2,1)}), bf16[4,256,256]{2,1,0:T(8,128)(2,1)S(1)}, u32[]{:S(2)}, u32[]{:S(2)}) async-start(bf16[4,256,256]{2,1,0:T(8,128)(2,1)} %bitcast.20), calls=%async_computation.5 | async-start | bytes 1048576 | tf_op jit(solution)/shard_map/all_to_all | solution.py:78
  331.3 5.2 %fusion.24 = bf16[1024,256]{1,0:T(8,128)(2,1)} fusion(bf16[4096,256]{1,0:T(8,128)(2,1)} %bitcast.29, s32[4096]{0:T(1024)S(1)} %add.62), kind=kOutput, calls=%fused_computation.30 | convolution fusion | flops 2151940096 | bytes 2637824 | tf_op jit(solution)/shard_map/dot_general | solution.py:76
  336.5 9.6 %all-to-all-done.5 = bf16[4,256,256]{2,1,0:T(8,128)(2,1)S(1)} async-done(((bf16[4,256,256]{2,1,0:T(8,128)(2,1)}), bf16[4,256,256]{2,1,0:T(8,128)(2,1)S(1)}, u32[]{:S(2)}, u32[]{:S(2)}) %all-to-all-start.5) | async-done | bytes 524320 | tf_op jit(solution)/shard_map/all_to_all | solution.py:78
  349.8 5.1 %fusion.25 = bf16[1024,256]{1,0:T(8,128)(2,1)} fusion(bf16[4096,256]{1,0:T(8,128)(2,1)} %bitcast.39, s32[4096]{0:T(1024)S(1)} %add.62), kind=kOutput, calls=%fused_computation.31 | convolution fusion | flops 2151940096 | bytes 2637824 | tf_op jit(solution)/shard_map/dot_general | solution.py:76
  354.9 8.8 %all-to-all-done.7 = bf16[4,256,256]{2,1,0:T(8,128)(2,1)S(1)} async-done(((bf16[4,256,256]{2,1,0:T(8,128)(2,1)}), bf16[4,256,256]{2,1,0:T(8,128)(2,1)S(1)}, u32[]{:S(2)}, u32[]{:S(2)}) %all-to-all-start.7) | async-done | bytes 524320 | tf_op jit(solution)/shard_map/all_to_all | solution.py:78
  371.5 10.5 %all-to-all-done.9 = bf16[4,256,256]{2,1,0:T(8,128)(2,1)} async-done(((bf16[4,256,256]{2,1,0:T(8,128)(2,1)}), bf16[4,256,256]{2,1,0:T(8,128)(2,1)}, u32[]{:S(2)}, u32[]{:S(2)}) %all-to-all-start.9) | async-done | bytes 524320 | tf_op jit(solution)/shard_map/all_to_all | solution.py:78
  388.8 10.6 %all-to-all-done.11 = bf16[4,256,256]{2,1,0:T(8,128)(2,1)S(1)} async-done(((bf16[4,256,256]{2,1,0:T(8,128)(2,1)}), bf16[4,256,256]{2,1,0:T(8,128)(2,1)S(1)}, u32[]{:S(2)}, u32[]{:S(2)}) %all-to-all-start.11) | async-done | bytes 524320 | tf_op jit(solution)/shard_map/all_to_all | solution.py:78
  (73 shorter events, 88.7 us)
Async XLA Ops:
  7.5 40.6 %all-to-all-start.2 = ((bf16[8,96,2048]{2,1,0:T(8,128)(2,1)}), bf16[8,96,2048]{2,1,0:T(8,128)(2,1)S(1)}, u32[]{:S(2)}, u32[]{:S(2)}) async-start(bf16[8,96,2048]{2,1,0:T(8,128)(2,1)} %bitcast.205), calls=%async_computation.2 | async-start | bytes 6291456 | tf_op jit(solution)/shard_map/all_to_all | solution.py:43
  48.1 42.3 %all-to-all-start.1 = ((bf16[8,96,2048]{2,1,0:T(8,128)(2,1)}), bf16[8,96,2048]{2,1,0:T(8,128)(2,1)}, u32[]{:S(2)}, u32[]{:S(2)}) async-start(bf16[8,96,2048]{2,1,0:T(8,128)(2,1)} %bitcast.203), calls=%async_computation.1 | async-start | bytes 6291456 | tf_op jit(solution)/shard_map/all_to_all | solution.py:43
  90.4 42.3 %all-to-all-start.3 = ((bf16[8,96,2048]{2,1,0:T(8,128)(2,1)}), bf16[8,96,2048]{2,1,0:T(8,128)(2,1)}, u32[]{:S(2)}, u32[]{:S(2)}) async-start(bf16[8,96,2048]{2,1,0:T(8,128)(2,1)} %bitcast.204), calls=%async_computation.3 | async-start | bytes 6291456 | tf_op jit(solution)/shard_map/all_to_all | solution.py:43
  132.8 42.5 %all-to-all-start = ((bf16[8,96,2048]{2,1,0:T(8,128)(2,1)}), bf16[8,96,2048]{2,1,0:T(8,128)(2,1)}, u32[]{:S(2)}, u32[]{:S(2)}) async-start(bf16[8,96,2048]{2,1,0:T(8,128)(2,1)} %bitcast.202), calls=%async_computation | async-start | bytes 6291456 | tf_op jit(solution)/shard_map/all_to_all | solution.py:43
  181.6 10.8 %copy-start = (bf16[768,512]{0,1:T(8,128)(2,1)}, bf16[768,512]{0,1:T(8,128)(2,1)S(1)}, u32[]{:S(2)}) copy-start(bf16[768,512]{0,1:T(8,128)(2,1)S(1)} %divide_convert_fusion) | copy-start | bytes 2359300
  195.1 8.0 %all-to-all-start.12 = ((f32[8,1,96]{2,1,0:T(1,128)}), f32[8,1,96]{2,1,0:T(1,128)S(1)}, u32[]{:S(2)}, u32[]{:S(2)}) async-start(f32[8,1,96]{2,1,0:T(1,128)} %add.68), calls=%async_computation.12 | async-start | bytes 8192 | tf_op jit(solution)/shard_map/all_to_all | solution.py:82
  203.1 31.0 %all-to-all-start.4 = ((bf16[8,512,256]{2,1,0:T(8,128)(2,1)}), bf16[8,512,256]{2,1,0:T(8,128)(2,1)}, u32[]{:S(2)}, u32[]{:S(2)}) async-start(bf16[8,512,256]{2,1,0:T(8,128)(2,1)} %fusion.42), calls=%async_computation.4 | async-start | bytes 4194304 | tf_op jit(solution)/shard_map/all_to_all | solution.py:74
  208.8 4.7 %copy-start.1 = (bf16[768,512]{0,1:T(8,128)(2,1)S(1)}, bf16[768,512]{0,1:T(8,128)(2,1)}, u32[]{:S(2)}) copy-start(bf16[768,512]{0,1:T(8,128)(2,1)} %copy-done) | copy-start | bytes 2359300
  234.0 31.2 %all-to-all-start.6 = ((bf16[8,512,256]{2,1,0:T(8,128)(2,1)}), bf16[8,512,256]{2,1,0:T(8,128)(2,1)}, u32[]{:S(2)}, u32[]{:S(2)}) async-start(bf16[8,512,256]{2,1,0:T(8,128)(2,1)} %fusion.58), calls=%async_computation.6 | async-start | bytes 4194304 | tf_op jit(solution)/shard_map/all_to_all | solution.py:74
  240.0 4.7 %copy-start.2 = (bf16[768,512]{0,1:T(8,128)(2,1)S(1)}, bf16[768,512]{0,1:T(8,128)(2,1)}, u32[]{:S(2)}) copy-start(bf16[768,512]{0,1:T(8,128)(2,1)} %copy-done) | copy-start | bytes 2359300
  265.3 31.0 %all-to-all-start.8 = ((bf16[8,512,256]{2,1,0:T(8,128)(2,1)}), bf16[8,512,256]{2,1,0:T(8,128)(2,1)}, u32[]{:S(2)}, u32[]{:S(2)}) async-start(bf16[8,512,256]{2,1,0:T(8,128)(2,1)} %fusion.74), calls=%async_computation.8 | async-start | bytes 4194304 | tf_op jit(solution)/shard_map/all_to_all | solution.py:74
  271.0 4.7 %copy-start.3 = (bf16[768,512]{0,1:T(8,128)(2,1)S(1)}, bf16[768,512]{0,1:T(8,128)(2,1)}, u32[]{:S(2)}) copy-start(bf16[768,512]{0,1:T(8,128)(2,1)} %copy-done) | copy-start | bytes 2359300
  286.2 15.1 %copy-start.4 = (s32[8,64]{1,0:T(8,128)S(1)}, s32[8,64]{1,0:T(8,128)}, u32[]{:S(2)}) copy-start(s32[8,64]{1,0:T(8,128)} %param.9) | copy-start | bytes 6148
  286.2 15.1 %copy-start.5 = (s32[8,64]{1,0:T(8,128)S(1)}, s32[8,64]{1,0:T(8,128)}, u32[]{:S(2)}) copy-start(s32[8,64]{1,0:T(8,128)} %param.8) | copy-start | bytes 6148
  296.3 30.2 %all-to-all-start.10 = ((bf16[8,512,256]{2,1,0:T(8,128)(2,1)}), bf16[8,512,256]{2,1,0:T(8,128)(2,1)S(1)}, u32[]{:S(2)}, u32[]{:S(2)}) async-start(bf16[8,512,256]{2,1,0:T(8,128)(2,1)} %fusion.90), calls=%async_computation.10 | async-start | bytes 4194304 | tf_op jit(solution)/shard_map/all_to_all | solution.py:74
  326.4 19.6 %all-to-all-start.5 = ((bf16[4,256,256]{2,1,0:T(8,128)(2,1)}), bf16[4,256,256]{2,1,0:T(8,128)(2,1)S(1)}, u32[]{:S(2)}, u32[]{:S(2)}) async-start(bf16[4,256,256]{2,1,0:T(8,128)(2,1)} %bitcast.20), calls=%async_computation.5 | async-start | bytes 1048576 | tf_op jit(solution)/shard_map/all_to_all | solution.py:78
  346.0 17.7 %all-to-all-start.7 = ((bf16[4,256,256]{2,1,0:T(8,128)(2,1)}), bf16[4,256,256]{2,1,0:T(8,128)(2,1)S(1)}, u32[]{:S(2)}, u32[]{:S(2)}) async-start(bf16[4,256,256]{2,1,0:T(8,128)(2,1)} %bitcast.209), calls=%async_computation.7 | async-start | bytes 1048576 | tf_op jit(solution)/shard_map/all_to_all | solution.py:78
  363.8 18.2 %all-to-all-start.9 = ((bf16[4,256,256]{2,1,0:T(8,128)(2,1)}), bf16[4,256,256]{2,1,0:T(8,128)(2,1)}, u32[]{:S(2)}, u32[]{:S(2)}) async-start(bf16[4,256,256]{2,1,0:T(8,128)(2,1)} %bitcast.208), calls=%async_computation.9 | async-start | bytes 1048576 | tf_op jit(solution)/shard_map/all_to_all | solution.py:78
  382.0 17.4 %all-to-all-start.11 = ((bf16[4,256,256]{2,1,0:T(8,128)(2,1)}), bf16[4,256,256]{2,1,0:T(8,128)(2,1)S(1)}, u32[]{:S(2)}, u32[]{:S(2)}) async-start(bf16[4,256,256]{2,1,0:T(8,128)(2,1)} %bitcast.207), calls=%async_computation.11 | async-start | bytes 1048576 | tf_op jit(solution)/shard_map/all_to_all | solution.py:78

commit v2 on v1

v2 whole, which is shorter than its diff:
```python
import functools
import math

import jax
import jax.numpy as jnp
from jax import lax
from jax.experimental import pallas as pl
from jax.experimental.pallas import tpu as pltpu
from jax.sharding import PartitionSpec as P

G = 8
SLAB_ROWS = 256
BETA = 2.0
F32 = jnp.float32
BF16 = jnp.bfloat16
VMEM_LIMIT = 48 * 1024 * 1024


def slots(labels, groups, capacity):
    onehot = (labels[:, None] == jnp.arange(groups, dtype=jnp.int32)[None, :]).astype(jnp.int32)
    ordinal = jnp.sum((jnp.cumsum(onehot, axis=0) - 1) * onehot, axis=1)
    return labels * capacity + ordinal


def swap(x, axis, offset):
    count = lax.axis_size(axis)
    return lax.ppermute(x, axis, [(i, i ^ offset) for i in range(count)])


def call(kernel, name, grid, in_specs, out_specs, out_shape, scratch, flops, size):
    return pl.pallas_call(
        kernel,
        name=name,
        grid_spec=pltpu.PrefetchScalarGridSpec(
            num_scalar_prefetch=1,
            grid=grid,
            in_specs=in_specs,
            out_specs=out_specs,
            scratch_shapes=scratch,
        ),
        out_shape=out_shape,
        compiler_params=pltpu.CompilerParams(vmem_limit_bytes=VMEM_LIMIT),
        cost_estimate=pl.CostEstimate(flops=flops, bytes_accessed=size, transcendentals=0),
    )


def gather_kernel(offsets, capacity, owned, me_ref, slot_ref, images_ref, *rest):
    outs, select = rest[:-1], rest[-1]
    me = me_ref[0]

    @pl.when(pl.program_id(0) == 0)
    def _():
        row = lax.broadcasted_iota(jnp.int32, (capacity, slot_ref.shape[1]), 0)
        for n, offset in enumerate(offsets):
            hit = slot_ref[...] == row + (me ^ offset) * capacity
            select[n * capacity : (n + 1) * capacity, :] = hit.astype(BF16)

    for parity in range(2):
        members = [n for n, offset in enumerate(offsets) if offset & 1 == parity]
        if not members:
            continue
        rows = slice(members[0] * capacity, (members[-1] + 1) * capacity)
        for part in range(2):
            which = (me & 1) ^ parity ^ part
            block = images_ref[:, pl.ds(pl.multiple_of(which * owned, owned), owned)]
            found = jnp.dot(select[rows, :], block, preferred_element_type=F32).astype(BF16)
            for n in members:
                k = n - members[0]
                outs[2 * n + part][...] = found[k * capacity : (k + 1) * capacity]


def gather(offsets, me, slot_of, images, orient_count, capacity):
    offsets = sorted(offsets, key=lambda r: (r & 1, r))
    rows, window = images.shape
    owned = window // orient_count
    blocks = orient_count // 2
    shape = jax.ShapeDtypeStruct((capacity, window // 2), BF16)
    outs = call(
        functools.partial(gather_kernel, offsets, capacity, owned),
        "gather",
        (blocks,),
        [
            pl.BlockSpec((1, rows), lambda j, me: (0, 0)),
            pl.BlockSpec((rows, 2 * owned), lambda j, me: (0, j)),
        ],
        [pl.BlockSpec((capacity, owned), lambda j, me: (0, j))] * (2 * len(offsets)),
        [shape] * (2 * len(offsets)),
        [pltpu.VMEM((len(offsets) * capacity, rows), BF16)],
        2 * len(offsets) * capacity * rows * window,
        2 * window * (rows + len(offsets) * capacity),
    )(me, slot_of, images)
    return {(r, part): outs[2 * n + part] for n, r in enumerate(offsets) for part in range(2)}


def score_kernel(count, owned, scale, me_ref, panel_ref, *rest):
    rows, (weight_ref, logsum_ref, total) = rest[: 2 * count], rest[2 * count :]
    step = pl.program_id(0)
    low = me_ref[0] & 1
    found = None
    for part in range(2):
        block = jnp.concatenate([rows[2 * n + part][...] for n in range(count)], axis=0)
        which = low ^ part
        panel = panel_ref[:, pl.ds(pl.multiple_of(which * owned, owned), owned)]
        term = lax.dot_general(
            block, panel, (((1,), (1,)), ((), ())), preferred_element_type=F32
        )
        found = term if found is None else found + term

    @pl.when(step == 0)
    def _():
        total[...] = found

    @pl.when(step > 0)
    def _():
        total[...] += found

    @pl.when(step == pl.num_programs(0) - 1)
    def _():
        scores = total[...] * scale
        largest = jnp.max(scores, axis=1, keepdims=True)
        exponent = jnp.exp(scores - largest)
        totals = jnp.sum(exponent, axis=1, keepdims=True)
        weight_ref[...] = (exponent / totals).astype(BF16)
        logsum_ref[...] = largest + jnp.log(totals)


def score(me, panel, rows, orient_count, scale):
    count = len(rows) // 2
    orient_total, window = panel.shape
    owned = window // orient_count
    capacity = rows[0].shape[0]
    return call(
        functools.partial(score_kernel, count, owned, scale),
        "score",
        (orient_count // 2,),
        [pl.BlockSpec((orient_total, 2 * owned), lambda j, me: (0, j))]
        + [pl.BlockSpec((capacity, owned), lambda j, me: (0, j))] * len(rows),
        [
            pl.BlockSpec((count * capacity, orient_total), lambda j, me: (0, 0)),
            pl.BlockSpec((count * capacity, 1), lambda j, me: (0, 0)),
        ],
        [
            jax.ShapeDtypeStruct((count * capacity, orient_total), BF16),
            jax.ShapeDtypeStruct((count * capacity, 1), F32),
        ],
        [pltpu.VMEM((count * capacity, orient_total), F32)],
        2 * count * capacity * orient_total * window,
        2 * window * (orient_total + count * capacity),
    )(me, panel, *rows)


def mix_block(mix, rows, stacked):
    begin = 0
    for ref in rows:
        stacked[begin : begin + ref.shape[0], :] = ref[...]
        begin += ref.shape[0]
    return jnp.dot(mix, stacked[...], preferred_element_type=F32)


def send_kernel(groups, count, me_ref, wanted_ref, target_ref, *rest):
    weights, rows = rest[:groups], rest[groups : groups + count]
    out_ref, mix_ref, stacked, joined = rest[groups + count :]

    @pl.when(pl.program_id(0) == 0)
    def _():
        begin = 0
        for ref in weights:
            joined[begin : begin + ref.shape[0], :] = ref[...]
            begin += ref.shape[0]
        spread = (wanted_ref[...] == target_ref[...]).astype(BF16)
        mix_ref[...] = lax.dot_general(
            spread, joined[...], (((1,), (1,)), ((), ())), preferred_element_type=F32
        ).astype(BF16)

    out_ref[...] = mix_block(mix_ref[...], rows, stacked).astype(out_ref.dtype)


def mix_send(me, wanted, target, weights, rows, orient_count):
    volume_rows = wanted.shape[0]
    orient_total = target.shape[1]
    particles = sum(w.shape[0] for w in weights)
    half = rows[0].shape[1]
    blocks = orient_count // 2
    owned = half // blocks
    return call(
        functools.partial(send_kernel, len(weights), len(rows)),
        "mix_send",
        (blocks,),
        [
            pl.BlockSpec((volume_rows, 1), lambda j, me: (0, 0)),
            pl.BlockSpec((1, orient_total), lambda j, me: (0, 0)),
        ]
        + [pl.BlockSpec(w.shape, lambda j, me: (0, 0)) for w in weights]
        + [pl.BlockSpec((r.shape[0], owned), lambda j, me: (0, (me[0] >> 1) ^ j)) for r in rows],
        [
            pl.BlockSpec((volume_rows, owned), lambda j, me: (0, j)),
            pl.BlockSpec((volume_rows, particles), lambda j, me: (0, 0)),
        ],
        [
            jax.ShapeDtypeStruct((volume_rows, half), BF16),
            jax.ShapeDtypeStruct((volume_rows, particles), BF16),
        ],
        [pltpu.VMEM((particles, owned), BF16), pltpu.VMEM((particles, orient_total), BF16)],
        2 * volume_rows * particles * half,
        2 * half * (particles + volume_rows),
    )(me, wanted, target, *weights, *rows)


def keep_kernel(count, blocks, me_ref, mix_ref, got_ref, *rest):
    rows = rest[:count]
    upper_sent, upper_kept, lower_sent, lower_kept, stacked = rest[count:]
    step = pl.program_id(0)
    total = mix_block(mix_ref[...], rows, stacked) + got_ref[...].astype(F32)
    middle = total.shape[0] // 2
    upper, lower = total[:middle], total[middle:]

    @pl.when(step % 2 == 1)
    def _():
        upper_sent[step // 2] = upper.astype(BF16)

    @pl.when(step % 2 == 0)
    def _():
        upper_kept[step // 2] = upper

    @pl.when(step >= blocks // 2)
    def _():
        lower_sent[step % (blocks // 2)] = lower.astype(BF16)

    @pl.when(step < blocks // 2)
    def _():
        lower_kept[step % (blocks // 2)] = lower


def mix_keep(me, mix, first_row, got, rows, orient_count):
    particles = mix.shape[1]
    half = rows[0].shape[1]
    blocks = orient_count // 2
    owned = half // blocks
    place = first_row // SLAB_ROWS
    part = (blocks // 2, SLAB_ROWS // 2, owned)
    return call(
        functools.partial(keep_kernel, len(rows), blocks),
        "mix_keep",
        (blocks,),
        [
            pl.BlockSpec((SLAB_ROWS, particles), lambda j, me: (place, 0)),
            pl.BlockSpec((SLAB_ROWS, owned), lambda j, me: (place, j)),
        ]
        + [pl.BlockSpec((r.shape[0], owned), lambda j, me: (0, (me[0] >> 1) ^ j)) for r in rows],
        [pl.BlockSpec(part, lambda j, me: (0, 0, 0))] * 4,
        [jax.ShapeDtypeStruct(part, BF16), jax.ShapeDtypeStruct(part, F32)] * 2,
        [pltpu.VMEM((particles, owned), BF16)],
        2 * SLAB_ROWS * particles * half,
        2 * half * (particles + 2 * SLAB_ROWS),
    )(me, mix, got, *rows)


def reduce_chips(upper_sent, upper_kept, lower_sent, lower_kept, orient_count):
    bits = list(range(1, orient_count.bit_length() - 1))
    for n in range(len(bits)):
        upper = upper_kept + swap(upper_sent, "orient", 1 << bits[n]).astype(F32)
        lower = lower_kept + swap(lower_sent, "orient", 1 << bits[-1 - n]).astype(F32)
        left = upper.shape[0]
        upper_kept, upper_sent = upper[0::2], upper[1::2].astype(BF16)
        lower_kept, lower_sent = lower[: (left + 1) // 2], lower[(left + 1) // 2 :].astype(BF16)
    return jnp.concatenate([upper_kept[0], lower_kept[0]])


def body(images, bucket, panels, tile_slab, tile_row):
    orient_count = lax.axis_size("orient")
    slab_count = lax.axis_size("slab")
    me = lax.axis_index("orient")
    here = lax.axis_index("slab")
    me_ref = me.astype(jnp.int32).reshape(1)
    per_device, window = images.shape
    capacity = 2 * per_device // orient_count
    panel = panels[0]
    score_scale = BETA / math.sqrt(window)

    slot_of = slots(bucket[:, 0], orient_count, capacity)
    slot_row = slot_of[None, :]

    far = sorted(range(2, orient_count), key=lambda r: (-(r >> 1).bit_count(), r & 1, r))
    outgoing = gather(far[:2], me_ref, slot_row, images, orient_count, capacity)
    outgoing |= gather([0, 1] + far[2:], me_ref, slot_row, images, orient_count, capacity)
    arrived = {(0, part): outgoing[0, part] for part in range(2)}
    for offset in far[:2] + [1] + far[2:]:
        for part in range(2):
            arrived[offset, part] = swap(outgoing[offset, part], "orient", offset)

    order = [0, 1] + far
    weights, logsums = [], []
    for first in range(0, orient_count, 2):
        rows = [arrived[r, part] for r in order[first : first + 2] for part in range(2)]
        weight, logsum = score(me_ref, panel, rows, orient_count, score_scale)
        weights.append(weight)
        logsums.append(logsum.reshape(2, capacity))

    my_slab = lax.dynamic_index_in_dim(tile_slab, me, 0, keepdims=False)
    my_row = lax.dynamic_index_in_dim(tile_row, me, 0, keepdims=False)
    within = jnp.arange(G, dtype=jnp.int32)
    target = (my_slab[:, None] * SLAB_ROWS + my_row[:, None] + within).reshape(1, -1)
    slab_order = [2, 3, 1, 0] if slab_count == 4 else list(range(slab_count - 1, -1, -1))
    ours = [arrived[r, 0] for r in order]
    theirs = [arrived[r, 1] for r in order]
    volume = None
    incoming = []
    for lot in (slab_order[:1], slab_order[1:]):
        wanted = jnp.concatenate(
            [(here ^ r) * SLAB_ROWS + jnp.arange(SLAB_ROWS, dtype=jnp.int32) for r in lot]
        )
        sent, mix = mix_send(me_ref, wanted[:, None], target, weights, theirs, orient_count)
        got = swap(sent, "orient", 1)
        for n, offset in enumerate(lot):
            split = mix_keep(me_ref, mix, n * SLAB_ROWS, got, ours, orient_count)
            total = reduce_chips(*split, orient_count)
            if offset:
                incoming.append(swap(total.astype(BF16), "slab", offset))
            else:
                volume = total
    for block in incoming:
        volume = volume + block.astype(F32)

    logsum = jnp.concatenate(logsums)
    logsum = jnp.stack([logsum[order.index(r)] for r in range(orient_count)])
    logsum = jnp.take(logsum, me ^ jnp.arange(orient_count, dtype=jnp.int32), axis=0)
    returned = lax.all_to_all(logsum[:, None, :], "orient", split_axis=0, concat_axis=0, tiled=True)
    place = slot_of[None, :] == jnp.arange(orient_count * capacity, dtype=jnp.int32)[:, None]
    loglik = jnp.sum(jnp.where(place, returned.reshape(-1)[:, None], 0.0), axis=0)
    return (volume, loglik)


def solution(mesh):
    in_specs = (
        P(("orient", "slab"), None),
        P(("orient", "slab"), None),
        P("orient", None, None),
        P(),
        P(),
    )
    out_specs = (P("slab", "orient"), P(("orient", "slab")))
    return jax.shard_map(body, mesh=mesh, in_specs=in_specs, out_specs=out_specs, check_vma=False)
```

time: 409 us -> 307 us (0.75); the launches traced: 401 us -> 304 us
  matrix products: 121 us -> 0 us
  waiting for transfers between devices: 206 us -> 121 us
  Pallas kernels: 0 us -> 81.9 us
  local copies, waits for them, and re-layouts: 1.65 us -> 12.4 us
  starting transfers between devices: 65.4 us -> 75.6 us
  other arithmetic: 6.25 us -> 11.1 us
    all_to_all x13 -> x1, waiting for transfers between devices: 206 us -> 8.2 us  [body(): lax.all_to_all(logsum[:, None, :], 'orient', split_axis=0, concat_axis=0,...]
    dot_general x44 -> x0, matrix products: 121 us -> none  [the longest x32 60.7 us: body(): lax.dot_general(weights, block, (((0,), (0,)), ((), ())), preferred_eleme...]
    ppermute x0 -> x35, waiting for transfers between devices: none -> 113 us  [swap(): return lax.ppermute(x, axis, [(i, i ^ offset) for i in range(count)])]
    pallas_call x0 -> x12, Pallas kernels: none -> 81.9 us  [the longest x4 25.9 us: score(): call(functools.partial(score_kernel, count, owned, scale), 'score', (orie...]
    ppermute x0 -> x35, starting transfers between devices: none -> 72.1 us  [swap(): return lax.ppermute(x, axis, [(i, i ^ offset) for i in range(count)])]
    all_to_all x13 -> x1, starting transfers between devices: 65.4 us -> 3.44 us  [body(): lax.all_to_all(logsum[:, None, :], 'orient', split_axis=0, concat_axis=0,...]
    unnamed x12 -> x76, local copies, waits for them, and re-layouts: 0.02 us -> 10.1 us
    add x3 -> x14, other arithmetic: 0.14 us -> 6 us  [the longest x4 2.12 us: reduce_chips(): upper = upper_kept + swap(upper_sent, 'orient', 1 << bits[n]).astype(F32)]
  transfers between devices with their start and end apart: 13 -> 36, of which waited for: 13 -> 17; matrix products, arithmetic and copies ran while one was open for 25% -> 3% of each run, Pallas kernels for 0% -> 19%
where the time goes in v2:
time: 307 us; the launch traced here: 304 us
  waiting for transfers between devices  121 us (39%)
  Pallas kernels  81.9 us (27%)
  starting transfers between devices  75.6 us (25%)
  local copies, waits for them, and re-layouts  12.4 us (4%)
  other arithmetic  11.1 us (4%)
    ppermute x35, waiting for transfers between devices, swap(): return lax.ppermute(x, axis, [(i, i ^ offset) for i in range(count)])  113 us
    ppermute x35, starting transfers between devices, swap(): return lax.ppermute(x, axis, [(i, i ^ offset) for i in range(count)])  72.1 us
    pallas_call x4, Pallas kernels, score(): call(functools.partial(score_kernel, count, owned, scale), 'score', (orie...  25.9 us
    pallas_call x4, Pallas kernels, mix_keep(): call(functools.partial(keep_kernel, len(rows), blocks), 'mix_keep', (bloc...  25.5 us
    pallas_call x2, Pallas kernels, mix_send(): call(functools.partial(send_kernel, len(weights), len(rows)), 'mix_send',...  15.7 us
    pallas_call x2, Pallas kernels, gather(): call(functools.partial(gather_kernel, offsets, capacity, owned), 'gather'...  14.8 us
    unnamed x76, local copies, waits for them, and re-layouts  10.1 us
    all_to_all x1, waiting for transfers between devices, body(): lax.all_to_all(logsum[:, None, :], 'orient', split_axis=0, concat_axis=0,...  8.2 us
  transfers between devices with their start and end apart: 36, of which 17 were waited for; matrix products, arithmetic and copies ran while one was open for 3% of the time, Pallas kernels for 19%

profile of v2, /device:TPU:2, one launch (start us, length us, event | category | flops | bytes accessed | tf_op | source)
XLA Modules:
  0.0 303.9 jit_solution(8349080923402122441)
XLA Ops:
  3.2 9.4 %gather.12 = (bf16[96,4096]{1,0:T(8,128)(2,1)S(1)}, bf16[96,4096]{1,0:T(8,128)(2,1)S(1)}, bf16[96,4096]{1,0:T(8,128)(2,1)}, bf16[96,4096]{1,0:T(8,128)(2,1)}, bf...) custom-call(s32[1]{0:T(128)} %bitcast.me_ref, ...), custom_call_target="tpu_custom_call" | custom-call | flops 3623878656 | bytes 15728640 | tf_op jit(solution)/shard_map/gather/pallas_call | solution.py:78
  17.0 16.5 %collective-permute-done.10.rest_0_.rest_6_ = bf16[96,4096]{1,0:T(8,128)(2,1)S(1)} collective-permute-done((bf16[96,4096]{1,0:T(8,128)(2,1)}, bf16[96,4096]{1,0:T(8,128)(2,1)S(1)}, u32[]{:S(2)}, u32[]{:S(2)}) %collective-permute-start.10) | collective-permute-done | bytes 786464 | tf_op jit(solution)/shard_map/ppermute | solution.py:27
  35.6 14.8 %collective-permute-done.11.rest_1_.rest_10_ = bf16[96,4096]{1,0:T(8,128)(2,1)S(1)} collective-permute-done((bf16[96,4096]{1,0:T(8,128)(2,1)}, bf16[96,4096]{1,0:T(8,128)(2,1)S(1)}, u32[]{:S(2)}, u32[]{:S(2)}) %collective-permute-start.11) | collective-permute-done | bytes 786464 | tf_op jit(solution)/shard_map/ppermute | solution.py:27
  54.4 12.9 %collective-permute-done.6.rest_0_.rest_4_ = bf16[96,4096]{1,0:T(8,128)(2,1)S(1)} collective-permute-done((bf16[96,4096]{1,0:T(8,128)(2,1)}, bf16[96,4096]{1,0:T(8,128)(2,1)S(1)}, u32[]{:S(2)}, u32[]{:S(2)}) %collective-permute-start.6) | collective-permute-done | bytes 786464 | tf_op jit(solution)/shard_map/ppermute | solution.py:27
  67.7 5.5 %gather.13 = (bf16[96,4096]{1,0:T(8,128)(2,1)S(1)}, bf16[96,4096]{1,0:T(8,128)(2,1)S(1)}, bf16[96,4096]{1,0:T(8,128)(2,1)S(1)}, bf16[96,4096]{1,0:T(8,128)(2,1)S(1)}) custom-call(s32[1]{0:T(128)} %bitcast.me_ref, s32[1,384]{1,0:T(1,128)S(1)} %bitcast_add_fusion.slot_ref, bf16[384,8192]{1,0:T(8,128)(2,1)} %images_ref.3), custom_call_target="tpu_custom_call" | custom-call | flops 1207959552 | bytes 9437184 | tf_op jit(solution)/shard_map/gather/pallas_call | solution.py:78
  74.7 9.6 %collective-permute-done.7.rest_1_.rest_8_ = bf16[96,4096]{1,0:T(8,128)(2,1)} collective-permute-done((bf16[96,4096]{1,0:T(8,128)(2,1)}, bf16[96,4096]{1,0:T(8,128)(2,1)}, u32[]{:S(2)}, u32[]{:S(2)}) %collective-permute-start.7) | collective-permute-done | bytes 786464 | tf_op jit(solution)/shard_map/ppermute | solution.py:27
  85.4 35.0 %collective-permute-start.3 = (bf16[96,4096]{1,0:T(8,128)(2,1)S(1)}, bf16[96,4096]{1,0:T(8,128)(2,1)S(1)}, u32[]{:S(2)}, u32[]{:S(2)}) collective-permute-start(bf16[96,4096]{1,0:T(8,128)(2,1)S(1)} %get-tuple-element.52), channel_id=1, source_target_pairs={{0,24},{4,28},{8,16},{12,20},{16,8},{20,12},{24,0},{28,4},{1,25},{... | collective-permute-start | bytes 2359304 | tf_op jit(solution)/shard_map/ppermute | solution.py:27
  120.6 6.3 %score.7 = (bf16[192,512]{1,0:T(8,128)(2,1)S(1)}, f32[192,1]{1,0:T(8,128)S(1)}) custom-call(s32[1]{0:T(128)} %bitcast.me_ref, bf16[512,8192]{1,0:T(8,128)(2,1)} %bitcast.43, bf16[96,4096]{1,0:T(8,128)(2,1)S(1)} %collective-permute-done.10.rest_0_.rest_6_, bf16[96,4096]{1,0:T(8,128)(2,1)S(1)} %copy-done.10, ...), custom_call_target="tpu_custom_call" | custom-call | flops 1610612736 | bytes 11534336 | tf_op jit(solution)/shard_map/score/pallas_call | solution.py:132
  127.0 6.6 %score.6 = (bf16[192,512]{1,0:T(8,128)(2,1)S(1)}, f32[192,1]{1,0:T(8,128)S(1)}) custom-call(s32[1]{0:T(128)} %bitcast.me_ref, bf16[512,8192]{1,0:T(8,128)(2,1)} %bitcast.44, bf16[96,4096]{1,0:T(8,128)(2,1)S(1)} %collective-permute-done.6.rest_0_.rest_4_, bf16[96,4096]{1,0:T(8,128)(2,1)} %collective-permute-done.7.rest_1_.rest_8_, ...), custom_call_target="tpu_custom_call" | custom-call | flops 1610612736 | bytes 11534336 | tf_op jit(solution)/shard_map/score/pallas_call | solution.py:132
  133.6 6.4 %score.4 = (bf16[192,512]{1,0:T(8,128)(2,1)S(1)}, f32[192,1]{1,0:T(8,128)S(1)}) custom-call(s32[1]{0:T(128)} %bitcast.me_ref, bf16[512,8192]{1,0:T(8,128)(2,1)} %bitcast.45, bf16[96,4096]{1,0:T(8,128)(2,1)S(1)} %get-tuple-element.46.rest_0_, bf16[96,4096]{1,0:T(8,128)(2,1)S(1)} %copy-done.7, bf16[96,4096]{1,0:T(8,128)(2,1)} %collective-permute-done.rest_2_.rest_1_, ...), custom_call_target="tpu_custom_call" | custom-call | flops 1610612736 | bytes 11534336 | tf_op jit(solution)/shard_map/score/pallas_call | solution.py:132
  140.1 13.3 %collective-permute-done.5.rest_3_.rest_7_ = bf16[96,4096]{1,0:T(8,128)(2,1)S(1)} collective-permute-done((bf16[96,4096]{1,0:T(8,128)(2,1)S(1)}, bf16[96,4096]{1,0:T(8,128)(2,1)S(1)}, u32[]{:S(2)}, u32[]{:S(2)}) %collective-permute-start.5) | collective-permute-done | bytes 786464 | tf_op jit(solution)/shard_map/ppermute | solution.py:27
  153.5 6.6 %score.5 = (bf16[192,512]{1,0:T(8,128)(2,1)S(1)}, f32[192,1]{1,0:T(8,128)S(1)}) custom-call(s32[1]{0:T(128)} %bitcast.me_ref, bf16[512,8192]{1,0:T(8,128)(2,1)} %bitcast.46, bf16[96,4096]{1,0:T(8,128)(2,1)S(1)} %collective-permute-done.2.rest_0_.rest_2_, bf16[96,4096]{1,0:T(8,128)(2,1)S(1)} %collective-permute-done.3.rest_1_.rest_6_, ...), custom_call_target="tpu_custom_call" | custom-call | flops 1610612736 | bytes 11534336 | tf_op jit(solution)/shard_map/score/pallas_call | solution.py:132
  160.2 9.5 %mix_send.2 = (bf16[768,4096]{1,0:T(8,128)(2,1)}, bf16[768,768]{1,0:T(8,128)(2,1)}) custom-call(s32[1]{0:T(128)} %bitcast.me_ref, s32[768,1]{1,0:T(8,128)S(1)} %broadcast_in_dim.42.wanted_ref, s32[1,512]{1,0:T(1,128)S(1)} %add.170.target_ref, bf16[192,512]{1,0:T(8,128)(2,1)S(1)} %get-tuple-element.50.rest_0_, ...), custom_call_target="tpu_custom_call" | custom-call | flops 4831838208 | bytes 12582912 | tf_op jit(solution)/shard_map/mix_send/pallas_call | solution.py:185
  175.6 6.2 %mix_send.3 = (bf16[256,4096]{1,0:T(8,128)(2,1)}, bf16[256,768]{1,0:T(8,128)(2,1)S(1)}) custom-call(s32[1]{0:T(128)} %bitcast.me_ref, s32[256,1]{1,0:T(8,128)S(1)} %iota_add_fusion.wanted_ref, s32[1,512]{1,0:T(1,128)S(1)} %add.170.target_ref, bf16[192,512]{1,0:T(8,128)(2,1)S(1)} %copy-done.18, bf16[192,512]{1,0:T(8,128)(2,1)S(1)} %copy-done.20, ...), custom_call_target="tpu_custom_call" | custom-call | flops 1610612736 | bytes 8388608 | tf_op jit(solution)/shard_map/mix_send/pallas_call | solution.py:185
  182.2 4.0 %collective-permute-done.19.got_ref = bf16[256,4096]{1,0:T(8,128)(2,1)S(1)} collective-permute-done((bf16[256,4096]{1,0:T(8,128)(2,1)}, bf16[256,4096]{1,0:T(8,128)(2,1)S(1)}, u32[]{:S(2)}, u32[]{:S(2)}) %collective-permute-start.19) | collective-permute-done | bytes 2097184 | tf_op jit(solution)/shard_map/ppermute | solution.py:27
  187.4 6.5 %mix_keep.5 = (bf16[2,128,1024]{2,1,0:T(8,128)(2,1)}, f32[2,128,1024]{2,1,0:T(8,128)}, bf16[2,128,1024]{2,1,0:T(8,128)(2,1)S(1)}, f32[2,128,1024]{2,1,0:T(8,128)}) custom-call(s32[1]{0:T(128)} %bitcast.me_ref, bf16[256,768]{1,0:T(8,128)(2,1)S(1)} %get-tuple-element.72.mix_ref, bf16[256,4096]{1,0:T(8,128)(2,1)} %copy-done.30, ...), custom_call_target="tpu_custom_call" | custom-call | flops 1610612736 | bytes 10485760 | tf_op jit(solution)/shard_map/mix_keep/pallas_call | solution.py:241
  196.1 2.5 collective-permute-start.22
  199.3 3.4 %all-to-all-start = ((f32[8,1,96]{2,1,0:T(1,128)}), f32[8,1,96]{2,1,0:T(1,128)S(1)}, u32[]{:S(2)}, u32[]{:S(2)}) async-start(f32[8,1,96]{2,1,0:T(1,128)} %bitcast.16), calls=%async_computation | async-start | bytes 8192 | tf_op jit(solution)/shard_map/all_to_all | solution.py:327
  202.8 8.2 %all-to-all-done = f32[8,1,96]{2,1,0:T(1,128)S(1)} async-done(((f32[8,1,96]{2,1,0:T(1,128)}), f32[8,1,96]{2,1,0:T(1,128)S(1)}, u32[]{:S(2)}, u32[]{:S(2)}) %all-to-all-start) | async-done | bytes 3104 | tf_op jit(solution)/shard_map/all_to_all | solution.py:327
  217.4 4.9 %collective-permute-done.21 = bf16[1,128,1024]{2,1,0:T(8,128)(2,1)S(1)} collective-permute-done((bf16[1,128,1024]{2,1,0:T(8,128)(2,1)S(1)}, bf16[1,128,1024]{2,1,0:T(8,128)(2,1)S(1)}, u32[]{:S(2)}, u32[]{:S(2)}) %collective-permute-start.21) | collective-permute-done | bytes 262176 | tf_op jit(solution)/shard_map/ppermute | solution.py:27
  222.4 6.4 %mix_keep.6 = (bf16[2,128,1024]{2,1,0:T(8,128)(2,1)S(1)}, f32[2,128,1024]{2,1,0:T(8,128)}, bf16[2,128,1024]{2,1,0:T(8,128)(2,1)S(1)}, f32[2,128,1024]{2,1,0:T(8,128)}) custom-call(s32[1]{0:T(128)} %bitcast.me_ref, bf16[768,768]{1,0:T(8,128)(2,1)} %get-tuple-element.66.mix_ref, bf16[768,4096]{1,0:T(8,128)(2,1)} %collective-permute-done.14.got_ref, ...), custom_call_target="tpu_custom_call" | custom-call | flops 1610612736 | bytes 10485760 | tf_op jit(solution)/shard_map/mix_keep/pallas_call | solution.py:241
  229.4 2.7 collective-permute-start.24
  233.5 6.3 %mix_keep.7 = (bf16[2,128,1024]{2,1,0:T(8,128)(2,1)S(1)}, f32[2,128,1024]{2,1,0:T(8,128)}, bf16[2,128,1024]{2,1,0:T(8,128)(2,1)S(1)}, f32[2,128,1024]{2,1,0:T(8,128)}) custom-call(s32[1]{0:T(128)} %bitcast.me_ref, bf16[768,768]{1,0:T(8,128)(2,1)} %get-tuple-element.66.mix_ref, bf16[768,4096]{1,0:T(8,128)(2,1)} %collective-permute-done.14.got_ref, ...), custom_call_target="tpu_custom_call" | custom-call | flops 1610612736 | bytes 10485760 | tf_op jit(solution)/shard_map/mix_keep/pallas_call | solution.py:241
  241.9 6.3 %mix_keep.4 = (bf16[2,128,1024]{2,1,0:T(8,128)(2,1)S(1)}, f32[2,128,1024]{2,1,0:T(8,128)}, bf16[2,128,1024]{2,1,0:T(8,128)(2,1)S(1)}, f32[2,128,1024]{2,1,0:T(8,128)}) custom-call(s32[1]{0:T(128)} %bitcast.me_ref, bf16[768,768]{1,0:T(8,128)(2,1)} %get-tuple-element.66.mix_ref, bf16[768,4096]{1,0:T(8,128)(2,1)} %collective-permute-done.14.got_ref, ...), custom_call_target="tpu_custom_call" | custom-call | flops 1610612736 | bytes 10485760 | tf_op jit(solution)/shard_map/mix_keep/pallas_call | solution.py:241
  250.8 3.9 %collective-permute-done.30 = bf16[2,128,1024]{2,1,0:T(8,128)(2,1)S(1)} collective-permute-done((bf16[2,128,1024]{2,1,0:T(8,128)(2,1)S(1)}, bf16[2,128,1024]{2,1,0:T(8,128)(2,1)S(1)}, u32[]{:S(2)}, u32[]{:S(2)}) %collective-permute-start.30) | collective-permute-done | bytes 524320 | tf_op jit(solution)/shard_map/ppermute | solution.py:27
  254.7 1.8 collective-permute-start.26
  259.9 6.1 %collective-permute-done.15 = bf16[2,128,1024]{2,1,0:T(8,128)(2,1)S(1)} collective-permute-done((bf16[2,128,1024]{2,1,0:T(8,128)(2,1)S(1)}, bf16[2,128,1024]{2,1,0:T(8,128)(2,1)S(1)}, u32[]{:S(2)}, u32[]{:S(2)}) %collective-permute-start.15) | collective-permute-done | bytes 524320 | tf_op jit(solution)/shard_map/ppermute | solution.py:27
  266.0 1.8 collective-permute-start.31
  271.1 3.6 %collective-permute-done.26 = bf16[1,128,1024]{2,1,0:T(8,128)(2,1)S(1)} collective-permute-done((bf16[1,128,1024]{2,1,0:T(8,128)(2,1)S(1)}, bf16[1,128,1024]{2,1,0:T(8,128)(2,1)S(1)}, u32[]{:S(2)}, u32[]{:S(2)}) %collective-permute-start.26) | collective-permute-done | bytes 262176 | tf_op jit(solution)/shard_map/ppermute | solution.py:27
  278.5 1.9 collective-permute-done.31
  284.0 13.0 %collective-permute-done.29 = bf16[256,1024]{1,0:T(8,128)(2,1)S(1)} collective-permute-done((bf16[256,1024]{1,0:T(8,128)(2,1)S(1)}, bf16[256,1024]{1,0:T(8,128)(2,1)S(1)}, u32[]{:S(2)}, u32[]{:S(2)}) %collective-permute-start.29) | collective-permute-done | bytes 524320 | tf_op jit(solution)/shard_map/ppermute | solution.py:27
  297.0 5.6 %collective-permute-done.34 = bf16[256,1024]{1,0:T(8,128)(2,1)S(1)} collective-permute-done((bf16[256,1024]{1,0:T(8,128)(2,1)S(1)}, bf16[256,1024]{1,0:T(8,128)(2,1)S(1)}, u32[]{:S(2)}, u32[]{:S(2)}) %collective-permute-start.34) | collective-permute-done | bytes 524320 | tf_op jit(solution)/shard_map/ppermute | solution.py:27
  (186 shorter events, 55.0 us)
Async XLA Ops:
  13.5 20.0 %collective-permute-start.10 = (bf16[96,4096]{1,0:T(8,128)(2,1)}, bf16[96,4096]{1,0:T(8,128)(2,1)S(1)}, u32[]{:S(2)}, u32[]{:S(2)}) collective-permute-start(bf16[96,4096]{1,0:T(8,128)(2,1)} %get-tuple-element.61), channel_id=1, source_target_pairs={{0,12},{4,8},{8,4},{12,0},{16,28},{20,24},{24,20},{28,16},{1,13},{... | collective-permute-start | bytes 2359304 | tf_op jit(solution)/shard_map/ppermute | solution.py:27
  13.5 21.6 %collective-permute-start.12 = (bf16[96,4096]{1,0:T(8,128)(2,1)}, bf16[96,4096]{1,0:T(8,128)(2,1)S(1)}, u32[]{:S(2)}, u32[]{:S(2)}) collective-permute-start(bf16[96,4096]{1,0:T(8,128)(2,1)} %get-tuple-element.63), channel_id=1, source_target_pairs={{0,20},{4,16},{8,28},{12,24},{16,4},{20,0},{24,12},{28,8},{1,21},{... | collective-permute-start | bytes 2359304 | tf_op jit(solution)/shard_map/ppermute | solution.py:27
  15.3 35.1 %collective-permute-start.11 = (bf16[96,4096]{1,0:T(8,128)(2,1)}, bf16[96,4096]{1,0:T(8,128)(2,1)S(1)}, u32[]{:S(2)}, u32[]{:S(2)}) collective-permute-start(bf16[96,4096]{1,0:T(8,128)(2,1)} %get-tuple-element.62), channel_id=1, source_target_pairs={{0,12},{4,8},{8,4},{12,0},{16,28},{20,24},{24,20},{28,16},{1,13},{... | collective-permute-start | bytes 2359304 | tf_op jit(solution)/shard_map/ppermute | solution.py:27
  16.2 36.6 %collective-permute-start.13 = (bf16[96,4096]{1,0:T(8,128)(2,1)}, bf16[96,4096]{1,0:T(8,128)(2,1)S(1)}, u32[]{:S(2)}, u32[]{:S(2)}) collective-permute-start(bf16[96,4096]{1,0:T(8,128)(2,1)} %get-tuple-element.64), channel_id=1, source_target_pairs={{0,20},{4,16},{8,28},{12,24},{16,4},{20,0},{24,12},{28,8},{1,21},{... | collective-permute-start | bytes 2359304 | tf_op jit(solution)/shard_map/ppermute | solution.py:27
  17.0 50.3 %collective-permute-start.6 = (bf16[96,4096]{1,0:T(8,128)(2,1)}, bf16[96,4096]{1,0:T(8,128)(2,1)S(1)}, u32[]{:S(2)}, u32[]{:S(2)}) collective-permute-start(bf16[96,4096]{1,0:T(8,128)(2,1)} %get-tuple-element.56), channel_id=1, source_target_pairs={{0,8},{4,12},{8,0},{12,4},{16,24},{20,28},{24,16},{28,20},{1,9},{5... | collective-permute-start | bytes 2359304 | tf_op jit(solution)/shard_map/ppermute | solution.py:27
  33.6 39.6 %collective-permute-start.8 = (bf16[96,4096]{1,0:T(8,128)(2,1)}, bf16[96,4096]{1,0:T(8,128)(2,1)}, u32[]{:S(2)}, u32[]{:S(2)}) collective-permute-start(bf16[96,4096]{1,0:T(8,128)(2,1)} %get-tuple-element.58), channel_id=1, source_target_pairs={{0,16},{4,20},{8,24},{12,28},{16,0},{20,4},{24,8},{28,12},{1,17},{... | collective-permute-start | bytes 2359304 | tf_op jit(solution)/shard_map/ppermute | solution.py:27
  35.1 49.2 %collective-permute-start.7 = (bf16[96,4096]{1,0:T(8,128)(2,1)}, bf16[96,4096]{1,0:T(8,128)(2,1)}, u32[]{:S(2)}, u32[]{:S(2)}) collective-permute-start(bf16[96,4096]{1,0:T(8,128)(2,1)} %get-tuple-element.57), channel_id=1, source_target_pairs={{0,8},{4,12},{8,0},{12,4},{16,24},{20,28},{24,16},{28,20},{1,9},{5... | collective-permute-start | bytes 2359304 | tf_op jit(solution)/shard_map/ppermute | solution.py:27
  51.3 34.1 %collective-permute-start.9 = (bf16[96,4096]{1,0:T(8,128)(2,1)}, bf16[96,4096]{1,0:T(8,128)(2,1)}, u32[]{:S(2)}, u32[]{:S(2)}) collective-permute-start(bf16[96,4096]{1,0:T(8,128)(2,1)} %get-tuple-element.59), channel_id=1, source_target_pairs={{0,16},{4,20},{8,24},{12,28},{16,0},{20,4},{24,8},{28,12},{1,17},{... | collective-permute-start | bytes 2359304 | tf_op jit(solution)/shard_map/ppermute | solution.py:27
  53.7 66.7 %collective-permute-start = (bf16[96,4096]{1,0:T(8,128)(2,1)}, bf16[96,4096]{1,0:T(8,128)(2,1)}, u32[]{:S(2)}, u32[]{:S(2)}) collective-permute-start(bf16[96,4096]{1,0:T(8,128)(2,1)} %get-tuple-element.48), channel_id=1, source_target_pairs={{0,4},{4,0},{8,12},{12,8},{16,20},{20,16},{24,28},{28,24},{1,5},{5... | collective-permute-start | bytes 2359304 | tf_op jit(solution)/shard_map/ppermute | solution.py:27
  67.3 66.3 %collective-permute-start.1 = (bf16[96,4096]{1,0:T(8,128)(2,1)}, bf16[96,4096]{1,0:T(8,128)(2,1)}, u32[]{:S(2)}, u32[]{:S(2)}) collective-permute-start(bf16[96,4096]{1,0:T(8,128)(2,1)} %get-tuple-element.49), channel_id=1, source_target_pairs={{0,4},{4,0},{8,12},{12,8},{16,20},{20,16},{24,28},{28,24},{1,5},{5... | collective-permute-start | bytes 2359304 | tf_op jit(solution)/shard_map/ppermute | solution.py:27
  73.2 66.9 %collective-permute-start.2 = (bf16[96,4096]{1,0:T(8,128)(2,1)S(1)}, bf16[96,4096]{1,0:T(8,128)(2,1)S(1)}, u32[]{:S(2)}, u32[]{:S(2)}) collective-permute-start(bf16[96,4096]{1,0:T(8,128)(2,1)S(1)} %get-tuple-element.51), channel_id=1, source_target_pairs={{0,24},{4,28},{8,16},{12,20},{16,8},{20,12},{24,0},{28,4},{1,25},{... | collective-permute-start | bytes 2359304 | tf_op jit(solution)/shard_map/ppermute | solution.py:27
  84.3 55.8 %collective-permute-start.4 = (bf16[96,4096]{1,0:T(8,128)(2,1)S(1)}, bf16[96,4096]{1,0:T(8,128)(2,1)S(1)}, u32[]{:S(2)}, u32[]{:S(2)}) collective-permute-start(bf16[96,4096]{1,0:T(8,128)(2,1)S(1)} %get-tuple-element.53), channel_id=1, source_target_pairs={{0,28},{4,24},{8,20},{12,16},{16,12},{20,8},{24,4},{28,0},{1,29},{... | collective-permute-start | bytes 2359304 | tf_op jit(solution)/shard_map/ppermute | solution.py:27
  85.4 54.7 %collective-permute-start.3 = (bf16[96,4096]{1,0:T(8,128)(2,1)S(1)}, bf16[96,4096]{1,0:T(8,128)(2,1)S(1)}, u32[]{:S(2)}, u32[]{:S(2)}) collective-permute-start(bf16[96,4096]{1,0:T(8,128)(2,1)S(1)} %get-tuple-element.52), channel_id=1, source_target_pairs={{0,24},{4,28},{8,16},{12,20},{16,8},{20,12},{24,0},{28,4},{1,25},{... | collective-permute-start | bytes 2359304 | tf_op jit(solution)/shard_map/ppermute | solution.py:27
  120.4 33.1 %collective-permute-start.5 = (bf16[96,4096]{1,0:T(8,128)(2,1)S(1)}, bf16[96,4096]{1,0:T(8,128)(2,1)S(1)}, u32[]{:S(2)}, u32[]{:S(2)}) collective-permute-start(bf16[96,4096]{1,0:T(8,128)(2,1)S(1)} %get-tuple-element.54), channel_id=1, source_target_pairs={{0,28},{4,24},{8,20},{12,16},{16,12},{20,8},{24,4},{28,0},{1,29},{... | collective-permute-start | bytes 2359304 | tf_op jit(solution)/shard_map/ppermute | solution.py:27
  169.7 52.7 %collective-permute-start.14 = (bf16[768,4096]{1,0:T(8,128)(2,1)}, bf16[768,4096]{1,0:T(8,128)(2,1)}, u32[]{:S(2)}, u32[]{:S(2)}) collective-permute-start(bf16[768,4096]{1,0:T(8,128)(2,1)} %get-tuple-element.67), channel_id=1, source_target_pairs={{0,4},{4,0},{8,12},{12,8},{16,20},{20,16},{24,28},{28,24},{1,5},{5... | collective-permute-start | bytes 18874376 | tf_op jit(solution)/shard_map/ppermute | solution.py:27
  194.7 17.5 %collective-permute-start.20 = (bf16[2,128,1024]{2,1,0:T(8,128)(2,1)}, bf16[2,128,1024]{2,1,0:T(8,128)(2,1)}, u32[]{:S(2)}, u32[]{:S(2)}) collective-permute-start(bf16[2,128,1024]{2,1,0:T(8,128)(2,1)} %get-tuple-element.75), channel_id=1, source_target_pairs={{0,8},{4,12},{8,0},{12,4},{16,24},{20,28},{24,16},{28,20},{1,9},{5... | collective-permute-start | bytes 1572872 | tf_op jit(solution)/shard_map/ppermute | solution.py:27
  196.1 19.6 %collective-permute-start.22 = (bf16[2,128,1024]{2,1,0:T(8,128)(2,1)}, bf16[2,128,1024]{2,1,0:T(8,128)(2,1)}, u32[]{:S(2)}, u32[]{:S(2)}) collective-permute-start(bf16[2,128,1024]{2,1,0:T(8,128)(2,1)} %copy-done.29), channel_id=1, source_target_pairs={{0,16},{4,20},{8,24},{12,28},{16,0},{20,4},{24,8},{28,12},{1,17},{... | collective-permute-start | bytes 1572872 | tf_op jit(solution)/shard_map/ppermute | solution.py:27
  199.3 11.7 %all-to-all-start = ((f32[8,1,96]{2,1,0:T(1,128)}), f32[8,1,96]{2,1,0:T(1,128)S(1)}, u32[]{:S(2)}, u32[]{:S(2)}) async-start(f32[8,1,96]{2,1,0:T(1,128)} %bitcast.16), calls=%async_computation | async-start | bytes 8192 | tf_op jit(solution)/shard_map/all_to_all | solution.py:327
  217.0 12.3 %collective-permute-start.23 = (bf16[1,128,1024]{2,1,0:T(8,128)(2,1)S(1)}, bf16[1,128,1024]{2,1,0:T(8,128)(2,1)S(1)}, u32[]{:S(2)}, u32[]{:S(2)}) collective-permute-start(bf16[1,128,1024]{2,1,0:T(8,128)(2,1)S(1)} %slice.228), channel_id=1, source_target_pairs={{0,8},{4,12},{8,0},{12,4},{16,24},{20,28},{24,16},{28,20},{1,9},{5... | collective-permute-start | bytes 786440 | tf_op jit(solution)/shard_map/ppermute | solution.py:27
  228.7 19.5 %collective-permute-start.25 = (bf16[2,128,1024]{2,1,0:T(8,128)(2,1)S(1)}, bf16[2,128,1024]{2,1,0:T(8,128)(2,1)S(1)}, u32[]{:S(2)}, u32[]{:S(2)}) collective-permute-start(bf16[2,128,1024]{2,1,0:T(8,128)(2,1)S(1)} %get-tuple-element.79), channel_id=1, source_target_pairs={{0,8},{4,12},{8,0},{12,4},{16,24},{20,28},{24,16},{28,20},{1,9},{5... | collective-permute-start | bytes 1572872 | tf_op jit(solution)/shard_map/ppermute | solution.py:27
  229.4 54.7 %collective-permute-start.24 = (bf16[256,1024]{1,0:T(8,128)(2,1)S(1)}, bf16[256,1024]{1,0:T(8,128)(2,1)S(1)}, u32[]{:S(2)}, u32[]{:S(2)}) collective-permute-start(bf16[256,1024]{1,0:T(8,128)(2,1)S(1)} %pad_maximum_fusion), channel_id=1, source_target_pairs={{0,2},{1,3},{2,0},{3,1},{4,6},{5,7},{6,4},{7,5},{8,10},{9,11},{10,... | collective-permute-start | bytes 1572872 | tf_op jit(solution)/shard_map/ppermute | solution.py:27
  232.0 17.0 %collective-permute-start.27 = (bf16[2,128,1024]{2,1,0:T(8,128)(2,1)S(1)}, bf16[2,128,1024]{2,1,0:T(8,128)(2,1)S(1)}, u32[]{:S(2)}, u32[]{:S(2)}) collective-permute-start(bf16[2,128,1024]{2,1,0:T(8,128)(2,1)S(1)} %get-tuple-element.81), channel_id=1, source_target_pairs={{0,16},{4,20},{8,24},{12,28},{16,0},{20,4},{24,8},{28,12},{1,17},{... | collective-permute-start | bytes 1572872 | tf_op jit(solution)/shard_map/ppermute | solution.py:27
  239.9 14.9 %collective-permute-start.30 = (bf16[2,128,1024]{2,1,0:T(8,128)(2,1)S(1)}, bf16[2,128,1024]{2,1,0:T(8,128)(2,1)S(1)}, u32[]{:S(2)}, u32[]{:S(2)}) collective-permute-start(bf16[2,128,1024]{2,1,0:T(8,128)(2,1)S(1)} %get-tuple-element.83), channel_id=1, source_target_pairs={{0,8},{4,12},{8,0},{12,4},{16,24},{20,28},{24,16},{28,20},{1,9},{5... | collective-permute-start | bytes 1572872 | tf_op jit(solution)/shard_map/ppermute | solution.py:27
  241.6 16.3 %collective-permute-start.32 = (bf16[2,128,1024]{2,1,0:T(8,128)(2,1)S(1)}, bf16[2,128,1024]{2,1,0:T(8,128)(2,1)S(1)}, u32[]{:S(2)}, u32[]{:S(2)}) collective-permute-start(bf16[2,128,1024]{2,1,0:T(8,128)(2,1)S(1)} %get-tuple-element.85), channel_id=1, source_target_pairs={{0,16},{4,20},{8,24},{12,28},{16,0},{20,4},{24,8},{28,12},{1,17},{... | collective-permute-start | bytes 1572872 | tf_op jit(solution)/shard_map/ppermute | solution.py:27
  248.2 17.7 %collective-permute-start.15 = (bf16[2,128,1024]{2,1,0:T(8,128)(2,1)S(1)}, bf16[2,128,1024]{2,1,0:T(8,128)(2,1)S(1)}, u32[]{:S(2)}, u32[]{:S(2)}) collective-permute-start(bf16[2,128,1024]{2,1,0:T(8,128)(2,1)S(1)} %get-tuple-element.69), channel_id=1, source_target_pairs={{0,8},{4,12},{8,0},{12,4},{16,24},{20,28},{24,16},{28,20},{1,9},{5... | collective-permute-start | bytes 1572872 | tf_op jit(solution)/shard_map/ppermute | solution.py:27
  249.0 20.1 %collective-permute-start.17 = (bf16[2,128,1024]{2,1,0:T(8,128)(2,1)S(1)}, bf16[2,128,1024]{2,1,0:T(8,128)(2,1)S(1)}, u32[]{:S(2)}, u32[]{:S(2)}) collective-permute-start(bf16[2,128,1024]{2,1,0:T(8,128)(2,1)S(1)} %get-tuple-element.71), channel_id=1, source_target_pairs={{0,16},{4,20},{8,24},{12,28},{16,0},{20,4},{24,8},{28,12},{1,17},{... | collective-permute-start | bytes 1572872 | tf_op jit(solution)/shard_map/ppermute | solution.py:27
  254.7 20.0 %collective-permute-start.26 = (bf16[1,128,1024]{2,1,0:T(8,128)(2,1)S(1)}, bf16[1,128,1024]{2,1,0:T(8,128)(2,1)S(1)}, u32[]{:S(2)}, u32[]{:S(2)}) collective-permute-start(bf16[1,128,1024]{2,1,0:T(8,128)(2,1)S(1)} %slice.227), channel_id=1, source_target_pairs={{0,16},{4,20},{8,24},{12,28},{16,0},{20,4},{24,8},{28,12},{1,17},{... | collective-permute-start | bytes 786440 | tf_op jit(solution)/shard_map/ppermute | solution.py:27
  257.9 18.6 %collective-permute-start.28 = (bf16[1,128,1024]{2,1,0:T(8,128)(2,1)S(1)}, bf16[1,128,1024]{2,1,0:T(8,128)(2,1)S(1)}, u32[]{:S(2)}, u32[]{:S(2)}) collective-permute-start(bf16[1,128,1024]{2,1,0:T(8,128)(2,1)S(1)} %slice.226), channel_id=1, source_target_pairs={{0,8},{4,12},{8,0},{12,4},{16,24},{20,28},{24,16},{28,20},{1,9},{5... | collective-permute-start | bytes 786440 | tf_op jit(solution)/shard_map/ppermute | solution.py:27
  266.0 14.4 %collective-permute-start.31 = (bf16[1,128,1024]{2,1,0:T(8,128)(2,1)S(1)}, bf16[1,128,1024]{2,1,0:T(8,128)(2,1)S(1)}, u32[]{:S(2)}, u32[]{:S(2)}) collective-permute-start(bf16[1,128,1024]{2,1,0:T(8,128)(2,1)S(1)} %slice.225), channel_id=1, source_target_pairs={{0,16},{4,20},{8,24},{12,28},{16,0},{20,4},{24,8},{28,12},{1,17},{... | collective-permute-start | bytes 786440 | tf_op jit(solution)/shard_map/ppermute | solution.py:27
  269.1 12.7 %collective-permute-start.33 = (bf16[1,128,1024]{2,1,0:T(8,128)(2,1)S(1)}, bf16[1,128,1024]{2,1,0:T(8,128)(2,1)S(1)}, u32[]{:S(2)}, u32[]{:S(2)}) collective-permute-start(bf16[1,128,1024]{2,1,0:T(8,128)(2,1)S(1)} %slice.224), channel_id=1, source_target_pairs={{0,8},{4,12},{8,0},{12,4},{16,24},{20,28},{24,16},{28,20},{1,9},{5... | collective-permute-start | bytes 786440 | tf_op jit(solution)/shard_map/ppermute | solution.py:27
  280.4 16.7 %collective-permute-start.29 = (bf16[256,1024]{1,0:T(8,128)(2,1)S(1)}, bf16[256,1024]{1,0:T(8,128)(2,1)S(1)}, u32[]{:S(2)}, u32[]{:S(2)}) collective-permute-start(bf16[256,1024]{1,0:T(8,128)(2,1)S(1)} %pad_maximum_fusion.1), channel_id=1, source_target_pairs={{0,3},{1,2},{2,1},{3,0},{4,7},{5,6},{6,5},{7,4},{8,11},{9,10},{10,... | collective-permute-start | bytes 1572872 | tf_op jit(solution)/shard_map/ppermute | solution.py:27
  282.0 20.7 %collective-permute-start.34 = (bf16[256,1024]{1,0:T(8,128)(2,1)S(1)}, bf16[256,1024]{1,0:T(8,128)(2,1)S(1)}, u32[]{:S(2)}, u32[]{:S(2)}) collective-permute-start(bf16[256,1024]{1,0:T(8,128)(2,1)S(1)} %pad_maximum_fusion.2), channel_id=1, source_target_pairs={{0,1},{1,0},{2,3},{3,2},{4,5},{5,4},{6,7},{7,6},{8,9},{9,8},{10,11... | collective-permute-start | bytes 1572872 | tf_op jit(solution)/shard_map/ppermute | solution.py:27
  (42 other events, 565.7 us)

commit v3 on v1

v3 whole, which is shorter than its diff:
```python
import functools
import math

import jax
import jax.numpy as jnp
from jax import lax
from jax.experimental import pallas as pl
from jax.experimental.pallas import tpu as pltpu
from jax.sharding import PartitionSpec as P

G = 8
SLAB_ROWS = 256
BETA = 2.0
F32 = jnp.float32
BF16 = jnp.bfloat16
VMEM_LIMIT = 16 * 1024 * 1024


def slots(labels, groups, capacity):
    onehot = (labels[:, None] == jnp.arange(groups, dtype=jnp.int32)[None, :]).astype(jnp.int32)
    ordinal = jnp.sum((jnp.cumsum(onehot, axis=0) - 1) * onehot, axis=1)
    return labels * capacity + ordinal


def after(x, token):
    return lax.optimization_barrier((x, token))[0]


def swap(x, axis, offset):
    count = lax.axis_size(axis)
    return lax.ppermute(x, axis, [(i, i ^ offset) for i in range(count)])


def call(kernel, name, grid, in_specs, out_specs, out_shape, scratch, flops, size):
    return pl.pallas_call(
        kernel,
        name=name,
        grid_spec=pltpu.PrefetchScalarGridSpec(
            num_scalar_prefetch=1,
            grid=grid,
            in_specs=in_specs,
            out_specs=out_specs,
            scratch_shapes=scratch,
        ),
        out_shape=out_shape,
        compiler_params=pltpu.CompilerParams(vmem_limit_bytes=VMEM_LIMIT),
        cost_estimate=pl.CostEstimate(flops=20 * flops, bytes_accessed=20 * size, transcendentals=0),
    )


def gather_kernel(chips, capacity, owned, me_ref, slot_ref, images_ref, *rest):
    outs, select = rest[:-1], rest[-1]
    low, chip = me_ref[0] & 1, me_ref[0] >> 1
    both = 2 * capacity

    @pl.when(pl.program_id(0) == 0)
    def _():
        row = lax.broadcasted_iota(jnp.int32, (both, slot_ref.shape[1]), 0)
        for n, offset in enumerate(chips):
            hit = slot_ref[...] == row + (chip ^ offset) * both
            select[n * both : (n + 1) * both, :] = hit.astype(BF16)

    for which in range(2):
        block = images_ref[:, which * owned : (which + 1) * owned]
        found = jnp.dot(select[...], block, preferred_element_type=F32).astype(BF16)
        for core in range(2):

            @pl.when(low == core)
            def _():
                for n in range(len(chips)):
                    for member in range(2):
                        begin = n * both + member * capacity
                        rows = found[begin : begin + capacity]
                        out = 2 * n + (which ^ core)
                        outs[2 * out + member][...] = rows


def gather(chips, me, slot_of, images, orient_count, capacity):
    rows, window = images.shape
    owned = window // orient_count
    count = 4 * len(chips)
    outs = call(
        functools.partial(gather_kernel, chips, capacity, owned),
        "gather",
        (orient_count // 2,),
        [
            pl.BlockSpec((1, rows), lambda j, me: (0, 0)),
            pl.BlockSpec((rows, 2 * owned), lambda j, me: (0, j)),
        ],
        [pl.BlockSpec((capacity, owned), lambda j, me: (0, j))] * count,
        [jax.ShapeDtypeStruct((capacity, window // 2), BF16)] * count,
        [pltpu.VMEM((2 * len(chips) * capacity, rows), BF16)],
        4 * len(chips) * capacity * rows * window,
        2 * window * (rows + 2 * len(chips) * capacity),
    )(me, slot_of, images)
    offsets = [2 * q + swapped for q in chips for swapped in range(2)]
    return {r: [outs[2 * n], outs[2 * n + 1]] for n, r in enumerate(offsets)}


def score_kernel(members, count, me_ref, panels_ref, *rest):
    rows, out_ref = rest[:-1], rest[-1]
    for n, member in enumerate(members):
        block = jnp.concatenate([ref[...] for ref in rows[n * count : (n + 1) * count]], axis=0)
        term = lax.dot_general(
            block, panels_ref[n], (((1,), (1,)), ((), ())), preferred_element_type=F32
        )

        @pl.when(pl.program_id(0) == 0)
        def _():
            out_ref[n] = term

        @pl.when(pl.program_id(0) > 0)
        def _():
            out_ref[n] += term


def score(members, me, panels, pieces, orient_count):
    rows = [piece[member] for member in members for piece in pieces]
    _, orient_total, window = panels.shape
    owned = window // orient_count
    capacity = rows[0].shape[0]
    lead = members[0]
    shape = (len(members), len(pieces) * capacity, orient_total)
    return call(
        functools.partial(score_kernel, members, len(pieces)),
        "score",
        (orient_count // 2,),
        [
            pl.BlockSpec(
                (len(members), orient_total, owned), lambda j, me: (lead, 0, 2 * j + (me[0] & 1))
            )
        ]
        + [pl.BlockSpec((capacity, owned), lambda j, me: (0, j))] * len(rows),
        pl.BlockSpec(shape, lambda j, me: (0, 0, 0)),
        jax.ShapeDtypeStruct(shape, F32),
        [],
        shape[0] * shape[1] * orient_total * window,
        2 * window * (orient_total + shape[1]),
    )(me, panels, *rows)


def softmax(mine, got, capacity, scale):
    count = got.shape[0] // capacity
    got = jnp.concatenate(
        [got[(n ^ 1) * capacity : ((n ^ 1) + 1) * capacity] for n in range(count)], axis=0
    )
    scores = (mine + got) * scale
    largest = jnp.max(scores, axis=1, keepdims=True)
    exponent = jnp.exp(scores - largest)
    totals = jnp.sum(exponent, axis=1, keepdims=True)
    return (exponent / totals).astype(BF16), largest + jnp.log(totals)


def weigh_kernel(capacity, scale, me_ref, mine_ref, got_ref, weight_ref, logsum_ref):
    weight_ref[0], logsum_ref[0] = softmax(mine_ref[0], got_ref[0], capacity, scale)


def weigh(me, mine, got, capacity, scale):
    members, rows, orient_total = mine.shape
    block = pl.BlockSpec((1, rows, orient_total), lambda j, me: (j, 0, 0))
    return call(
        functools.partial(weigh_kernel, capacity, scale),
        "weigh",
        (members,),
        [block, block],
        [block, pl.BlockSpec((1, rows, 1), lambda j, me: (j, 0, 0))],
        [
            jax.ShapeDtypeStruct(mine.shape, BF16),
            jax.ShapeDtypeStruct((members, rows, 1), F32),
        ],
        [],
        10 * members * rows * orient_total,
        10 * members * rows * orient_total,
    )(me, mine, got)


def matrix_kernel(capacity, scale, me_ref, wanted_ref, target_ref, early_ref, *rest):
    mine, got, (logsum_ref, mix_ref, joined) = rest[:2], rest[2:4], rest[4:]
    early = early_ref.shape[1]
    late = mine[0].shape[1]
    for member in range(2):
        joined[:early, :] = early_ref[member]
        joined[early:, :], logsum_ref[member] = softmax(
            mine[member][0], got[member][0], capacity, scale
        )
        weights = joined[...]
        for n in range(wanted_ref.shape[0] // SLAB_ROWS):
            rows = slice(n * SLAB_ROWS, (n + 1) * SLAB_ROWS)
            spread = (wanted_ref[rows, :] == target_ref[member : member + 1, :]).astype(BF16)
            mix_ref[rows, member * (early + late) : (member + 1) * (early + late)] = lax.dot_general(
                spread, weights, (((1,), (1,)), ((), ())), preferred_element_type=F32
            ).astype(BF16)


def matrix(me, wanted, target, early, mine, got, capacity, scale):
    volume_rows = wanted.shape[0]
    _, late, orient_total = mine[0].shape
    particles = early.shape[1] + late

    def whole(shape):
        return pl.BlockSpec(shape, lambda j, me: (0,) * len(shape))

    return call(
        functools.partial(matrix_kernel, capacity, scale),
        "matrix",
        (1,),
        [whole(x.shape) for x in (wanted, target, early, *mine, *got)],
        [whole((2, late, 1)), whole((volume_rows, 2 * particles))],
        [
            jax.ShapeDtypeStruct((2, late, 1), F32),
            jax.ShapeDtypeStruct((volume_rows, 2 * particles), BF16),
        ],
        [pltpu.VMEM((particles, orient_total), BF16)],
        4 * volume_rows * particles * orient_total,
        4 * volume_rows * particles,
    )(me, wanted, target, early, *mine, *got)


def mix_kernel(count, blocks, me_ref, mix_ref, *rest):
    rows = rest[:count]
    upper_sent, upper_kept, lower_sent, lower_kept, stacked = rest[count:]
    step = pl.program_id(0)
    begin = 0
    for ref in rows:
        stacked[begin : begin + ref.shape[0], :] = ref[...]
        begin += ref.shape[0]
    total = jnp.dot(mix_ref[...], stacked[...], preferred_element_type=F32)
    middle = SLAB_ROWS // 2
    parts = [total[begin : begin + middle] for begin in range(0, total.shape[0], middle)]
    upper = jnp.concatenate(parts[0::2], axis=0)
    lower = jnp.concatenate(parts[1::2], axis=0)

    @pl.when(step % 2 == 1)
    def _():
        upper_sent[step // 2] = upper.astype(BF16)

    @pl.when(step % 2 == 0)
    def _():
        upper_kept[step // 2] = upper

    @pl.when(step >= blocks // 2)
    def _():
        lower_sent[step % (blocks // 2)] = lower.astype(BF16)

    @pl.when(step < blocks // 2)
    def _():
        lower_kept[step % (blocks // 2)] = lower


def mix(me, matrix, place, pieces, orient_count):
    rows = [piece[member] for member in range(2) for piece in pieces]
    particles = matrix.shape[1]
    half = rows[0].shape[1]
    blocks = orient_count // 2
    owned = half // blocks
    volume_rows = 2 * SLAB_ROWS
    part = (blocks // 2, SLAB_ROWS, owned)
    return call(
        functools.partial(mix_kernel, len(rows), blocks),
        "mix",
        (blocks,),
        [pl.BlockSpec((volume_rows, particles), lambda j, me: (place, 0))]
        + [pl.BlockSpec((r.shape[0], owned), lambda j, me: (0, (me[0] >> 1) ^ j)) for r in rows],
        [pl.BlockSpec(part, lambda j, me: (0, 0, 0))] * 4,
        [jax.ShapeDtypeStruct(part, BF16), jax.ShapeDtypeStruct(part, F32)] * 2,
        [pltpu.VMEM((particles, owned), BF16)],
        2 * volume_rows * particles * half,
        2 * half * (particles + volume_rows),
    )(me, matrix, *rows)


def exchange(state, n, bits):
    upper_sent, upper_kept, lower_sent, lower_kept = state
    got = (
        swap(upper_sent, "orient", 1 << bits[n]),
        swap(lower_sent, "orient", 1 << bits[-1 - n]),
    )
    return got, upper_kept, lower_kept


def add_split(got, upper_kept, lower_kept):
    upper = upper_kept + got[0].astype(F32)
    lower = lower_kept + got[1].astype(F32)
    middle = (lower.shape[0] + 1) // 2
    return upper[1::2].astype(BF16), upper[0::2], lower[middle:].astype(BF16), lower[:middle]


def body(images, bucket, panels, tile_slab, tile_row):
    orient_count = lax.axis_size("orient")
    slab_count = lax.axis_size("slab")
    me = lax.axis_index("orient")
    here = lax.axis_index("slab")
    me_ref = me.astype(jnp.int32).reshape(1)
    per_device, window = images.shape
    capacity = 2 * per_device // orient_count
    panel = panels[0]
    score_scale = BETA / math.sqrt(window)

    slot_of = slots(bucket[:, 0], orient_count, capacity)
    slot_row = slot_of[None, :]

    chips = sorted(range(1, orient_count // 2), key=lambda q: (-q.bit_count(), q))
    far, near = chips[:-2], chips[-2:]
    outgoing = gather(far[:1], me_ref, slot_row, images, orient_count, capacity)
    early = [0, 1] + [2 * q + swapped for q in far for swapped in range(2)]
    late = [2 * q + swapped for q in near for swapped in range(2)]
    order = early + late
    arrived = {}
    for offset in early[2:4]:
        arrived[offset] = [swap(half, "orient", offset) for half in outgoing[offset]]
    images = after(images, (arrived[early[2]][0], arrived[early[3]][0]))
    outgoing |= gather([0] + chips[1:], me_ref, slot_row, images, orient_count, capacity)
    arrived[0] = outgoing[0]
    for offset in early[4:] + early[1:2] + [2 * q + swapped for swapped in range(2) for q in near]:
        arrived[offset] = [swap(half, "orient", offset) for half in outgoing[offset]]
    pieces = [arrived[r] for r in order]

    both = lax.all_gather(
        panel, "orient", axis_index_groups=[[2 * q, 2 * q + 1] for q in range(orient_count // 2)]
    )
    early_pieces, late_pieces = pieces[: len(early)], pieces[len(early) :]
    early_scores = score((0, 1), me_ref, both, early_pieces, orient_count)
    early_weights, early_logs = weigh(
        me_ref, early_scores, swap(early_scores, "orient", 1), capacity, score_scale
    )
    late_scores, got_late = [], []
    for member in range(2):
        if member == 1:
            both = after(both, early_weights)
        found = score((member,), me_ref, both, late_pieces, orient_count)
        late_scores.append(found)
        got_late.append(swap(found, "orient", 1))

    within = jnp.arange(G, dtype=jnp.int32)
    buckets = (me & ~1) + jnp.arange(2, dtype=jnp.int32)
    first_rows = jnp.take(tile_slab, buckets, axis=0) * SLAB_ROWS + jnp.take(tile_row, buckets, axis=0)
    target = (first_rows[:, :, None] + within).reshape(2, -1)
    slab_order = list(range(slab_count - 1, -1, -1))
    wanted = jnp.concatenate(
        [(here ^ r) * SLAB_ROWS + jnp.arange(SLAB_ROWS, dtype=jnp.int32) for r in slab_order]
    )[:, None]
    late_logs, mixing = matrix(me_ref, wanted, target, early_weights, late_scores, got_late, capacity, score_scale)

    count = slab_count // 2
    bits = list(range(1, orient_count.bit_length() - 1))
    split, stage, sums = {}, {}, {}

    def keep(n, token):
        which = mixing if token is None else after(mixing, token)
        split[n] = mix(me_ref, which, n, pieces, orient_count)
        return split[n][1]

    def begin(n, token):
        state = tuple(split[n])
        if token is not None:
            state = after(state, token)
        stage[n] = exchange(state, 0, bits)

    def advance(n, step, token):
        landed, upper, lower = stage[n]
        state = add_split(after(landed, token), upper, lower)
        stage[n] = exchange(state, step, bits)
        return state[1]

    def gathered(n, token, tie=None):
        for step in range(2, len(bits)):
            token = advance(n, step, token)
        landed, upper, lower = stage[n]
        landed = after(landed, token if tie is None else (token, tie))
        upper = upper[0] + landed[0][0].astype(F32)
        lower = lower[0] + landed[1][0].astype(F32)
        middle = SLAB_ROWS // 2
        return [
            jnp.concatenate([upper[:middle], lower[:middle]]),
            jnp.concatenate([upper[middle:], lower[middle:]]),
        ]

    def deliver(n, totals):
        for total, offset in zip(totals, slab_order[2 * n : 2 * n + 2]):
            for block in sums.get(offset, []):
                total = total + block.astype(F32)
            if offset:
                step = offset & -offset
                token = total.astype(BF16)
                sums.setdefault(offset ^ step, []).append(swap(token, "slab", step))
        return total, token

    token = keep(0, None)
    begin(0, None)
    for n in range(count):
        if n + 1 < count:
            token = keep(n + 1, token)
        landed = stage[n][0]
        token = advance(n, 1, token)
        if n + 1 < count:
            begin(n + 1, landed)
        totals = gathered(n, token, sums[0] if n + 1 == count else None)
        volume, token = deliver(n, totals)
    logs = jnp.concatenate([early_logs, late_logs], axis=1)[:, :, 0]
    logs = lax.dynamic_index_in_dim(logs, me & 1, 0, keepdims=False)
    logsum = after(logs.reshape(orient_count, capacity), token)

    logsum = jnp.stack([logsum[order.index(r)] for r in range(orient_count)])
    logsum = jnp.take(logsum, me ^ jnp.arange(orient_count, dtype=jnp.int32), axis=0)
    returned = lax.all_to_all(logsum[:, None, :], "orient", split_axis=0, concat_axis=0, tiled=True)
    place = slot_of[None, :] == jnp.arange(orient_count * capacity, dtype=jnp.int32)[:, None]
    loglik = jnp.sum(jnp.where(place, returned.reshape(-1)[:, None], 0.0), axis=0)
    return (volume, loglik)


def solution(mesh):
    in_specs = (
        P(("orient", "slab"), None),
        P(("orient", "slab"), None),
        P("orient", None, None),
        P(),
        P(),
    )
    out_specs = (P("slab", "orient"), P(("orient", "slab")))
    return jax.shard_map(body, mesh=mesh, in_specs=in_specs, out_specs=out_specs, check_vma=False)
```

time: 409 us -> 295 us (0.72); the launches traced: 401 us -> 292 us
  matrix products: 121 us -> 0 us
  waiting for transfers between devices: 206 us -> 135 us
  Pallas kernels: 0 us -> 57.7 us
  local copies, waits for them, and re-layouts: 1.65 us -> 33 us
  starting transfers between devices: 65.4 us -> 35.6 us
  between operations: 1.22 us -> 14.7 us
  other arithmetic: 6.25 us -> 15.4 us
    all_to_all x13 -> x1, waiting for transfers between devices: 206 us -> 3.11 us  [body(): lax.all_to_all(logsum[:, None, :], 'orient', split_axis=0, concat_axis=0,...]
    ppermute x0 -> x28, waiting for transfers between devices: none -> 131 us  [swap(): return lax.ppermute(x, axis, [(i, i ^ offset) for i in range(count)])]
    dot_general x44 -> x0, matrix products: 121 us -> none  [the longest x32 60.7 us: body(): lax.dot_general(weights, block, (((0,), (0,)), ((), ())), preferred_eleme...]
    all_to_all x13 -> x1, starting transfers between devices: 65.4 us -> 4.02 us  [body(): lax.all_to_all(logsum[:, None, :], 'orient', split_axis=0, concat_axis=0,...]
    pallas_call x0 -> x9, Pallas kernels: none -> 57.7 us  [the longest x2 21.8 us: mix(): call(functools.partial(mix_kernel, len(rows), blocks), 'mix', (blocks,),...]
    ppermute x0 -> x28, starting transfers between devices: none -> 31.6 us  [swap(): return lax.ppermute(x, axis, [(i, i ^ offset) for i in range(count)])]
    unnamed x12 -> x110, local copies, waits for them, and re-layouts: 0.02 us -> 25.2 us
    add x3 -> x13, other arithmetic: 0.14 us -> 9.3 us  [the longest x1 2.41 us: deliver(): total = total + block.astype(F32)]
  transfers between devices with their start and end apart: 13 -> 30, of which waited for: 13 -> 18; matrix products, arithmetic and copies ran while one was open for 25% -> 6% of each run, Pallas kernels for 0% -> 15%
where the time goes in v3:
time: 295 us; the launch traced here: 292 us
  waiting for transfers between devices  135 us (46%)
  Pallas kernels  57.7 us (20%)
  starting transfers between devices  35.6 us (12%)
  local copies, waits for them, and re-layouts  33 us (11%)
  other arithmetic  15.4 us (5%)
  between operations  14.7 us (5%)
    ppermute x28, waiting for transfers between devices, swap(): return lax.ppermute(x, axis, [(i, i ^ offset) for i in range(count)])  131 us
    ppermute x28, starting transfers between devices, swap(): return lax.ppermute(x, axis, [(i, i ^ offset) for i in range(count)])  31.6 us
    unnamed x110, local copies, waits for them, and re-layouts  25.2 us
    pallas_call x2, Pallas kernels, mix(): call(functools.partial(mix_kernel, len(rows), blocks), 'mix', (blocks,),...  21.8 us
    pallas_call x3, Pallas kernels, score(): call(functools.partial(score_kernel, members, len(pieces)), 'score', (ori...  17.5 us
    pallas_call x2, Pallas kernels, gather(): call(functools.partial(gather_kernel, chips, capacity, owned), 'gather',...  13.7 us
  transfers between devices with their start and end apart: 30, of which 18 were waited for; matrix products, arithmetic and copies ran while one was open for 6% of the time, Pallas kernels for 15%

profile of v3, /device:TPU:2, one launch (start us, length us, event | category | flops | bytes accessed | tf_op | source)
XLA Modules:
  0.0 291.5 jit_solution(11304503517921567391)
XLA Ops:
  9.2 2.8 copy-done.6
  12.0 4.7 %gather.22 = (bf16[96,4096]{1,0:T(8,128)(2,1)S(1)}, bf16[96,4096]{1,0:T(8,128)(2,1)}, bf16[96,4096]{1,0:T(8,128)(2,1)S(1)}, bf16[96,4096]{1,0:T(8,128)(2,1)}) custom-call(s32[1]{0:T(128)} %bitcast.me_ref, s32[1,384]{1,0:T(1,128)S(1)} %bitcast_add_fusion.slot_ref, bf16[384,8192]{1,0:T(8,128)(2,1)S(1)} %copy-done.6), custom_call_target="tpu_custom_call" | custom-call | flops 24159191040 | bytes 188743680 | tf_op jit(solution)/shard_map/gather/pallas_call | solution.py:82
  20.3 1.7 collective-permute-start.5
  22.0 16.0 %collective-permute-done.rest_2_ = bf16[96,4096]{1,0:T(8,128)(2,1)S(1)} collective-permute-done((bf16[96,4096]{1,0:T(8,128)(2,1)S(1)}, bf16[96,4096]{1,0:T(8,128)(2,1)S(1)}, u32[]{:S(2)}, u32[]{:S(2)}) %collective-permute-start) | collective-permute-done | bytes 786464 | tf_op jit(solution)/shard_map/ppermute | solution.py:31
  38.0 14.9 %collective-permute-done.1.rest_3_ = bf16[96,4096]{1,0:T(8,128)(2,1)S(1)} collective-permute-done((bf16[96,4096]{1,0:T(8,128)(2,1)S(1)}, bf16[96,4096]{1,0:T(8,128)(2,1)S(1)}, u32[]{:S(2)}, u32[]{:S(2)}) %collective-permute-start.1) | collective-permute-done | bytes 786464 | tf_op jit(solution)/shard_map/ppermute | solution.py:31
  53.0 9.0 %gather.23 = (bf16[96,4096]{1,0:T(8,128)(2,1)S(1)}, bf16[96,4096]{1,0:T(8,128)(2,1)S(1)}, bf16[96,4096]{1,0:T(8,128)(2,1)}, bf16[96,4096]{1,0:T(8,128)(2,1)}, bf...) custom-call(s32[1]{0:T(128)} %bitcast.me_ref, ...), custom_call_target="tpu_custom_call" | custom-call | flops 72477573120 | bytes 314572800 | tf_op jit(solution)/shard_map/gather/pallas_call | solution.py:82
  69.2 1.8 collective-permute-start.2
  72.8 14.0 %collective-permute-done.5.rest_7_.rest_11_ = bf16[96,4096]{1,0:T(8,128)(2,1)} collective-permute-done((bf16[96,4096]{1,0:T(8,128)(2,1)}, bf16[96,4096]{1,0:T(8,128)(2,1)}, u32[]{:S(2)}, u32[]{:S(2)}) %collective-permute-start.5) | collective-permute-done | bytes 786464 | tf_op jit(solution)/shard_map/ppermute | solution.py:31
  91.5 5.8 %copy-done.4 = bf16[2,512,8192]{2,1,0:T(8,128)(2,1)S(1)} copy-done((bf16[2,512,8192]{2,1,0:T(8,128)(2,1)S(1)}, bf16[2,512,8192]{2,1,0:T(8,128)(2,1)}, u32[]{:S(2)}) %copy-start.4) | copy-done | bytes 16777240
  99.5 7.5 %score.3.mine_ref = f32[2,384,512]{2,1,0:T(8,128)S(1)} custom-call(s32[1]{0:T(128)} %bitcast.me_ref, bf16[2,512,8192]{2,1,0:T(8,128)(2,1)S(1)} %copy-done.4, bf16[96,4096]{1,0:T(8,128)(2,1)S(1)} %copy-done.36, bf16[96,4096]{1,0:T(8,128)(2,1)} %collective-permute-done.2.rest_1_, bf16[96,4096]{1,0:T(8,128)(2,1)S(1)} %collective-permute-done.rest_2_, ...), custom_call_target="tpu_custom_call" | custom-call | flops 64424509440 | bytes 293601280 | tf_op jit(solution)/shard_map/score/pallas_call | solution.py:124
  107.1 15.4 %collective-permute-done.7.rest_0_.rest_4_ = bf16[96,4096]{1,0:T(8,128)(2,1)} collective-permute-done((bf16[96,4096]{1,0:T(8,128)(2,1)}, bf16[96,4096]{1,0:T(8,128)(2,1)}, u32[]{:S(2)}, u32[]{:S(2)}) %collective-permute-start.7) | collective-permute-done | bytes 786464 | tf_op jit(solution)/shard_map/ppermute | solution.py:31
  123.0 14.3 %collective-permute-done.8.rest_1_.rest_5_ = bf16[96,4096]{1,0:T(8,128)(2,1)} collective-permute-done((bf16[96,4096]{1,0:T(8,128)(2,1)}, bf16[96,4096]{1,0:T(8,128)(2,1)}, u32[]{:S(2)}, u32[]{:S(2)}) %collective-permute-start.8) | collective-permute-done | bytes 786464 | tf_op jit(solution)/shard_map/ppermute | solution.py:31
  137.4 2.1 collective-permute-start.14
  139.5 4.7 %score.4.rest_0_ = f32[1,384,512]{2,1,0:T(8,128)S(1)} custom-call(s32[1]{0:T(128)} %bitcast.me_ref, bf16[2,512,8192]{2,1,0:T(8,128)(2,1)S(1)} %copy-done.5, bf16[96,4096]{1,0:T(8,128)(2,1)} %collective-permute-done.7.rest_0_.rest_4_, bf16[96,4096]{1,0:T(8,128)(2,1)} %collective-permute-done.8.rest_1_.rest_5_, ...), custom_call_target="tpu_custom_call" | custom-call | flops 32212254720 | bytes 293601280 | tf_op jit(solution)/shard_map/score/pallas_call | solution.py:124
  145.5 8.3 %collective-permute-done.12.rest_1_.rest_13_ = bf16[96,4096]{1,0:T(8,128)(2,1)S(1)} collective-permute-done((bf16[96,4096]{1,0:T(8,128)(2,1)S(1)}, bf16[96,4096]{1,0:T(8,128)(2,1)S(1)}, u32[]{:S(2)}, u32[]{:S(2)}) %collective-permute-start.12) | collective-permute-done | bytes 786464 | tf_op jit(solution)/shard_map/ppermute | solution.py:31
  153.7 2.9 collective-permute-done.14.rest_3_.rest_15_
  156.6 5.3 %score.5.rest_1_ = f32[1,384,512]{2,1,0:T(8,128)} custom-call(s32[1]{0:T(128)} %bitcast.me_ref, bf16[2,512,8192]{2,1,0:T(8,128)(2,1)S(1)} %copy-done.5, bf16[96,4096]{1,0:T(8,128)(2,1)} %collective-permute-done.11.rest_0_.rest_12_, bf16[96,4096]{1,0:T(8,128)(2,1)S(1)} %collective-permute-done.12.rest_1_.rest_13_, ...), custom_call_target="tpu_custom_call" | custom-call | flops 32212254720 | bytes 293601280 | tf_op jit(solution)/shard_map/score/pallas_call | solution.py:124
  167.5 4.1 %matrix.1 = (f32[2,384,1]{2,1,0:T(8,128)S(1)}, bf16[1024,1536]{1,0:T(8,128)(2,1)S(1)}) custom-call(s32[1]{0:T(128)} %bitcast.me_ref, s32[1024,1]{1,0:T(8,128)S(1)} %copy.12.wanted_ref, s32[2,512]{1,0:T(2,128)S(1)} %broadcast_add_fusion.target_ref, bf16[2,384,512]{2,1,0:T(8,128)(2,1)S(1)} %copy-done.34, f32[1,384,512]{2,1,0:T(8,128)S(1)} %copy-done.32, ...), custom_call_target="tpu_custom_call" | custom-call | flops 32212254720 | bytes 62914560 | tf_op jit(solution)/shard_map/matrix/pallas_call | solution.py:203
  171.7 10.4 %mix.2 = (bf16[2,256,1024]{2,1,0:T(8,128)(2,1)S(1)}, f32[2,256,1024]{2,1,0:T(8,128)S(1)}, bf16[2,256,1024]{2,1,0:T(8,128)(2,1)S(1)}, f32[2,256,1024]{2,1,0:T(8,128)S(1)}) custom-call(s32[1]{0:T(128)} %bitcast.me_ref, bf16[1024,1536]{1,0:T(8,128)(2,1)S(1)} %get-tuple-element.68.mix_ref, bf16[96,4096]{1,0:T(8,128)(2,1)S(1)} %copy-done.37, ...), custom_call_target="tpu_custom_call" | custom-call | flops 128849018880 | bytes 335544320 | tf_op jit(solution)/shard_map/mix/pallas_call | solution.py:258
  185.7 11.5 %mix.3 = (bf16[2,256,1024]{2,1,0:T(8,128)(2,1)}, f32[2,256,1024]{2,1,0:T(8,128)S(1)}, bf16[2,256,1024]{2,1,0:T(8,128)(2,1)}, f32[2,256,1024]{2,1,0:T(8,128)S(1)}) custom-call(s32[1]{0:T(128)} %bitcast.me_ref, bf16[1024,1536]{1,0:T(8,128)(2,1)S(1)} %get-tuple-element.68.mix_ref, bf16[96,4096]{1,0:T(8,128)(2,1)S(1)} %copy-done.37, ...), custom_call_target="tpu_custom_call" | custom-call | flops 128849018880 | bytes 335544320 | tf_op jit(solution)/shard_map/mix/pallas_call | solution.py:258
  197.1 10.5 %collective-permute-done.17 = bf16[2,256,1024]{2,1,0:T(8,128)(2,1)S(1)} collective-permute-done((bf16[2,256,1024]{2,1,0:T(8,128)(2,1)S(1)}, bf16[2,256,1024]{2,1,0:T(8,128)(2,1)S(1)}, u32[]{:S(2)}, u32[]{:S(2)}) %collective-permute-start.17) | collective-permute-done | bytes 1048608 | tf_op jit(solution)/shard_map/ppermute | solution.py:31
  213.5 10.4 %collective-permute-done.21 = bf16[1,256,1024]{2,1,0:T(8,128)(2,1)S(1)} collective-permute-done((bf16[1,256,1024]{2,1,0:T(8,128)(2,1)S(1)}, bf16[1,256,1024]{2,1,0:T(8,128)(2,1)S(1)}, u32[]{:S(2)}, u32[]{:S(2)}) %collective-permute-start.21) | collective-permute-done | bytes 524320 | tf_op jit(solution)/shard_map/ppermute | solution.py:31
  226.7 1.7 collective-permute-start.23
  230.7 6.7 %collective-permute-done.23 = bf16[256,1024]{1,0:T(8,128)(2,1)} collective-permute-done((bf16[256,1024]{1,0:T(8,128)(2,1)S(1)}, bf16[256,1024]{1,0:T(8,128)(2,1)}, u32[]{:S(2)}, u32[]{:S(2)}) %collective-permute-start.23) | collective-permute-done | bytes 524320 | tf_op jit(solution)/shard_map/ppermute | solution.py:31
  237.4 2.0 fusion
  239.4 2.3 collective-permute-start.26
  241.7 4.2 %collective-permute-done.19 = bf16[2,256,1024]{2,1,0:T(8,128)(2,1)} collective-permute-done((bf16[2,256,1024]{2,1,0:T(8,128)(2,1)}, bf16[2,256,1024]{2,1,0:T(8,128)(2,1)}, u32[]{:S(2)}, u32[]{:S(2)}) %collective-permute-start.19) | collective-permute-done | bytes 1048608 | tf_op jit(solution)/shard_map/ppermute | solution.py:31
  254.8 6.3 %collective-permute-done.24 = bf16[1,256,1024]{2,1,0:T(8,128)(2,1)S(1)} collective-permute-done((bf16[1,256,1024]{2,1,0:T(8,128)(2,1)}, bf16[1,256,1024]{2,1,0:T(8,128)(2,1)S(1)}, u32[]{:S(2)}, u32[]{:S(2)}) %collective-permute-start.24) | collective-permute-done | bytes 524320 | tf_op jit(solution)/shard_map/ppermute | solution.py:31
  261.1 4.4 %collective-permute-done.25 = bf16[1,256,1024]{2,1,0:T(8,128)(2,1)} collective-permute-done((bf16[1,256,1024]{2,1,0:T(8,128)(2,1)}, bf16[1,256,1024]{2,1,0:T(8,128)(2,1)}, u32[]{:S(2)}, u32[]{:S(2)}) %collective-permute-start.25) | collective-permute-done | bytes 524320 | tf_op jit(solution)/shard_map/ppermute | solution.py:31
  273.0 4.0 %all-to-all-start = ((f32[8,1,96]{2,1,0:T(1,128)}), f32[8,1,96]{2,1,0:T(1,128)S(1)}, u32[]{:S(2)}, u32[]{:S(2)}) async-start(f32[8,1,96]{2,1,0:T(1,128)} %bitcast.15), calls=%async_computation | async-start | bytes 8192 | tf_op jit(solution)/shard_map/all_to_all | solution.py:405
  277.1 3.1 %all-to-all-done = f32[8,1,96]{2,1,0:T(1,128)S(1)} async-done(((f32[8,1,96]{2,1,0:T(1,128)}), f32[8,1,96]{2,1,0:T(1,128)S(1)}, u32[]{:S(2)}, u32[]{:S(2)}) %all-to-all-start) | async-done | bytes 3104 | tf_op jit(solution)/shard_map/all_to_all | solution.py:405
  282.3 2.4 fusion.1
  (211 shorter events, 61.6 us)
Async XLA Ops:
  7.2 155.9 %copy-start = (s32[8,64]{1,0:T(8,128)S(1)}, s32[8,64]{1,0:T(8,128)}, u32[]{:S(2)}) copy-start(s32[8,64]{1,0:T(8,128)} %param.10) | copy-start | bytes 6148
  7.2 84.3 %all-gather.2.cloned.1.call-start = ((), (), s32[]{:S(2)}) async-start(), calls=%async_computation.1 | async-start | bytes 25165824 | tf_op jit(solution)/shard_map/all_gather | solution.py:318
  16.7 21.3 %collective-permute-start = (bf16[96,4096]{1,0:T(8,128)(2,1)S(1)}, bf16[96,4096]{1,0:T(8,128)(2,1)S(1)}, u32[]{:S(2)}, u32[]{:S(2)}) collective-permute-start(bf16[96,4096]{1,0:T(8,128)(2,1)S(1)} %get-tuple-element.47), channel_id=1, source_target_pairs={{0,24},{4,28},{8,16},{12,20},{16,8},{20,12},{24,0},{28,4},{1,25},{... | collective-permute-start | bytes 2359304 | tf_op jit(solution)/shard_map/ppermute | solution.py:31
  18.2 34.8 %collective-permute-start.1 = (bf16[96,4096]{1,0:T(8,128)(2,1)S(1)}, bf16[96,4096]{1,0:T(8,128)(2,1)S(1)}, u32[]{:S(2)}, u32[]{:S(2)}) collective-permute-start(bf16[96,4096]{1,0:T(8,128)(2,1)S(1)} %get-tuple-element.48), channel_id=1, source_target_pairs={{0,28},{4,24},{8,20},{12,16},{16,12},{20,8},{24,4},{28,0},{1,29},{... | collective-permute-start | bytes 2359304 | tf_op jit(solution)/shard_map/ppermute | solution.py:31
  18.8 53.0 %collective-permute-start.4 = (bf16[96,4096]{1,0:T(8,128)(2,1)}, bf16[96,4096]{1,0:T(8,128)(2,1)S(1)}, u32[]{:S(2)}, u32[]{:S(2)}) collective-permute-start(bf16[96,4096]{1,0:T(8,128)(2,1)} %get-tuple-element.54), channel_id=1, source_target_pairs={{0,24},{4,28},{8,16},{12,20},{16,8},{20,12},{24,0},{28,4},{1,25},{... | collective-permute-start | bytes 2359304 | tf_op jit(solution)/shard_map/ppermute | solution.py:31
  20.3 66.5 %collective-permute-start.5 = (bf16[96,4096]{1,0:T(8,128)(2,1)}, bf16[96,4096]{1,0:T(8,128)(2,1)}, u32[]{:S(2)}, u32[]{:S(2)}) collective-permute-start(bf16[96,4096]{1,0:T(8,128)(2,1)} %get-tuple-element.55), channel_id=1, source_target_pairs={{0,28},{4,24},{8,20},{12,16},{16,12},{20,8},{24,4},{28,0},{1,29},{... | collective-permute-start | bytes 2359304 | tf_op jit(solution)/shard_map/ppermute | solution.py:31
  38.0 133.6 %copy-start.8 = (bf16[96,4096]{1,0:T(8,128)(2,1)}, bf16[96,4096]{1,0:T(8,128)(2,1)S(1)}, u32[]{:S(2)}) copy-start(bf16[96,4096]{1,0:T(8,128)(2,1)S(1)} %collective-permute-done.rest_2_) | copy-start | bytes 2359300
  69.2 19.2 %collective-permute-start.2 = (bf16[96,4096]{1,0:T(8,128)(2,1)}, bf16[96,4096]{1,0:T(8,128)(2,1)}, u32[]{:S(2)}, u32[]{:S(2)}) collective-permute-start(bf16[96,4096]{1,0:T(8,128)(2,1)} %get-tuple-element.51), channel_id=1, source_target_pairs={{0,4},{4,0},{8,12},{12,8},{16,20},{20,16},{24,28},{28,24},{1,5},{5... | collective-permute-start | bytes 2359304 | tf_op jit(solution)/shard_map/ppermute | solution.py:31
  70.9 19.0 %collective-permute-start.3 = (bf16[96,4096]{1,0:T(8,128)(2,1)}, bf16[96,4096]{1,0:T(8,128)(2,1)}, u32[]{:S(2)}, u32[]{:S(2)}) collective-permute-start(bf16[96,4096]{1,0:T(8,128)(2,1)} %get-tuple-element.53), channel_id=1, source_target_pairs={{0,4},{4,0},{8,12},{12,8},{16,20},{20,16},{24,28},{28,24},{1,5},{5... | collective-permute-start | bytes 2359304 | tf_op jit(solution)/shard_map/ppermute | solution.py:31
  71.4 74.0 %collective-permute-start.11 = (bf16[96,4096]{1,0:T(8,128)(2,1)}, bf16[96,4096]{1,0:T(8,128)(2,1)}, u32[]{:S(2)}, u32[]{:S(2)}) collective-permute-start(bf16[96,4096]{1,0:T(8,128)(2,1)} %copy-done.24), channel_id=1, source_target_pairs={{0,8},{4,12},{8,0},{12,4},{16,24},{20,28},{24,16},{28,20},{1,9},{5... | collective-permute-start | bytes 2359304 | tf_op jit(solution)/shard_map/ppermute | solution.py:31
  71.8 35.3 %collective-permute-start.10 = (bf16[96,4096]{1,0:T(8,128)(2,1)}, bf16[96,4096]{1,0:T(8,128)(2,1)}, u32[]{:S(2)}, u32[]{:S(2)}) collective-permute-start(bf16[96,4096]{1,0:T(8,128)(2,1)} %copy-done.30), channel_id=1, source_target_pairs={{0,20},{4,16},{8,28},{12,24},{16,4},{20,0},{24,12},{28,8},{1,21},{... | collective-permute-start | bytes 2359304 | tf_op jit(solution)/shard_map/ppermute | solution.py:31
  86.8 35.7 %collective-permute-start.7 = (bf16[96,4096]{1,0:T(8,128)(2,1)}, bf16[96,4096]{1,0:T(8,128)(2,1)}, u32[]{:S(2)}, u32[]{:S(2)}) collective-permute-start(bf16[96,4096]{1,0:T(8,128)(2,1)} %copy-done.29), channel_id=1, source_target_pairs={{0,8},{4,12},{8,0},{12,4},{16,24},{20,28},{24,16},{28,20},{1,9},{5... | collective-permute-start | bytes 2359304 | tf_op jit(solution)/shard_map/ppermute | solution.py:31
  88.4 49.0 %collective-permute-start.8 = (bf16[96,4096]{1,0:T(8,128)(2,1)}, bf16[96,4096]{1,0:T(8,128)(2,1)}, u32[]{:S(2)}, u32[]{:S(2)}) collective-permute-start(bf16[96,4096]{1,0:T(8,128)(2,1)} %copy-done.28), channel_id=1, source_target_pairs={{0,12},{4,8},{8,4},{12,0},{16,28},{20,24},{24,20},{28,16},{1,13},{... | collective-permute-start | bytes 2359304 | tf_op jit(solution)/shard_map/ppermute | solution.py:31
  89.9 49.6 %collective-permute-start.9 = (bf16[96,4096]{1,0:T(8,128)(2,1)}, bf16[96,4096]{1,0:T(8,128)(2,1)}, u32[]{:S(2)}, u32[]{:S(2)}) collective-permute-start(bf16[96,4096]{1,0:T(8,128)(2,1)} %copy-done.27), channel_id=1, source_target_pairs={{0,16},{4,20},{8,24},{12,28},{16,0},{20,4},{24,8},{28,12},{1,17},{... | collective-permute-start | bytes 2359304 | tf_op jit(solution)/shard_map/ppermute | solution.py:31
  107.1 46.7 %collective-permute-start.12 = (bf16[96,4096]{1,0:T(8,128)(2,1)S(1)}, bf16[96,4096]{1,0:T(8,128)(2,1)S(1)}, u32[]{:S(2)}, u32[]{:S(2)}) collective-permute-start(bf16[96,4096]{1,0:T(8,128)(2,1)S(1)} %copy-done.23), channel_id=1, source_target_pairs={{0,12},{4,8},{8,4},{12,0},{16,28},{20,24},{24,20},{28,16},{1,13},{... | collective-permute-start | bytes 2359304 | tf_op jit(solution)/shard_map/ppermute | solution.py:31
  122.5 31.2 %collective-permute-start.13 = (bf16[96,4096]{1,0:T(8,128)(2,1)S(1)}, bf16[96,4096]{1,0:T(8,128)(2,1)S(1)}, u32[]{:S(2)}, u32[]{:S(2)}) collective-permute-start(bf16[96,4096]{1,0:T(8,128)(2,1)S(1)} %copy-done.19), channel_id=1, source_target_pairs={{0,16},{4,20},{8,24},{12,28},{16,0},{20,4},{24,8},{28,12},{1,17},{... | collective-permute-start | bytes 2359304 | tf_op jit(solution)/shard_map/ppermute | solution.py:31
  137.4 19.3 %collective-permute-start.14 = (bf16[96,4096]{1,0:T(8,128)(2,1)S(1)}, bf16[96,4096]{1,0:T(8,128)(2,1)S(1)}, u32[]{:S(2)}, u32[]{:S(2)}) collective-permute-start(bf16[96,4096]{1,0:T(8,128)(2,1)S(1)} %copy-done.17), channel_id=1, source_target_pairs={{0,20},{4,16},{8,28},{12,24},{16,4},{20,0},{24,12},{28,8},{1,21},{... | collective-permute-start | bytes 2359304 | tf_op jit(solution)/shard_map/ppermute | solution.py:31
  139.5 4.7 %collective-permute-start.6 = (f32[2,384,512]{2,1,0:T(8,128)S(1)}, f32[2,384,512]{2,1,0:T(8,128)S(1)}, u32[]{:S(2)}, u32[]{:S(2)}) collective-permute-start(f32[2,384,512]{2,1,0:T(8,128)S(1)} %score.3.mine_ref), channel_id=1, source_target_pairs={{0,4},{4,0},{8,12},{12,8},{16,20},{20,16},{24,28},{28,24},{1,5},{5... | collective-permute-start | bytes 4718600 | tf_op jit(solution)/shard_map/ppermute | solution.py:31
  144.2 20.4 %collective-permute-start.15 = (f32[1,384,512]{2,1,0:T(8,128)S(1)}, f32[1,384,512]{2,1,0:T(8,128)}, u32[]{:S(2)}, u32[]{:S(2)}) collective-permute-start(f32[1,384,512]{2,1,0:T(8,128)S(1)} %score.4.rest_0_), channel_id=1, source_target_pairs={{0,4},{4,0},{8,12},{12,8},{16,20},{20,16},{24,28},{28,24},{1,5},{5... | collective-permute-start | bytes 2359304 | tf_op jit(solution)/shard_map/ppermute | solution.py:31
  161.9 3.1 %collective-permute-start.16 = (f32[1,384,512]{2,1,0:T(8,128)}, f32[1,384,512]{2,1,0:T(8,128)}, u32[]{:S(2)}, u32[]{:S(2)}) collective-permute-start(f32[1,384,512]{2,1,0:T(8,128)} %score.5.rest_1_), channel_id=1, source_target_pairs={{0,4},{4,0},{8,12},{12,8},{16,20},{20,16},{24,28},{28,24},{1,5},{5... | collective-permute-start | bytes 2359304 | tf_op jit(solution)/shard_map/ppermute | solution.py:31
  182.0 25.6 %collective-permute-start.17 = (bf16[2,256,1024]{2,1,0:T(8,128)(2,1)S(1)}, bf16[2,256,1024]{2,1,0:T(8,128)(2,1)S(1)}, u32[]{:S(2)}, u32[]{:S(2)}) collective-permute-start(bf16[2,256,1024]{2,1,0:T(8,128)(2,1)S(1)} %get-tuple-element.73), channel_id=1, source_target_pairs={{0,8},{4,12},{8,0},{12,4},{16,24},{20,28},{24,16},{28,20},{1,9},{5... | collective-permute-start | bytes 3145736 | tf_op jit(solution)/shard_map/ppermute | solution.py:31
  183.3 25.3 %collective-permute-start.18 = (bf16[2,256,1024]{2,1,0:T(8,128)(2,1)S(1)}, bf16[2,256,1024]{2,1,0:T(8,128)(2,1)S(1)}, u32[]{:S(2)}, u32[]{:S(2)}) collective-permute-start(bf16[2,256,1024]{2,1,0:T(8,128)(2,1)S(1)} %get-tuple-element.74), channel_id=1, source_target_pairs={{0,16},{4,20},{8,24},{12,28},{16,0},{20,4},{24,8},{28,12},{1,17},{... | collective-permute-start | bytes 3145736 | tf_op jit(solution)/shard_map/ppermute | solution.py:31
  209.0 14.9 %collective-permute-start.21 = (bf16[1,256,1024]{2,1,0:T(8,128)(2,1)S(1)}, bf16[1,256,1024]{2,1,0:T(8,128)(2,1)S(1)}, u32[]{:S(2)}, u32[]{:S(2)}) collective-permute-start(bf16[1,256,1024]{2,1,0:T(8,128)(2,1)S(1)} %slice.187), channel_id=1, source_target_pairs={{0,16},{4,20},{8,24},{12,28},{16,0},{20,4},{24,8},{28,12},{1,17},{... | collective-permute-start | bytes 1572872 | tf_op jit(solution)/shard_map/ppermute | solution.py:31
  210.1 14.9 %collective-permute-start.22 = (bf16[1,256,1024]{2,1,0:T(8,128)(2,1)S(1)}, bf16[1,256,1024]{2,1,0:T(8,128)(2,1)S(1)}, u32[]{:S(2)}, u32[]{:S(2)}) collective-permute-start(bf16[1,256,1024]{2,1,0:T(8,128)(2,1)S(1)} %slice.186), channel_id=1, source_target_pairs={{0,8},{4,12},{8,0},{12,4},{16,24},{20,28},{24,16},{28,20},{1,9},{5... | collective-permute-start | bytes 1572872 | tf_op jit(solution)/shard_map/ppermute | solution.py:31
  211.9 34.1 %collective-permute-start.19 = (bf16[2,256,1024]{2,1,0:T(8,128)(2,1)}, bf16[2,256,1024]{2,1,0:T(8,128)(2,1)}, u32[]{:S(2)}, u32[]{:S(2)}) collective-permute-start(bf16[2,256,1024]{2,1,0:T(8,128)(2,1)} %get-tuple-element.76), channel_id=1, source_target_pairs={{0,8},{4,12},{8,0},{12,4},{16,24},{20,28},{24,16},{28,20},{1,9},{5... | collective-permute-start | bytes 3145736 | tf_op jit(solution)/shard_map/ppermute | solution.py:31
  212.2 33.7 %collective-permute-start.20 = (bf16[2,256,1024]{2,1,0:T(8,128)(2,1)}, bf16[2,256,1024]{2,1,0:T(8,128)(2,1)}, u32[]{:S(2)}, u32[]{:S(2)}) collective-permute-start(bf16[2,256,1024]{2,1,0:T(8,128)(2,1)} %get-tuple-element.77), channel_id=1, source_target_pairs={{0,16},{4,20},{8,24},{12,28},{16,0},{20,4},{24,8},{28,12},{1,17},{... | collective-permute-start | bytes 3145736 | tf_op jit(solution)/shard_map/ppermute | solution.py:31
  226.7 10.8 %collective-permute-start.23 = (bf16[256,1024]{1,0:T(8,128)(2,1)S(1)}, bf16[256,1024]{1,0:T(8,128)(2,1)}, u32[]{:S(2)}, u32[]{:S(2)}) collective-permute-start(bf16[256,1024]{1,0:T(8,128)(2,1)S(1)} %pad_maximum_fusion), channel_id=1, source_target_pairs={{0,1},{1,0},{2,3},{3,2},{4,5},{5,4},{6,7},{7,6},{8,9},{9,8},{10,11... | collective-permute-start | bytes 1572872 | tf_op jit(solution)/shard_map/ppermute | solution.py:31
  239.4 26.1 %collective-permute-start.26 = (bf16[256,1024]{1,0:T(8,128)(2,1)}, bf16[256,1024]{1,0:T(8,128)(2,1)}, u32[]{:S(2)}, u32[]{:S(2)}) collective-permute-start(bf16[256,1024]{1,0:T(8,128)(2,1)} %fusion), channel_id=1, source_target_pairs={{0,2},{1,3},{2,0},{3,1},{4,6},{5,7},{6,4},{7,5},{8,10},{9,11},{10,... | collective-permute-start | bytes 1572872 | tf_op jit(solution)/shard_map/ppermute | solution.py:31
  248.6 12.5 %collective-permute-start.24 = (bf16[1,256,1024]{2,1,0:T(8,128)(2,1)}, bf16[1,256,1024]{2,1,0:T(8,128)(2,1)S(1)}, u32[]{:S(2)}, u32[]{:S(2)}) collective-permute-start(bf16[1,256,1024]{2,1,0:T(8,128)(2,1)} %slice.185), channel_id=1, source_target_pairs={{0,16},{4,20},{8,24},{12,28},{16,0},{20,4},{24,8},{28,12},{1,17},{... | collective-permute-start | bytes 1572872 | tf_op jit(solution)/shard_map/ppermute | solution.py:31
  253.4 12.1 %collective-permute-start.25 = (bf16[1,256,1024]{2,1,0:T(8,128)(2,1)}, bf16[1,256,1024]{2,1,0:T(8,128)(2,1)}, u32[]{:S(2)}, u32[]{:S(2)}) collective-permute-start(bf16[1,256,1024]{2,1,0:T(8,128)(2,1)} %slice.184), channel_id=1, source_target_pairs={{0,8},{4,12},{8,0},{12,4},{16,24},{20,28},{24,16},{28,20},{1,9},{5... | collective-permute-start | bytes 1572872 | tf_op jit(solution)/shard_map/ppermute | solution.py:31
  270.2 12.1 %collective-permute-start.27 = (bf16[256,1024]{1,0:T(8,128)(2,1)}, bf16[256,1024]{1,0:T(8,128)(2,1)}, u32[]{:S(2)}, u32[]{:S(2)}) collective-permute-start(bf16[256,1024]{1,0:T(8,128)(2,1)} %pad_maximum_fusion.1), channel_id=1, source_target_pairs={{0,1},{1,0},{2,3},{3,2},{4,5},{5,4},{6,7},{7,6},{8,9},{9,8},{10,11... | collective-permute-start | bytes 1572872 | tf_op jit(solution)/shard_map/ppermute | solution.py:31
  273.0 7.2 %all-to-all-start = ((f32[8,1,96]{2,1,0:T(1,128)}), f32[8,1,96]{2,1,0:T(1,128)S(1)}, u32[]{:S(2)}, u32[]{:S(2)}) async-start(f32[8,1,96]{2,1,0:T(1,128)} %bitcast.15), calls=%async_computation | async-start | bytes 8192 | tf_op jit(solution)/shard_map/all_to_all | solution.py:405
  (53 other events, 467.3 us)
Sparse Core Ops, SparseCore 0:
  9.6 31.5 all-gather.1

commit v4 on v3

--- a/solution.py
+++ b/solution.py
@@ -342,6 +342,7 @@
     late_logs, mixing = matrix(me_ref, wanted, target, early_weights, late_scores, got_late, capacity, score_scale)
 
     count = slab_count // 2
+    middle = SLAB_ROWS // 2
     bits = list(range(1, orient_count.bit_length() - 1))
     split, stage, sums = {}, {}, {}
 
@@ -359,17 +360,31 @@
     def advance(n, step, token):
         landed, upper, lower = stage[n]
         state = add_split(after(landed, token), upper, lower)
-        stage[n] = exchange(state, step, bits)
+        if n + 1 == count and step + 1 == len(bits):
+            stage[n] = [
+                exchange(tuple(x[:, begin : begin + middle] for x in state), step, bits)
+                for begin in (0, middle)
+            ]
+        else:
+            stage[n] = exchange(state, step, bits)
         return state[1]
 
     def gathered(n, token, tie=None):
         for step in range(2, len(bits)):
             token = advance(n, step, token)
+        if n + 1 == count:
+            totals = []
+            for k, (landed, upper, lower) in enumerate(stage[n]):
+                landed = after(landed, (token, tie) if k == 0 else token)
+                token = jnp.concatenate(
+                    [upper[0] + landed[0][0].astype(F32), lower[0] + landed[1][0].astype(F32)]
+                )
+                totals.append(token)
+            return totals
         landed, upper, lower = stage[n]
-        landed = after(landed, token if tie is None else (token, tie))
+        landed = after(landed, token)
         upper = upper[0] + landed[0][0].astype(F32)
         lower = lower[0] + landed[1][0].astype(F32)
-        middle = SLAB_ROWS // 2
         return [
             jnp.concatenate([upper[:middle], lower[:middle]]),
             jnp.concatenate([upper[middle:], lower[middle:]]),
@@ -399,7 +414,6 @@
     logs = jnp.concatenate([early_logs, late_logs], axis=1)[:, :, 0]
     logs = lax.dynamic_index_in_dim(logs, me & 1, 0, keepdims=False)
     logsum = after(logs.reshape(orient_count, capacity), token)
-
     logsum = jnp.stack([logsum[order.index(r)] for r in range(orient_count)])
     logsum = jnp.take(logsum, me ^ jnp.arange(orient_count, dtype=jnp.int32), axis=0)
     returned = lax.all_to_all(logsum[:, None, :], "orient", split_axis=0, concat_axis=0, tiled=True)

time: 295 us -> 287 us (0.973)
  local copies, waits for them, and re-layouts: 33 us -> 24 us
    unnamed x110 -> x78, local copies, waits for them, and re-layouts: 25.2 us -> 20.3 us
    add x0 -> x4, other arithmetic: none -> 4.54 us  [the longest x2 2.28 us: gathered(): lower[0] + landed[1][0].astype(F32)]
    another operation x2 -> x4, other arithmetic: 0.91 us -> 4.52 us
    ppermute x28 -> x30, starting transfers between devices: 31.6 us -> 33.2 us  [swap(): return lax.ppermute(x, axis, [(i, i ^ offset) for i in range(count)])]
    ppermute x28 -> x30, waiting for transfers between devices: 131 us -> 133 us  [swap(): return lax.ppermute(x, axis, [(i, i ^ offset) for i in range(count)])]
  transfers between devices with their start and end apart: 30 -> 32, of which waited for: 18 -> 19; matrix products, arithmetic and copies ran while one was open for 6% -> 5% of each run, Pallas kernels for 15% -> 15%
where the time goes in v4:
time: 287 us; the launch traced here: 284 us
  waiting for transfers between devices  135 us (47%)
  Pallas kernels  57.6 us (20%)
  starting transfers between devices  37.3 us (13%)
  local copies, waits for them, and re-layouts  24 us (8%)
  other arithmetic  14.7 us (5%)
  between operations  14.6 us (5%)
    ppermute x30, waiting for transfers between devices, swap(): return lax.ppermute(x, axis, [(i, i ^ offset) for i in range(count)])  133 us
    ppermute x30, starting transfers between devices, swap(): return lax.ppermute(x, axis, [(i, i ^ offset) for i in range(count)])  33.2 us
    pallas_call x2, Pallas kernels, mix(): call(functools.partial(mix_kernel, len(rows), blocks), 'mix', (blocks,),...  20.6 us
    unnamed x78, local copies, waits for them, and re-layouts  20.3 us
    pallas_call x3, Pallas kernels, score(): call(functools.partial(score_kernel, members, len(pieces)), 'score', (ori...  18.4 us
    pallas_call x2, Pallas kernels, gather(): call(functools.partial(gather_kernel, chips, capacity, owned), 'gather',...  13.7 us
  transfers between devices with their start and end apart: 32, of which 19 were waited for; matrix products, arithmetic and copies ran while one was open for 5% of the time, Pallas kernels for 15%

profile of v4, /device:TPU:2, one launch (start us, length us, event | category | flops | bytes accessed | tf_op | source)
XLA Modules:
  0.0 283.7 jit_solution(5594908379316370545)
XLA Ops:
  9.2 2.8 copy-done.4
  12.0 4.7 %gather.22 = (bf16[96,4096]{1,0:T(8,128)(2,1)S(1)}, bf16[96,4096]{1,0:T(8,128)(2,1)}, bf16[96,4096]{1,0:T(8,128)(2,1)S(1)}, bf16[96,4096]{1,0:T(8,128)(2,1)}) custom-call(s32[1]{0:T(128)} %bitcast.me_ref, s32[1,384]{1,0:T(1,128)S(1)} %bitcast_add_fusion.slot_ref, bf16[384,8192]{1,0:T(8,128)(2,1)S(1)} %copy-done.4), custom_call_target="tpu_custom_call" | custom-call | flops 24159191040 | bytes 188743680 | tf_op jit(solution)/shard_map/gather/pallas_call | solution.py:82
  20.3 1.7 collective-permute-start.5
  22.0 16.0 %collective-permute-done.rest_2_ = bf16[96,4096]{1,0:T(8,128)(2,1)S(1)} collective-permute-done((bf16[96,4096]{1,0:T(8,128)(2,1)S(1)}, bf16[96,4096]{1,0:T(8,128)(2,1)S(1)}, u32[]{:S(2)}, u32[]{:S(2)}) %collective-permute-start) | collective-permute-done | bytes 786464 | tf_op jit(solution)/shard_map/ppermute | solution.py:31
  38.0 14.9 %collective-permute-done.1.rest_3_ = bf16[96,4096]{1,0:T(8,128)(2,1)S(1)} collective-permute-done((bf16[96,4096]{1,0:T(8,128)(2,1)S(1)}, bf16[96,4096]{1,0:T(8,128)(2,1)S(1)}, u32[]{:S(2)}, u32[]{:S(2)}) %collective-permute-start.1) | collective-permute-done | bytes 786464 | tf_op jit(solution)/shard_map/ppermute | solution.py:31
  52.9 9.1 %gather.23 = (bf16[96,4096]{1,0:T(8,128)(2,1)S(1)}, bf16[96,4096]{1,0:T(8,128)(2,1)S(1)}, bf16[96,4096]{1,0:T(8,128)(2,1)}, bf16[96,4096]{1,0:T(8,128)(2,1)}, bf...) custom-call(s32[1]{0:T(128)} %bitcast.me_ref, ...), custom_call_target="tpu_custom_call" | custom-call | flops 72477573120 | bytes 314572800 | tf_op jit(solution)/shard_map/gather/pallas_call | solution.py:82
  70.1 1.8 collective-permute-start.2
  74.3 12.5 %collective-permute-done.5.rest_7_.rest_11_ = bf16[96,4096]{1,0:T(8,128)(2,1)} collective-permute-done((bf16[96,4096]{1,0:T(8,128)(2,1)}, bf16[96,4096]{1,0:T(8,128)(2,1)}, u32[]{:S(2)}, u32[]{:S(2)}) %collective-permute-start.5) | collective-permute-done | bytes 786464 | tf_op jit(solution)/shard_map/ppermute | solution.py:31
  91.4 5.8 %copy-done.2 = bf16[2,512,8192]{2,1,0:T(8,128)(2,1)S(1)} copy-done((bf16[2,512,8192]{2,1,0:T(8,128)(2,1)S(1)}, bf16[2,512,8192]{2,1,0:T(8,128)(2,1)}, u32[]{:S(2)}) %copy-start.2) | copy-done | bytes 16777240
  99.5 7.5 %score.3.mine_ref = f32[2,384,512]{2,1,0:T(8,128)S(1)} custom-call(s32[1]{0:T(128)} %bitcast.me_ref, bf16[2,512,8192]{2,1,0:T(8,128)(2,1)S(1)} %copy-done.2, bf16[96,4096]{1,0:T(8,128)(2,1)S(1)} %copy-done.27, bf16[96,4096]{1,0:T(8,128)(2,1)} %collective-permute-done.2.rest_1_, bf16[96,4096]{1,0:T(8,128)(2,1)S(1)} %collective-permute-done.rest_2_, ...), custom_call_target="tpu_custom_call" | custom-call | flops 64424509440 | bytes 293601280 | tf_op jit(solution)/shard_map/score/pallas_call | solution.py:124
  107.1 15.4 %collective-permute-done.7.rest_0_.rest_4_ = bf16[96,4096]{1,0:T(8,128)(2,1)} collective-permute-done((bf16[96,4096]{1,0:T(8,128)(2,1)}, bf16[96,4096]{1,0:T(8,128)(2,1)}, u32[]{:S(2)}, u32[]{:S(2)}) %collective-permute-start.7) | collective-permute-done | bytes 786464 | tf_op jit(solution)/shard_map/ppermute | solution.py:31
  123.0 14.3 %collective-permute-done.8.rest_1_.rest_5_ = bf16[96,4096]{1,0:T(8,128)(2,1)} collective-permute-done((bf16[96,4096]{1,0:T(8,128)(2,1)}, bf16[96,4096]{1,0:T(8,128)(2,1)}, u32[]{:S(2)}, u32[]{:S(2)}) %collective-permute-start.8) | collective-permute-done | bytes 786464 | tf_op jit(solution)/shard_map/ppermute | solution.py:31
  137.4 2.1 collective-permute-start.14
  139.5 5.6 %score.4.rest_0_ = f32[1,384,512]{2,1,0:T(8,128)} custom-call(s32[1]{0:T(128)} %bitcast.me_ref, bf16[2,512,8192]{2,1,0:T(8,128)(2,1)S(1)} %copy-done.3, bf16[96,4096]{1,0:T(8,128)(2,1)} %collective-permute-done.7.rest_0_.rest_4_, bf16[96,4096]{1,0:T(8,128)(2,1)} %collective-permute-done.8.rest_1_.rest_5_, ...), custom_call_target="tpu_custom_call" | custom-call | flops 32212254720 | bytes 293601280 | tf_op jit(solution)/shard_map/score/pallas_call | solution.py:124
  146.2 7.5 %collective-permute-done.12.rest_1_.rest_13_ = bf16[96,4096]{1,0:T(8,128)(2,1)S(1)} collective-permute-done((bf16[96,4096]{1,0:T(8,128)(2,1)S(1)}, bf16[96,4096]{1,0:T(8,128)(2,1)S(1)}, u32[]{:S(2)}, u32[]{:S(2)}) %collective-permute-start.12) | collective-permute-done | bytes 786464 | tf_op jit(solution)/shard_map/ppermute | solution.py:31
  153.7 2.9 %collective-permute-done.14.rest_3_.rest_15_ = bf16[96,4096]{1,0:T(8,128)(2,1)S(1)} collective-permute-done((bf16[96,4096]{1,0:T(8,128)(2,1)S(1)}, bf16[96,4096]{1,0:T(8,128)(2,1)S(1)}, u32[]{:S(2)}, u32[]{:S(2)}) %collective-permute-start.14) | collective-permute-done | bytes 786464 | tf_op jit(solution)/shard_map/ppermute | solution.py:31
  156.6 5.3 %score.5.rest_1_ = f32[1,384,512]{2,1,0:T(8,128)} custom-call(s32[1]{0:T(128)} %bitcast.me_ref, bf16[2,512,8192]{2,1,0:T(8,128)(2,1)S(1)} %copy-done.3, bf16[96,4096]{1,0:T(8,128)(2,1)} %collective-permute-done.11.rest_0_.rest_12_, bf16[96,4096]{1,0:T(8,128)(2,1)S(1)} %collective-permute-done.12.rest_1_.rest_13_, ...), custom_call_target="tpu_custom_call" | custom-call | flops 32212254720 | bytes 293601280 | tf_op jit(solution)/shard_map/score/pallas_call | solution.py:124
  166.4 4.2 %matrix.1 = (f32[2,384,1]{2,1,0:T(8,128)S(1)}, bf16[1024,1536]{1,0:T(8,128)(2,1)S(1)}) custom-call(s32[1]{0:T(128)} %bitcast.me_ref, s32[1024,1]{1,0:T(8,128)S(1)} %copy.12.wanted_ref, s32[2,512]{1,0:T(2,128)S(1)} %broadcast_add_fusion.target_ref, bf16[2,384,512]{2,1,0:T(8,128)(2,1)S(1)} %copy-done.25, f32[1,384,512]{2,1,0:T(8,128)} %score.4.rest_0_, ...), custom_call_target="tpu_custom_call" | custom-call | flops 32212254720 | bytes 62914560 | tf_op jit(solution)/shard_map/matrix/pallas_call | solution.py:203
  170.7 10.3 %mix.2 = (bf16[2,256,1024]{2,1,0:T(8,128)(2,1)S(1)}, f32[2,256,1024]{2,1,0:T(8,128)S(1)}, bf16[2,256,1024]{2,1,0:T(8,128)(2,1)S(1)}, f32[2,256,1024]{2,1,0:T(8,128)S(1)}) custom-call(s32[1]{0:T(128)} %bitcast.me_ref, bf16[1024,1536]{1,0:T(8,128)(2,1)S(1)} %get-tuple-element.70.mix_ref, bf16[96,4096]{1,0:T(8,128)(2,1)S(1)} %copy-done.28, ...), custom_call_target="tpu_custom_call" | custom-call | flops 128849018880 | bytes 335544320 | tf_op jit(solution)/shard_map/mix/pallas_call | solution.py:258
  183.4 10.2 %mix.3 = (bf16[2,256,1024]{2,1,0:T(8,128)(2,1)S(1)}, f32[2,256,1024]{2,1,0:T(8,128)S(1)}, bf16[2,256,1024]{2,1,0:T(8,128)(2,1)S(1)}, f32[2,256,1024]{2,1,0:T(8,128)S(1)}) custom-call(s32[1]{0:T(128)} %bitcast.me_ref, bf16[1024,1536]{1,0:T(8,128)(2,1)S(1)} %get-tuple-element.70.mix_ref, bf16[96,4096]{1,0:T(8,128)(2,1)S(1)} %copy-done.28, ...), custom_call_target="tpu_custom_call" | custom-call | flops 128849018880 | bytes 335544320 | tf_op jit(solution)/shard_map/mix/pallas_call | solution.py:258
  193.7 12.8 %collective-permute-done.17 = bf16[2,256,1024]{2,1,0:T(8,128)(2,1)S(1)} collective-permute-done((bf16[2,256,1024]{2,1,0:T(8,128)(2,1)S(1)}, bf16[2,256,1024]{2,1,0:T(8,128)(2,1)S(1)}, u32[]{:S(2)}, u32[]{:S(2)}) %collective-permute-start.17) | collective-permute-done | bytes 1048608 | tf_op jit(solution)/shard_map/ppermute | solution.py:31
  212.6 10.2 %collective-permute-done.21 = bf16[1,256,1024]{2,1,0:T(8,128)(2,1)S(1)} collective-permute-done((bf16[1,256,1024]{2,1,0:T(8,128)(2,1)S(1)}, bf16[1,256,1024]{2,1,0:T(8,128)(2,1)S(1)}, u32[]{:S(2)}, u32[]{:S(2)}) %collective-permute-start.21) | collective-permute-done | bytes 524320 | tf_op jit(solution)/shard_map/ppermute | solution.py:31
  226.5 10.8 %collective-permute-done.23 = bf16[256,1024]{1,0:T(8,128)(2,1)S(1)} collective-permute-done((bf16[256,1024]{1,0:T(8,128)(2,1)S(1)}, bf16[256,1024]{1,0:T(8,128)(2,1)S(1)}, u32[]{:S(2)}, u32[]{:S(2)}) %collective-permute-start.23) | collective-permute-done | bytes 524320 | tf_op jit(solution)/shard_map/ppermute | solution.py:31
  237.5 1.7 collective-permute-start.28
  239.3 5.4 %collective-permute-done.19 = bf16[2,256,1024]{2,1,0:T(8,128)(2,1)S(1)} collective-permute-done((bf16[2,256,1024]{2,1,0:T(8,128)(2,1)S(1)}, bf16[2,256,1024]{2,1,0:T(8,128)(2,1)S(1)}, u32[]{:S(2)}, u32[]{:S(2)}) %collective-permute-start.19) | collective-permute-done | bytes 1048608 | tf_op jit(solution)/shard_map/ppermute | solution.py:31
  244.7 1.8 fusion.15
  246.6 1.8 fusion.14
  250.4 1.6 collective-permute-start.26
  253.0 4.4 %collective-permute-done.24 = bf16[1,128,1024]{2,1,0:T(8,128)(2,1)S(1)} collective-permute-done((bf16[1,128,1024]{2,1,0:T(8,128)(2,1)S(1)}, bf16[1,128,1024]{2,1,0:T(8,128)(2,1)S(1)}, u32[]{:S(2)}, u32[]{:S(2)}) %collective-permute-start.24) | collective-permute-done | bytes 262176 | tf_op jit(solution)/shard_map/ppermute | solution.py:31
  263.5 1.6 collective-permute-start.29
  266.4 4.0 %all-to-all-start = ((f32[8,1,96]{2,1,0:T(1,128)}), f32[8,1,96]{2,1,0:T(1,128)S(1)}, u32[]{:S(2)}, u32[]{:S(2)}) async-start(f32[8,1,96]{2,1,0:T(1,128)} %bitcast.15), calls=%async_computation | async-start | bytes 8192 | tf_op jit(solution)/shard_map/all_to_all | solution.py:419
  271.6 2.0 all-to-all-done
  (181 shorter events, 56.1 us)
Async XLA Ops:
  7.2 84.3 %all-gather.2.cloned.1.call-start = ((), (), s32[]{:S(2)}) async-start(), calls=%async_computation.1 | async-start | bytes 25165824 | tf_op jit(solution)/shard_map/all_gather | solution.py:318
  16.7 21.4 %collective-permute-start = (bf16[96,4096]{1,0:T(8,128)(2,1)S(1)}, bf16[96,4096]{1,0:T(8,128)(2,1)S(1)}, u32[]{:S(2)}, u32[]{:S(2)}) collective-permute-start(bf16[96,4096]{1,0:T(8,128)(2,1)S(1)} %get-tuple-element.49), channel_id=1, source_target_pairs={{0,24},{4,28},{8,16},{12,20},{16,8},{20,12},{24,0},{28,4},{1,25},{... | collective-permute-start | bytes 2359304 | tf_op jit(solution)/shard_map/ppermute | solution.py:31
  18.1 34.8 %collective-permute-start.1 = (bf16[96,4096]{1,0:T(8,128)(2,1)S(1)}, bf16[96,4096]{1,0:T(8,128)(2,1)S(1)}, u32[]{:S(2)}, u32[]{:S(2)}) collective-permute-start(bf16[96,4096]{1,0:T(8,128)(2,1)S(1)} %get-tuple-element.50), channel_id=1, source_target_pairs={{0,28},{4,24},{8,20},{12,16},{16,12},{20,8},{24,4},{28,0},{1,29},{... | collective-permute-start | bytes 2359304 | tf_op jit(solution)/shard_map/ppermute | solution.py:31
  18.7 54.0 %collective-permute-start.4 = (bf16[96,4096]{1,0:T(8,128)(2,1)}, bf16[96,4096]{1,0:T(8,128)(2,1)S(1)}, u32[]{:S(2)}, u32[]{:S(2)}) collective-permute-start(bf16[96,4096]{1,0:T(8,128)(2,1)} %get-tuple-element.56), channel_id=1, source_target_pairs={{0,24},{4,28},{8,16},{12,20},{16,8},{20,12},{24,0},{28,4},{1,25},{... | collective-permute-start | bytes 2359304 | tf_op jit(solution)/shard_map/ppermute | solution.py:31
  20.3 66.5 %collective-permute-start.5 = (bf16[96,4096]{1,0:T(8,128)(2,1)}, bf16[96,4096]{1,0:T(8,128)(2,1)}, u32[]{:S(2)}, u32[]{:S(2)}) collective-permute-start(bf16[96,4096]{1,0:T(8,128)(2,1)} %get-tuple-element.57), channel_id=1, source_target_pairs={{0,28},{4,24},{8,20},{12,16},{16,12},{20,8},{24,4},{28,0},{1,29},{... | collective-permute-start | bytes 2359304 | tf_op jit(solution)/shard_map/ppermute | solution.py:31
  70.1 18.3 %collective-permute-start.2 = (bf16[96,4096]{1,0:T(8,128)(2,1)}, bf16[96,4096]{1,0:T(8,128)(2,1)}, u32[]{:S(2)}, u32[]{:S(2)}) collective-permute-start(bf16[96,4096]{1,0:T(8,128)(2,1)} %get-tuple-element.53), channel_id=1, source_target_pairs={{0,4},{4,0},{8,12},{12,8},{16,20},{20,16},{24,28},{28,24},{1,5},{5... | collective-permute-start | bytes 2359304 | tf_op jit(solution)/shard_map/ppermute | solution.py:31
  71.8 18.1 %collective-permute-start.3 = (bf16[96,4096]{1,0:T(8,128)(2,1)}, bf16[96,4096]{1,0:T(8,128)(2,1)}, u32[]{:S(2)}, u32[]{:S(2)}) collective-permute-start(bf16[96,4096]{1,0:T(8,128)(2,1)} %get-tuple-element.55), channel_id=1, source_target_pairs={{0,4},{4,0},{8,12},{12,8},{16,20},{20,16},{24,28},{28,24},{1,5},{5... | collective-permute-start | bytes 2359304 | tf_op jit(solution)/shard_map/ppermute | solution.py:31
  72.4 73.8 %collective-permute-start.11 = (bf16[96,4096]{1,0:T(8,128)(2,1)S(1)}, bf16[96,4096]{1,0:T(8,128)(2,1)}, u32[]{:S(2)}, u32[]{:S(2)}) collective-permute-start(bf16[96,4096]{1,0:T(8,128)(2,1)S(1)} %get-tuple-element.64), channel_id=1, source_target_pairs={{0,8},{4,12},{8,0},{12,4},{16,24},{20,28},{24,16},{28,20},{1,9},{5... | collective-permute-start | bytes 2359304 | tf_op jit(solution)/shard_map/ppermute | solution.py:31
  72.7 34.3 %collective-permute-start.10 = (bf16[96,4096]{1,0:T(8,128)(2,1)}, bf16[96,4096]{1,0:T(8,128)(2,1)}, u32[]{:S(2)}, u32[]{:S(2)}) collective-permute-start(bf16[96,4096]{1,0:T(8,128)(2,1)} %copy-done.23), channel_id=1, source_target_pairs={{0,20},{4,16},{8,28},{12,24},{16,4},{20,0},{24,12},{28,8},{1,21},{... | collective-permute-start | bytes 2359304 | tf_op jit(solution)/shard_map/ppermute | solution.py:31
  86.8 35.7 %collective-permute-start.7 = (bf16[96,4096]{1,0:T(8,128)(2,1)}, bf16[96,4096]{1,0:T(8,128)(2,1)}, u32[]{:S(2)}, u32[]{:S(2)}) collective-permute-start(bf16[96,4096]{1,0:T(8,128)(2,1)} %copy-done.22), channel_id=1, source_target_pairs={{0,8},{4,12},{8,0},{12,4},{16,24},{20,28},{24,16},{28,20},{1,9},{5... | collective-permute-start | bytes 2359304 | tf_op jit(solution)/shard_map/ppermute | solution.py:31
  88.3 49.0 %collective-permute-start.8 = (bf16[96,4096]{1,0:T(8,128)(2,1)}, bf16[96,4096]{1,0:T(8,128)(2,1)}, u32[]{:S(2)}, u32[]{:S(2)}) collective-permute-start(bf16[96,4096]{1,0:T(8,128)(2,1)} %copy-done.21), channel_id=1, source_target_pairs={{0,12},{4,8},{8,4},{12,0},{16,28},{20,24},{24,20},{28,16},{1,13},{... | collective-permute-start | bytes 2359304 | tf_op jit(solution)/shard_map/ppermute | solution.py:31
  89.9 49.6 %collective-permute-start.9 = (bf16[96,4096]{1,0:T(8,128)(2,1)}, bf16[96,4096]{1,0:T(8,128)(2,1)}, u32[]{:S(2)}, u32[]{:S(2)}) collective-permute-start(bf16[96,4096]{1,0:T(8,128)(2,1)} %copy-done.20), channel_id=1, source_target_pairs={{0,16},{4,20},{8,24},{12,28},{16,0},{20,4},{24,8},{28,12},{1,17},{... | collective-permute-start | bytes 2359304 | tf_op jit(solution)/shard_map/ppermute | solution.py:31
  107.1 46.6 %collective-permute-start.12 = (bf16[96,4096]{1,0:T(8,128)(2,1)S(1)}, bf16[96,4096]{1,0:T(8,128)(2,1)S(1)}, u32[]{:S(2)}, u32[]{:S(2)}) collective-permute-start(bf16[96,4096]{1,0:T(8,128)(2,1)S(1)} %copy-done.17), channel_id=1, source_target_pairs={{0,12},{4,8},{8,4},{12,0},{16,28},{20,24},{24,20},{28,16},{1,13},{... | collective-permute-start | bytes 2359304 | tf_op jit(solution)/shard_map/ppermute | solution.py:31
  122.5 31.2 %collective-permute-start.13 = (bf16[96,4096]{1,0:T(8,128)(2,1)S(1)}, bf16[96,4096]{1,0:T(8,128)(2,1)S(1)}, u32[]{:S(2)}, u32[]{:S(2)}) collective-permute-start(bf16[96,4096]{1,0:T(8,128)(2,1)S(1)} %copy-done.13), channel_id=1, source_target_pairs={{0,16},{4,20},{8,24},{12,28},{16,0},{20,4},{24,8},{28,12},{1,17},{... | collective-permute-start | bytes 2359304 | tf_op jit(solution)/shard_map/ppermute | solution.py:31
  137.4 19.3 %collective-permute-start.14 = (bf16[96,4096]{1,0:T(8,128)(2,1)S(1)}, bf16[96,4096]{1,0:T(8,128)(2,1)S(1)}, u32[]{:S(2)}, u32[]{:S(2)}) collective-permute-start(bf16[96,4096]{1,0:T(8,128)(2,1)S(1)} %copy-done.11), channel_id=1, source_target_pairs={{0,20},{4,16},{8,28},{12,24},{16,4},{20,0},{24,12},{28,8},{1,21},{... | collective-permute-start | bytes 2359304 | tf_op jit(solution)/shard_map/ppermute | solution.py:31
  139.5 5.6 %collective-permute-start.6 = (f32[2,384,512]{2,1,0:T(8,128)S(1)}, f32[2,384,512]{2,1,0:T(8,128)S(1)}, u32[]{:S(2)}, u32[]{:S(2)}) collective-permute-start(f32[2,384,512]{2,1,0:T(8,128)S(1)} %score.3.mine_ref), channel_id=1, source_target_pairs={{0,4},{4,0},{8,12},{12,8},{16,20},{20,16},{24,28},{28,24},{1,5},{5... | collective-permute-start | bytes 4718600 | tf_op jit(solution)/shard_map/ppermute | solution.py:31
  145.1 19.5 %collective-permute-start.15 = (f32[1,384,512]{2,1,0:T(8,128)}, f32[1,384,512]{2,1,0:T(8,128)}, u32[]{:S(2)}, u32[]{:S(2)}) collective-permute-start(f32[1,384,512]{2,1,0:T(8,128)} %score.4.rest_0_), channel_id=1, source_target_pairs={{0,4},{4,0},{8,12},{12,8},{16,20},{20,16},{24,28},{28,24},{1,5},{5... | collective-permute-start | bytes 2359304 | tf_op jit(solution)/shard_map/ppermute | solution.py:31
  161.9 3.1 %collective-permute-start.16 = (f32[1,384,512]{2,1,0:T(8,128)}, f32[1,384,512]{2,1,0:T(8,128)}, u32[]{:S(2)}, u32[]{:S(2)}) collective-permute-start(f32[1,384,512]{2,1,0:T(8,128)} %score.5.rest_1_), channel_id=1, source_target_pairs={{0,4},{4,0},{8,12},{12,8},{16,20},{20,16},{24,28},{28,24},{1,5},{5... | collective-permute-start | bytes 2359304 | tf_op jit(solution)/shard_map/ppermute | solution.py:31
  181.1 25.4 %collective-permute-start.17 = (bf16[2,256,1024]{2,1,0:T(8,128)(2,1)S(1)}, bf16[2,256,1024]{2,1,0:T(8,128)(2,1)S(1)}, u32[]{:S(2)}, u32[]{:S(2)}) collective-permute-start(bf16[2,256,1024]{2,1,0:T(8,128)(2,1)S(1)} %get-tuple-element.75), channel_id=1, source_target_pairs={{0,8},{4,12},{8,0},{12,4},{16,24},{20,28},{24,16},{28,20},{1,9},{5... | collective-permute-start | bytes 3145736 | tf_op jit(solution)/shard_map/ppermute | solution.py:31
  182.3 25.1 %collective-permute-start.18 = (bf16[2,256,1024]{2,1,0:T(8,128)(2,1)S(1)}, bf16[2,256,1024]{2,1,0:T(8,128)(2,1)S(1)}, u32[]{:S(2)}, u32[]{:S(2)}) collective-permute-start(bf16[2,256,1024]{2,1,0:T(8,128)(2,1)S(1)} %get-tuple-element.76), channel_id=1, source_target_pairs={{0,16},{4,20},{8,24},{12,28},{16,0},{20,4},{24,8},{28,12},{1,17},{... | collective-permute-start | bytes 3145736 | tf_op jit(solution)/shard_map/ppermute | solution.py:31
  207.9 14.9 %collective-permute-start.21 = (bf16[1,256,1024]{2,1,0:T(8,128)(2,1)S(1)}, bf16[1,256,1024]{2,1,0:T(8,128)(2,1)S(1)}, u32[]{:S(2)}, u32[]{:S(2)}) collective-permute-start(bf16[1,256,1024]{2,1,0:T(8,128)(2,1)S(1)} %slice.179), channel_id=1, source_target_pairs={{0,16},{4,20},{8,24},{12,28},{16,0},{20,4},{24,8},{28,12},{1,17},{... | collective-permute-start | bytes 1572872 | tf_op jit(solution)/shard_map/ppermute | solution.py:31
  209.5 14.9 %collective-permute-start.22 = (bf16[1,256,1024]{2,1,0:T(8,128)(2,1)S(1)}, bf16[1,256,1024]{2,1,0:T(8,128)(2,1)S(1)}, u32[]{:S(2)}, u32[]{:S(2)}) collective-permute-start(bf16[1,256,1024]{2,1,0:T(8,128)(2,1)S(1)} %slice.178), channel_id=1, source_target_pairs={{0,8},{4,12},{8,0},{12,4},{16,24},{20,28},{24,16},{28,20},{1,9},{5... | collective-permute-start | bytes 1572872 | tf_op jit(solution)/shard_map/ppermute | solution.py:31
  210.9 33.8 %collective-permute-start.19 = (bf16[2,256,1024]{2,1,0:T(8,128)(2,1)S(1)}, bf16[2,256,1024]{2,1,0:T(8,128)(2,1)S(1)}, u32[]{:S(2)}, u32[]{:S(2)}) collective-permute-start(bf16[2,256,1024]{2,1,0:T(8,128)(2,1)S(1)} %get-tuple-element.78), channel_id=1, source_target_pairs={{0,8},{4,12},{8,0},{12,4},{16,24},{20,28},{24,16},{28,20},{1,9},{5... | collective-permute-start | bytes 3145736 | tf_op jit(solution)/shard_map/ppermute | solution.py:31
  211.5 33.2 %collective-permute-start.20 = (bf16[2,256,1024]{2,1,0:T(8,128)(2,1)S(1)}, bf16[2,256,1024]{2,1,0:T(8,128)(2,1)S(1)}, u32[]{:S(2)}, u32[]{:S(2)}) collective-permute-start(bf16[2,256,1024]{2,1,0:T(8,128)(2,1)S(1)} %get-tuple-element.79), channel_id=1, source_target_pairs={{0,16},{4,20},{8,24},{12,28},{16,0},{20,4},{24,8},{28,12},{1,17},{... | collective-permute-start | bytes 3145736 | tf_op jit(solution)/shard_map/ppermute | solution.py:31
  224.9 12.4 %collective-permute-start.23 = (bf16[256,1024]{1,0:T(8,128)(2,1)S(1)}, bf16[256,1024]{1,0:T(8,128)(2,1)S(1)}, u32[]{:S(2)}, u32[]{:S(2)}) collective-permute-start(bf16[256,1024]{1,0:T(8,128)(2,1)S(1)} %pad_maximum_fusion.1), channel_id=1, source_target_pairs={{0,1},{1,0},{2,3},{3,2},{4,5},{5,4},{6,7},{7,6},{8,9},{9,8},{10,11... | collective-permute-start | bytes 1572872 | tf_op jit(solution)/shard_map/ppermute | solution.py:31
  237.5 23.6 %collective-permute-start.28 = (bf16[256,1024]{1,0:T(8,128)(2,1)S(1)}, bf16[256,1024]{1,0:T(8,128)(2,1)S(1)}, u32[]{:S(2)}, u32[]{:S(2)}) collective-permute-start(bf16[256,1024]{1,0:T(8,128)(2,1)S(1)} %fusion), channel_id=1, source_target_pairs={{0,2},{1,3},{2,0},{3,1},{4,6},{5,7},{6,4},{7,5},{8,10},{9,11},{10,... | collective-permute-start | bytes 1572872 | tf_op jit(solution)/shard_map/ppermute | solution.py:31
  248.4 9.0 %collective-permute-start.24 = (bf16[1,128,1024]{2,1,0:T(8,128)(2,1)S(1)}, bf16[1,128,1024]{2,1,0:T(8,128)(2,1)S(1)}, u32[]{:S(2)}, u32[]{:S(2)}) collective-permute-start(bf16[1,128,1024]{2,1,0:T(8,128)(2,1)S(1)} %get-tuple-element.102), channel_id=1, source_target_pairs={{0,16},{4,20},{8,24},{12,28},{16,0},{20,4},{24,8},{28,12},{1,17},{... | collective-permute-start | bytes 786440 | tf_op jit(solution)/shard_map/ppermute | solution.py:31
  249.5 8.7 %collective-permute-start.25 = (bf16[1,128,1024]{2,1,0:T(8,128)(2,1)S(1)}, bf16[1,128,1024]{2,1,0:T(8,128)(2,1)S(1)}, u32[]{:S(2)}, u32[]{:S(2)}) collective-permute-start(bf16[1,128,1024]{2,1,0:T(8,128)(2,1)S(1)} %get-tuple-element.100), channel_id=1, source_target_pairs={{0,8},{4,12},{8,0},{12,4},{16,24},{20,28},{24,16},{28,20},{1,9},{5... | collective-permute-start | bytes 786440 | tf_op jit(solution)/shard_map/ppermute | solution.py:31
  250.4 10.0 %collective-permute-start.26 = (bf16[1,128,1024]{2,1,0:T(8,128)(2,1)S(1)}, bf16[1,128,1024]{2,1,0:T(8,128)(2,1)}, u32[]{:S(2)}, u32[]{:S(2)}) collective-permute-start(bf16[1,128,1024]{2,1,0:T(8,128)(2,1)S(1)} %get-tuple-element.101), channel_id=1, source_target_pairs={{0,16},{4,20},{8,24},{12,28},{16,0},{20,4},{24,8},{28,12},{1,17},{... | collective-permute-start | bytes 786440 | tf_op jit(solution)/shard_map/ppermute | solution.py:31
  252.0 9.2 %collective-permute-start.27 = (bf16[1,128,1024]{2,1,0:T(8,128)(2,1)S(1)}, bf16[1,128,1024]{2,1,0:T(8,128)(2,1)}, u32[]{:S(2)}, u32[]{:S(2)}) collective-permute-start(bf16[1,128,1024]{2,1,0:T(8,128)(2,1)S(1)} %get-tuple-element.99), channel_id=1, source_target_pairs={{0,8},{4,12},{8,0},{12,4},{16,24},{20,28},{24,16},{28,20},{1,9},{5... | collective-permute-start | bytes 786440 | tf_op jit(solution)/shard_map/ppermute | solution.py:31
  263.5 12.1 %collective-permute-start.29 = (bf16[256,1024]{1,0:T(8,128)(2,1)S(1)}, bf16[256,1024]{1,0:T(8,128)(2,1)S(1)}, u32[]{:S(2)}, u32[]{:S(2)}) collective-permute-start(bf16[256,1024]{1,0:T(8,128)(2,1)S(1)} %fusion.13), channel_id=1, source_target_pairs={{0,1},{1,0},{2,3},{3,2},{4,5},{5,4},{6,7},{7,6},{8,9},{9,8},{10,11... | collective-permute-start | bytes 1572872 | tf_op jit(solution)/shard_map/ppermute | solution.py:31
  266.4 7.2 %all-to-all-start = ((f32[8,1,96]{2,1,0:T(1,128)}), f32[8,1,96]{2,1,0:T(1,128)S(1)}, u32[]{:S(2)}, u32[]{:S(2)}) async-start(f32[8,1,96]{2,1,0:T(1,128)} %bitcast.15), calls=%async_computation | async-start | bytes 8192 | tf_op jit(solution)/shard_map/all_to_all | solution.py:419
  (39 other events, 491.1 us)
Sparse Core Ops, SparseCore 0:
  9.6 31.5 all-gather.1

commit v5 on v4

--- a/solution.py
+++ b/solution.py
@@ -97,12 +97,34 @@
     return {r: [outs[2 * n], outs[2 * n + 1]] for n, r in enumerate(offsets)}
 
 
-def score_kernel(members, count, me_ref, panels_ref, *rest):
+def copy_kernel(me_ref, panel_ref, out_ref):
+    out_ref[...] = panel_ref[...]
+
+
+def partner_columns(me, panel, orient_count):
+    rows, window = panel.shape
+    owned = window // orient_count
+    return call(
+        copy_kernel,
+        "partner_columns",
+        (orient_count // 2,),
+        [pl.BlockSpec((rows, owned), lambda j, me: (0, 2 * j + 1 - (me[0] & 1)))],
+        pl.BlockSpec((rows, owned), lambda j, me: (0, j)),
+        jax.ShapeDtypeStruct((rows, window // 2), BF16),
+        [],
+        0,
+        2 * rows * window,
+    )(me, panel)
+
+
+def score_kernel(members, count, me_ref, mine_ref, other_ref, *rest):
     rows, out_ref = rest[:-1], rest[-1]
+    low = me_ref[0] & 1
     for n, member in enumerate(members):
         block = jnp.concatenate([ref[...] for ref in rows[n * count : (n + 1) * count]], axis=0)
+        panel = jnp.where(low == member, mine_ref[...], other_ref[...])
         term = lax.dot_general(
-            block, panels_ref[n], (((1,), (1,)), ((), ())), preferred_element_type=F32
+            block, panel, (((1,), (1,)), ((), ())), preferred_element_type=F32
         )
 
         @pl.when(pl.program_id(0) == 0)
@@ -114,21 +136,19 @@
             out_ref[n] += term
 
 
-def score(members, me, panels, pieces, orient_count):
+def score(members, me, panel, other, pieces, orient_count):
     rows = [piece[member] for member in members for piece in pieces]
-    _, orient_total, window = panels.shape
+    orient_total, window = panel.shape
     owned = window // orient_count
     capacity = rows[0].shape[0]
-    lead = members[0]
     shape = (len(members), len(pieces) * capacity, orient_total)
     return call(
         functools.partial(score_kernel, members, len(pieces)),
         "score",
         (orient_count // 2,),
         [
-            pl.BlockSpec(
-                (len(members), orient_total, owned), lambda j, me: (lead, 0, 2 * j + (me[0] & 1))
-            )
+            pl.BlockSpec((orient_total, owned), lambda j, me: (0, 2 * j + (me[0] & 1))),
+            pl.BlockSpec((orient_total, owned), lambda j, me: (0, j)),
         ]
         + [pl.BlockSpec((capacity, owned), lambda j, me: (0, j))] * len(rows),
         pl.BlockSpec(shape, lambda j, me: (0, 0, 0)),
@@ -136,7 +156,7 @@
         [],
         shape[0] * shape[1] * orient_total * window,
         2 * window * (orient_total + shape[1]),
-    )(me, panels, *rows)
+    )(me, panel, other, *rows)
 
 
 def softmax(mine, got, capacity, scale):
@@ -308,26 +328,25 @@
     arrived = {}
     for offset in early[2:4]:
         arrived[offset] = [swap(half, "orient", offset) for half in outgoing[offset]]
-    images = after(images, (arrived[early[2]][0], arrived[early[3]][0]))
+    images, panel_ready = after((images, panel), (arrived[early[2]][0], arrived[early[3]][0]))
+    sent_panel = partner_columns(me_ref, panel_ready, orient_count)
     outgoing |= gather([0] + chips[1:], me_ref, slot_row, images, orient_count, capacity)
     arrived[0] = outgoing[0]
     for offset in early[4:] + early[1:2] + [2 * q + swapped for swapped in range(2) for q in near]:
         arrived[offset] = [swap(half, "orient", offset) for half in outgoing[offset]]
     pieces = [arrived[r] for r in order]
 
-    both = lax.all_gather(
-        panel, "orient", axis_index_groups=[[2 * q, 2 * q + 1] for q in range(orient_count // 2)]
-    )
+    other = swap(sent_panel, "orient", 1)
     early_pieces, late_pieces = pieces[: len(early)], pieces[len(early) :]
-    early_scores = score((0, 1), me_ref, both, early_pieces, orient_count)
+    early_scores = score((0, 1), me_ref, panel, other, early_pieces, orient_count)
     early_weights, early_logs = weigh(
         me_ref, early_scores, swap(early_scores, "orient", 1), capacity, score_scale
     )
     late_scores, got_late = [], []
     for member in range(2):
         if member == 1:
-            both = after(both, early_weights)
-        found = score((member,), me_ref, both, late_pieces, orient_count)
+            other = after(other, early_weights)
+        found = score((member,), me_ref, panel, other, late_pieces, orient_count)
         late_scores.append(found)
         got_late.append(swap(found, "orient", 1))
 

time: 287 us -> 278 us (0.969)
  between operations: 14.6 us -> 1.27 us
  Pallas kernels: 57.6 us -> 61.3 us
    ppermute x30 -> x31, waiting for transfers between devices: 133 us -> 135 us  [swap(): return lax.ppermute(x, axis, [(i, i ^ offset) for i in range(count)])]
    unnamed x78 -> x98, local copies, waits for them, and re-layouts: 20.3 us -> 18.4 us
    ppermute x30 -> x31, starting transfers between devices: 33.2 us -> 32.2 us  [swap(): return lax.ppermute(x, axis, [(i, i ^ offset) for i in range(count)])]
  transfers between devices with their start and end apart: 32 -> 32, of which waited for: 19 -> 20; matrix products, arithmetic and copies ran while one was open for 5% -> 5% of each run, Pallas kernels for 15% -> 15%
where the time goes in v5:
time: 278 us; the launch traced here: 275 us
  waiting for transfers between devices  137 us (49%)
  Pallas kernels  61.3 us (22%)
  starting transfers between devices  36.7 us (13%)
  local copies, waits for them, and re-layouts  23.7 us (9%)
  other arithmetic  15.3 us (6%)
    ppermute x31, waiting for transfers between devices, swap(): return lax.ppermute(x, axis, [(i, i ^ offset) for i in range(count)])  135 us
    ppermute x31, starting transfers between devices, swap(): return lax.ppermute(x, axis, [(i, i ^ offset) for i in range(count)])  32.2 us
    pallas_call x2, Pallas kernels, mix(): call(functools.partial(mix_kernel, len(rows), blocks), 'mix', (blocks,),...  20.2 us
    pallas_call x3, Pallas kernels, score(): call(functools.partial(score_kernel, members, len(pieces)), 'score', (ori...  19.8 us
    unnamed x98, local copies, waits for them, and re-layouts  18.4 us
    pallas_call x2, Pallas kernels, gather(): call(functools.partial(gather_kernel, chips, capacity, owned), 'gather',...  13.6 us
  transfers between devices with their start and end apart: 32, of which 20 were waited for; matrix products, arithmetic and copies ran while one was open for 5% of the time, Pallas kernels for 15%

profile of v5, /device:TPU:2, one launch (start us, length us, event | category | flops | bytes accessed | tf_op | source)
XLA Modules:
  0.0 275.2 jit_solution(407328917968941478)
XLA Ops:
  3.3 2.9 %copy-done.4 = bf16[384,8192]{1,0:T(8,128)(2,1)S(1)} copy-done((bf16[384,8192]{1,0:T(8,128)(2,1)S(1)}, bf16[384,8192]{1,0:T(8,128)(2,1)}, u32[]{:S(2)}) %copy-start.4) | copy-done | bytes 6291480
  6.2 4.6 %gather.22 = (bf16[96,4096]{1,0:T(8,128)(2,1)S(1)}, bf16[96,4096]{1,0:T(8,128)(2,1)}, bf16[96,4096]{1,0:T(8,128)(2,1)S(1)}, bf16[96,4096]{1,0:T(8,128)(2,1)}) custom-call(s32[1]{0:T(128)} %bitcast.me_ref, s32[1,384]{1,0:T(1,128)S(1)} %bitcast_add_fusion.slot_ref, bf16[384,8192]{1,0:T(8,128)(2,1)S(1)} %copy-done.4), custom_call_target="tpu_custom_call" | custom-call | flops 24159191040 | bytes 188743680 | tf_op jit(solution)/shard_map/gather/pallas_call | solution.py:82
  14.4 1.7 collective-permute-start.6
  16.2 16.0 %collective-permute-done.rest_2_ = bf16[96,4096]{1,0:T(8,128)(2,1)S(1)} collective-permute-done((bf16[96,4096]{1,0:T(8,128)(2,1)S(1)}, bf16[96,4096]{1,0:T(8,128)(2,1)S(1)}, u32[]{:S(2)}, u32[]{:S(2)}) %collective-permute-start) | collective-permute-done | bytes 786464 | tf_op jit(solution)/shard_map/ppermute | solution.py:31
  32.2 15.0 %collective-permute-done.1.rest_3_ = bf16[96,4096]{1,0:T(8,128)(2,1)S(1)} collective-permute-done((bf16[96,4096]{1,0:T(8,128)(2,1)S(1)}, bf16[96,4096]{1,0:T(8,128)(2,1)S(1)}, u32[]{:S(2)}, u32[]{:S(2)}) %collective-permute-start.1) | collective-permute-done | bytes 786464 | tf_op jit(solution)/shard_map/ppermute | solution.py:31
  47.2 2.8 %partner_columns.1 = bf16[512,4096]{1,0:T(8,128)(2,1)} custom-call(s32[1]{0:T(128)} %bitcast.me_ref, bf16[512,8192]{1,0:T(8,128)(2,1)S(1)} %bitcast.36), custom_call_target="tpu_custom_call" | custom-call | bytes 167772160 | tf_op jit(solution)/shard_map/partner_columns/pallas_call | solution.py:107
  50.0 1.7 collective-permute-start.2
  51.7 9.0 %gather.23 = (bf16[96,4096]{1,0:T(8,128)(2,1)S(1)}, bf16[96,4096]{1,0:T(8,128)(2,1)S(1)}, bf16[96,4096]{1,0:T(8,128)(2,1)}, bf16[96,4096]{1,0:T(8,128)(2,1)}, bf...) custom-call(s32[1]{0:T(128)} %bitcast.me_ref, ...), custom_call_target="tpu_custom_call" | custom-call | flops 72477573120 | bytes 314572800 | tf_op jit(solution)/shard_map/gather/pallas_call | solution.py:82
  69.5 11.5 %collective-permute-done.6.rest_7_.rest_11_ = bf16[96,4096]{1,0:T(8,128)(2,1)} collective-permute-done((bf16[96,4096]{1,0:T(8,128)(2,1)}, bf16[96,4096]{1,0:T(8,128)(2,1)}, u32[]{:S(2)}, u32[]{:S(2)}) %collective-permute-start.6) | collective-permute-done | bytes 786464 | tf_op jit(solution)/shard_map/ppermute | solution.py:31
  82.3 2.1 collective-permute-start.10
  85.9 3.4 %copy-done.2 = bf16[1,512,8192]{2,1,0:T(8,128)(2,1)S(1)} copy-done((bf16[1,512,8192]{2,1,0:T(8,128)(2,1)S(1)}, bf16[1,512,8192]{2,1,0:T(8,128)(2,1)}, u32[]{:S(2)}) %copy-start.2) | copy-done | bytes 8388632
  91.5 7.5 %score.3.mine_ref = f32[2,384,512]{2,1,0:T(8,128)S(1)} custom-call(s32[1]{0:T(128)} %bitcast.me_ref, bf16[512,8192]{1,0:T(8,128)(2,1)S(1)} %bitcast.37, bf16[512,4096]{1,0:T(8,128)(2,1)} %collective-permute-done.2.other_ref, bf16[96,4096]{1,0:T(8,128)(2,1)S(1)} %copy-done.36, bf16[96,4096]{1,0:T(8,128)(2,1)} %collective-permute-done.3.rest_1_, ...), custom_call_target="tpu_custom_call" | custom-call | flops 64424509440 | bytes 293601280 | tf_op jit(solution)/shard_map/score/pallas_call | solution.py:145
  99.7 15.0 %collective-permute-done.9.rest_1_.rest_5_ = bf16[96,4096]{1,0:T(8,128)(2,1)S(1)} collective-permute-done((bf16[96,4096]{1,0:T(8,128)(2,1)}, bf16[96,4096]{1,0:T(8,128)(2,1)S(1)}, u32[]{:S(2)}, u32[]{:S(2)}) %collective-permute-start.9) | collective-permute-done | bytes 786464 | tf_op jit(solution)/shard_map/ppermute | solution.py:31
  114.7 3.3 %collective-permute-start.15 = (bf16[96,4096]{1,0:T(8,128)(2,1)S(1)}, bf16[96,4096]{1,0:T(8,128)(2,1)S(1)}, u32[]{:S(2)}, u32[]{:S(2)}) collective-permute-start(bf16[96,4096]{1,0:T(8,128)(2,1)S(1)} %copy-done.24), channel_id=1, source_target_pairs={{0,20},{4,16},{8,28},{12,24},{16,4},{20,0},{24,12},{28,8},{1,21},{... | collective-permute-start | bytes 2359304 | tf_op jit(solution)/shard_map/ppermute | solution.py:31
  119.4 6.3 %score.4.rest_0_ = f32[1,384,512]{2,1,0:T(8,128)} custom-call(s32[1]{0:T(128)} %bitcast.me_ref, bf16[512,8192]{1,0:T(8,128)(2,1)S(1)} %bitcast.38, bf16[512,4096]{1,0:T(8,128)(2,1)} %collective-permute-done.2.other_ref, bf16[96,4096]{1,0:T(8,128)(2,1)S(1)} %collective-permute-done.8.rest_0_.rest_4_, ...), custom_call_target="tpu_custom_call" | custom-call | flops 32212254720 | bytes 293601280 | tf_op jit(solution)/shard_map/score/pallas_call | solution.py:145
  126.6 6.7 %collective-permute-done.12.rest_0_.rest_12_ = bf16[96,4096]{1,0:T(8,128)(2,1)S(1)} collective-permute-done((bf16[96,4096]{1,0:T(8,128)(2,1)S(1)}, bf16[96,4096]{1,0:T(8,128)(2,1)S(1)}, u32[]{:S(2)}, u32[]{:S(2)}) %collective-permute-start.12) | collective-permute-done | bytes 786464 | tf_op jit(solution)/shard_map/ppermute | solution.py:31
  133.4 14.6 %collective-permute-done.13.rest_1_.rest_13_ = bf16[96,4096]{1,0:T(8,128)(2,1)S(1)} collective-permute-done((bf16[96,4096]{1,0:T(8,128)(2,1)S(1)}, bf16[96,4096]{1,0:T(8,128)(2,1)S(1)}, u32[]{:S(2)}, u32[]{:S(2)}) %collective-permute-start.13) | collective-permute-done | bytes 786464 | tf_op jit(solution)/shard_map/ppermute | solution.py:31
  148.0 4.9 %collective-permute-done.15.rest_3_.rest_15_ = bf16[96,4096]{1,0:T(8,128)(2,1)S(1)} collective-permute-done((bf16[96,4096]{1,0:T(8,128)(2,1)S(1)}, bf16[96,4096]{1,0:T(8,128)(2,1)S(1)}, u32[]{:S(2)}, u32[]{:S(2)}) %collective-permute-start.15) | collective-permute-done | bytes 786464 | tf_op jit(solution)/shard_map/ppermute | solution.py:31
  152.9 6.0 %score.5.rest_1_ = f32[1,384,512]{2,1,0:T(8,128)} custom-call(s32[1]{0:T(128)} %bitcast.me_ref, bf16[512,8192]{1,0:T(8,128)(2,1)S(1)} %bitcast.39, bf16[512,4096]{1,0:T(8,128)(2,1)} %collective-permute-done.2.other_ref, bf16[96,4096]{1,0:T(8,128)(2,1)S(1)} %collective-permute-done.12.rest_0_.rest_12_, ...), custom_call_target="tpu_custom_call" | custom-call | flops 32212254720 | bytes 293601280 | tf_op jit(solution)/shard_map/score/pallas_call | solution.py:145
  163.2 4.3 %matrix.1 = (f32[2,384,1]{2,1,0:T(8,128)S(1)}, bf16[1024,1536]{1,0:T(8,128)(2,1)S(1)}) custom-call(s32[1]{0:T(128)} %bitcast.me_ref, s32[1024,1]{1,0:T(8,128)S(1)} %copy.12.wanted_ref, s32[2,512]{1,0:T(2,128)S(1)} %broadcast_add_fusion.target_ref, bf16[2,384,512]{2,1,0:T(8,128)(2,1)S(1)} %copy-done.30, f32[1,384,512]{2,1,0:T(8,128)} %score.4.rest_0_, ...), custom_call_target="tpu_custom_call" | custom-call | flops 32212254720 | bytes 62914560 | tf_op jit(solution)/shard_map/matrix/pallas_call | solution.py:223
  167.5 10.2 %mix.2 = (bf16[2,256,1024]{2,1,0:T(8,128)(2,1)S(1)}, f32[2,256,1024]{2,1,0:T(8,128)S(1)}, bf16[2,256,1024]{2,1,0:T(8,128)(2,1)S(1)}, f32[2,256,1024]{2,1,0:T(8,128)S(1)}) custom-call(s32[1]{0:T(128)} %bitcast.me_ref, bf16[1024,1536]{1,0:T(8,128)(2,1)S(1)} %get-tuple-element.72.mix_ref, bf16[96,4096]{1,0:T(8,128)(2,1)S(1)} %copy-done.37, ...), custom_call_target="tpu_custom_call" | custom-call | flops 128849018880 | bytes 335544320 | tf_op jit(solution)/shard_map/mix/pallas_call | solution.py:278
  179.6 9.9 %mix.3 = (bf16[2,256,1024]{2,1,0:T(8,128)(2,1)S(1)}, f32[2,256,1024]{2,1,0:T(8,128)S(1)}, bf16[2,256,1024]{2,1,0:T(8,128)(2,1)S(1)}, f32[2,256,1024]{2,1,0:T(8,128)S(1)}) custom-call(s32[1]{0:T(128)} %bitcast.me_ref, bf16[1024,1536]{1,0:T(8,128)(2,1)S(1)} %get-tuple-element.72.mix_ref, bf16[96,4096]{1,0:T(8,128)(2,1)S(1)} %copy-done.37, ...), custom_call_target="tpu_custom_call" | custom-call | flops 128849018880 | bytes 335544320 | tf_op jit(solution)/shard_map/mix/pallas_call | solution.py:278
  189.5 13.8 %collective-permute-done.18 = bf16[2,256,1024]{2,1,0:T(8,128)(2,1)S(1)} collective-permute-done((bf16[2,256,1024]{2,1,0:T(8,128)(2,1)S(1)}, bf16[2,256,1024]{2,1,0:T(8,128)(2,1)S(1)}, u32[]{:S(2)}, u32[]{:S(2)}) %collective-permute-start.18) | collective-permute-done | bytes 1048608 | tf_op jit(solution)/shard_map/ppermute | solution.py:31
  208.6 10.8 %collective-permute-done.22 = bf16[1,256,1024]{2,1,0:T(8,128)(2,1)S(1)} collective-permute-done((bf16[1,256,1024]{2,1,0:T(8,128)(2,1)S(1)}, bf16[1,256,1024]{2,1,0:T(8,128)(2,1)S(1)}, u32[]{:S(2)}, u32[]{:S(2)}) %collective-permute-start.22) | collective-permute-done | bytes 524320 | tf_op jit(solution)/shard_map/ppermute | solution.py:31
  222.7 10.3 %collective-permute-done.24 = bf16[256,1024]{1,0:T(8,128)(2,1)S(1)} collective-permute-done((bf16[256,1024]{1,0:T(8,128)(2,1)S(1)}, bf16[256,1024]{1,0:T(8,128)(2,1)S(1)}, u32[]{:S(2)}, u32[]{:S(2)}) %collective-permute-start.24) | collective-permute-done | bytes 524320 | tf_op jit(solution)/shard_map/ppermute | solution.py:31
  233.1 2.6 collective-permute-start.29
  235.7 5.0 %collective-permute-done.20 = bf16[2,256,1024]{2,1,0:T(8,128)(2,1)S(1)} collective-permute-done((bf16[2,256,1024]{2,1,0:T(8,128)(2,1)S(1)}, bf16[2,256,1024]{2,1,0:T(8,128)(2,1)S(1)}, u32[]{:S(2)}, u32[]{:S(2)}) %collective-permute-start.20) | collective-permute-done | bytes 1048608 | tf_op jit(solution)/shard_map/ppermute | solution.py:31
  240.6 1.8 fusion.15
  244.6 1.8 fusion.14
  250.6 5.6 %collective-permute-done.26 = bf16[1,128,1024]{2,1,0:T(8,128)(2,1)S(1)} collective-permute-done((bf16[1,128,1024]{2,1,0:T(8,128)(2,1)}, bf16[1,128,1024]{2,1,0:T(8,128)(2,1)S(1)}, u32[]{:S(2)}, u32[]{:S(2)}) %collective-permute-start.26) | collective-permute-done | bytes 262176 | tf_op jit(solution)/shard_map/ppermute | solution.py:31
  264.2 4.6 %all-to-all-start = ((f32[8,1,96]{2,1,0:T(1,128)}), f32[8,1,96]{2,1,0:T(1,128)S(1)}, u32[]{:S(2)}, u32[]{:S(2)}) async-start(f32[8,1,96]{2,1,0:T(1,128)} %bitcast.16), calls=%async_computation | async-start | bytes 8192 | tf_op jit(solution)/shard_map/all_to_all | solution.py:438
  270.0 2.0 all-to-all-done
  (202 shorter events, 56.2 us)
Async XLA Ops:
  10.8 21.4 %collective-permute-start = (bf16[96,4096]{1,0:T(8,128)(2,1)S(1)}, bf16[96,4096]{1,0:T(8,128)(2,1)S(1)}, u32[]{:S(2)}, u32[]{:S(2)}) collective-permute-start(bf16[96,4096]{1,0:T(8,128)(2,1)S(1)} %get-tuple-element.50), channel_id=1, source_target_pairs={{0,24},{4,28},{8,16},{12,20},{16,8},{20,12},{24,0},{28,4},{1,25},{... | collective-permute-start | bytes 2359304 | tf_op jit(solution)/shard_map/ppermute | solution.py:31
  12.4 34.8 %collective-permute-start.1 = (bf16[96,4096]{1,0:T(8,128)(2,1)S(1)}, bf16[96,4096]{1,0:T(8,128)(2,1)S(1)}, u32[]{:S(2)}, u32[]{:S(2)}) collective-permute-start(bf16[96,4096]{1,0:T(8,128)(2,1)S(1)} %get-tuple-element.51), channel_id=1, source_target_pairs={{0,28},{4,24},{8,20},{12,16},{16,12},{20,8},{24,4},{28,0},{1,29},{... | collective-permute-start | bytes 2359304 | tf_op jit(solution)/shard_map/ppermute | solution.py:31
  13.0 56.4 %collective-permute-start.5 = (bf16[96,4096]{1,0:T(8,128)(2,1)}, bf16[96,4096]{1,0:T(8,128)(2,1)S(1)}, u32[]{:S(2)}, u32[]{:S(2)}) collective-permute-start(bf16[96,4096]{1,0:T(8,128)(2,1)} %get-tuple-element.58), channel_id=1, source_target_pairs={{0,24},{4,28},{8,16},{12,20},{16,8},{20,12},{24,0},{28,4},{1,25},{... | collective-permute-start | bytes 2359304 | tf_op jit(solution)/shard_map/ppermute | solution.py:31
  14.4 66.6 %collective-permute-start.6 = (bf16[96,4096]{1,0:T(8,128)(2,1)}, bf16[96,4096]{1,0:T(8,128)(2,1)}, u32[]{:S(2)}, u32[]{:S(2)}) collective-permute-start(bf16[96,4096]{1,0:T(8,128)(2,1)} %get-tuple-element.59), channel_id=1, source_target_pairs={{0,28},{4,24},{8,20},{12,16},{16,12},{20,8},{24,4},{28,0},{1,29},{... | collective-permute-start | bytes 2359304 | tf_op jit(solution)/shard_map/ppermute | solution.py:31
  50.0 34.4 %collective-permute-start.2 = (bf16[512,4096]{1,0:T(8,128)(2,1)}, bf16[512,4096]{1,0:T(8,128)(2,1)}, u32[]{:S(2)}, u32[]{:S(2)}) collective-permute-start(bf16[512,4096]{1,0:T(8,128)(2,1)} %partner_columns.1), channel_id=1, source_target_pairs={{0,4},{4,0},{8,12},{12,8},{16,20},{20,16},{24,28},{28,24},{1,5},{5... | collective-permute-start | bytes 12582920 | tf_op jit(solution)/shard_map/ppermute | solution.py:31
  68.9 13.4 %collective-permute-start.3 = (bf16[96,4096]{1,0:T(8,128)(2,1)}, bf16[96,4096]{1,0:T(8,128)(2,1)}, u32[]{:S(2)}, u32[]{:S(2)}) collective-permute-start(bf16[96,4096]{1,0:T(8,128)(2,1)} %get-tuple-element.55), channel_id=1, source_target_pairs={{0,4},{4,0},{8,12},{12,8},{16,20},{20,16},{24,28},{28,24},{1,5},{5... | collective-permute-start | bytes 2359304 | tf_op jit(solution)/shard_map/ppermute | solution.py:31
  68.9 15.5 %collective-permute-start.4 = (bf16[96,4096]{1,0:T(8,128)(2,1)}, bf16[96,4096]{1,0:T(8,128)(2,1)}, u32[]{:S(2)}, u32[]{:S(2)}) collective-permute-start(bf16[96,4096]{1,0:T(8,128)(2,1)} %get-tuple-element.57), channel_id=1, source_target_pairs={{0,4},{4,0},{8,12},{12,8},{16,20},{20,16},{24,28},{28,24},{1,5},{5... | collective-permute-start | bytes 2359304 | tf_op jit(solution)/shard_map/ppermute | solution.py:31
  69.4 30.2 %collective-permute-start.8 = (bf16[96,4096]{1,0:T(8,128)(2,1)}, bf16[96,4096]{1,0:T(8,128)(2,1)S(1)}, u32[]{:S(2)}, u32[]{:S(2)}) collective-permute-start(bf16[96,4096]{1,0:T(8,128)(2,1)} %copy-done.34), channel_id=1, source_target_pairs={{0,8},{4,12},{8,0},{12,4},{16,24},{20,28},{24,16},{28,20},{1,9},{5... | collective-permute-start | bytes 2359304 | tf_op jit(solution)/shard_map/ppermute | solution.py:31
  81.0 33.7 %collective-permute-start.9 = (bf16[96,4096]{1,0:T(8,128)(2,1)}, bf16[96,4096]{1,0:T(8,128)(2,1)S(1)}, u32[]{:S(2)}, u32[]{:S(2)}) collective-permute-start(bf16[96,4096]{1,0:T(8,128)(2,1)} %copy-done.33), channel_id=1, source_target_pairs={{0,12},{4,8},{8,4},{12,0},{16,28},{20,24},{24,20},{28,16},{1,13},{... | collective-permute-start | bytes 2359304 | tf_op jit(solution)/shard_map/ppermute | solution.py:31
  82.3 32.4 %collective-permute-start.10 = (bf16[96,4096]{1,0:T(8,128)(2,1)}, bf16[96,4096]{1,0:T(8,128)(2,1)S(1)}, u32[]{:S(2)}, u32[]{:S(2)}) collective-permute-start(bf16[96,4096]{1,0:T(8,128)(2,1)} %copy-done.32), channel_id=1, source_target_pairs={{0,16},{4,20},{8,24},{12,28},{16,0},{20,4},{24,8},{28,12},{1,17},{... | collective-permute-start | bytes 2359304 | tf_op jit(solution)/shard_map/ppermute | solution.py:31
  84.4 34.8 %collective-permute-start.11 = (bf16[96,4096]{1,0:T(8,128)(2,1)}, bf16[96,4096]{1,0:T(8,128)(2,1)S(1)}, u32[]{:S(2)}, u32[]{:S(2)}) collective-permute-start(bf16[96,4096]{1,0:T(8,128)(2,1)} %copy-done.31), channel_id=1, source_target_pairs={{0,20},{4,16},{8,28},{12,24},{16,4},{20,0},{24,12},{28,8},{1,21},{... | collective-permute-start | bytes 2359304 | tf_op jit(solution)/shard_map/ppermute | solution.py:31
  84.4 49.0 %collective-permute-start.12 = (bf16[96,4096]{1,0:T(8,128)(2,1)S(1)}, bf16[96,4096]{1,0:T(8,128)(2,1)S(1)}, u32[]{:S(2)}, u32[]{:S(2)}) collective-permute-start(bf16[96,4096]{1,0:T(8,128)(2,1)S(1)} %get-tuple-element.66), channel_id=1, source_target_pairs={{0,8},{4,12},{8,0},{12,4},{16,24},{20,28},{24,16},{28,20},{1,9},{5... | collective-permute-start | bytes 2359304 | tf_op jit(solution)/shard_map/ppermute | solution.py:31
  99.7 48.3 %collective-permute-start.13 = (bf16[96,4096]{1,0:T(8,128)(2,1)S(1)}, bf16[96,4096]{1,0:T(8,128)(2,1)S(1)}, u32[]{:S(2)}, u32[]{:S(2)}) collective-permute-start(bf16[96,4096]{1,0:T(8,128)(2,1)S(1)} %copy-done.28), channel_id=1, source_target_pairs={{0,12},{4,8},{8,4},{12,0},{16,28},{20,24},{24,20},{28,16},{1,13},{... | collective-permute-start | bytes 2359304 | tf_op jit(solution)/shard_map/ppermute | solution.py:31
  114.7 33.3 %collective-permute-start.14 = (bf16[96,4096]{1,0:T(8,128)(2,1)S(1)}, bf16[96,4096]{1,0:T(8,128)(2,1)S(1)}, u32[]{:S(2)}, u32[]{:S(2)}) collective-permute-start(bf16[96,4096]{1,0:T(8,128)(2,1)S(1)} %copy-done.26), channel_id=1, source_target_pairs={{0,16},{4,20},{8,24},{12,28},{16,0},{20,4},{24,8},{28,12},{1,17},{... | collective-permute-start | bytes 2359304 | tf_op jit(solution)/shard_map/ppermute | solution.py:31
  114.7 38.2 %collective-permute-start.15 = (bf16[96,4096]{1,0:T(8,128)(2,1)S(1)}, bf16[96,4096]{1,0:T(8,128)(2,1)S(1)}, u32[]{:S(2)}, u32[]{:S(2)}) collective-permute-start(bf16[96,4096]{1,0:T(8,128)(2,1)S(1)} %copy-done.24), channel_id=1, source_target_pairs={{0,20},{4,16},{8,28},{12,24},{16,4},{20,0},{24,12},{28,8},{1,21},{... | collective-permute-start | bytes 2359304 | tf_op jit(solution)/shard_map/ppermute | solution.py:31
  119.2 6.4 %collective-permute-start.7 = (f32[2,384,512]{2,1,0:T(8,128)S(1)}, f32[2,384,512]{2,1,0:T(8,128)S(1)}, u32[]{:S(2)}, u32[]{:S(2)}) collective-permute-start(f32[2,384,512]{2,1,0:T(8,128)S(1)} %score.3.mine_ref), channel_id=1, source_target_pairs={{0,4},{4,0},{8,12},{12,8},{16,20},{20,16},{24,28},{28,24},{1,5},{5... | collective-permute-start | bytes 4718600 | tf_op jit(solution)/shard_map/ppermute | solution.py:31
  125.7 35.3 %collective-permute-start.16 = (f32[1,384,512]{2,1,0:T(8,128)}, f32[1,384,512]{2,1,0:T(8,128)}, u32[]{:S(2)}, u32[]{:S(2)}) collective-permute-start(f32[1,384,512]{2,1,0:T(8,128)} %score.4.rest_0_), channel_id=1, source_target_pairs={{0,4},{4,0},{8,12},{12,8},{16,20},{20,16},{24,28},{28,24},{1,5},{5... | collective-permute-start | bytes 2359304 | tf_op jit(solution)/shard_map/ppermute | solution.py:31
  159.0 2.7 collective-permute-start.17
  177.8 25.5 %collective-permute-start.18 = (bf16[2,256,1024]{2,1,0:T(8,128)(2,1)S(1)}, bf16[2,256,1024]{2,1,0:T(8,128)(2,1)S(1)}, u32[]{:S(2)}, u32[]{:S(2)}) collective-permute-start(bf16[2,256,1024]{2,1,0:T(8,128)(2,1)S(1)} %get-tuple-element.77), channel_id=1, source_target_pairs={{0,8},{4,12},{8,0},{12,4},{16,24},{20,28},{24,16},{28,20},{1,9},{5... | collective-permute-start | bytes 3145736 | tf_op jit(solution)/shard_map/ppermute | solution.py:31
  178.3 25.1 %collective-permute-start.19 = (bf16[2,256,1024]{2,1,0:T(8,128)(2,1)S(1)}, bf16[2,256,1024]{2,1,0:T(8,128)(2,1)S(1)}, u32[]{:S(2)}, u32[]{:S(2)}) collective-permute-start(bf16[2,256,1024]{2,1,0:T(8,128)(2,1)S(1)} %get-tuple-element.78), channel_id=1, source_target_pairs={{0,16},{4,20},{8,24},{12,28},{16,0},{20,4},{24,8},{28,12},{1,17},{... | collective-permute-start | bytes 3145736 | tf_op jit(solution)/shard_map/ppermute | solution.py:31
  204.5 14.9 %collective-permute-start.22 = (bf16[1,256,1024]{2,1,0:T(8,128)(2,1)S(1)}, bf16[1,256,1024]{2,1,0:T(8,128)(2,1)S(1)}, u32[]{:S(2)}, u32[]{:S(2)}) collective-permute-start(bf16[1,256,1024]{2,1,0:T(8,128)(2,1)S(1)} %slice.179), channel_id=1, source_target_pairs={{0,16},{4,20},{8,24},{12,28},{16,0},{20,4},{24,8},{28,12},{1,17},{... | collective-permute-start | bytes 1572872 | tf_op jit(solution)/shard_map/ppermute | solution.py:31
  205.6 14.9 %collective-permute-start.23 = (bf16[1,256,1024]{2,1,0:T(8,128)(2,1)S(1)}, bf16[1,256,1024]{2,1,0:T(8,128)(2,1)S(1)}, u32[]{:S(2)}, u32[]{:S(2)}) collective-permute-start(bf16[1,256,1024]{2,1,0:T(8,128)(2,1)S(1)} %slice.178), channel_id=1, source_target_pairs={{0,8},{4,12},{8,0},{12,4},{16,24},{20,28},{24,16},{28,20},{1,9},{5... | collective-permute-start | bytes 1572872 | tf_op jit(solution)/shard_map/ppermute | solution.py:31
  207.1 33.6 %collective-permute-start.20 = (bf16[2,256,1024]{2,1,0:T(8,128)(2,1)S(1)}, bf16[2,256,1024]{2,1,0:T(8,128)(2,1)S(1)}, u32[]{:S(2)}, u32[]{:S(2)}) collective-permute-start(bf16[2,256,1024]{2,1,0:T(8,128)(2,1)S(1)} %get-tuple-element.80), channel_id=1, source_target_pairs={{0,8},{4,12},{8,0},{12,4},{16,24},{20,28},{24,16},{28,20},{1,9},{5... | collective-permute-start | bytes 3145736 | tf_op jit(solution)/shard_map/ppermute | solution.py:31
  207.6 33.0 %collective-permute-start.21 = (bf16[2,256,1024]{2,1,0:T(8,128)(2,1)S(1)}, bf16[2,256,1024]{2,1,0:T(8,128)(2,1)S(1)}, u32[]{:S(2)}, u32[]{:S(2)}) collective-permute-start(bf16[2,256,1024]{2,1,0:T(8,128)(2,1)S(1)} %get-tuple-element.81), channel_id=1, source_target_pairs={{0,16},{4,20},{8,24},{12,28},{16,0},{20,4},{24,8},{28,12},{1,17},{... | collective-permute-start | bytes 3145736 | tf_op jit(solution)/shard_map/ppermute | solution.py:31
  220.9 12.0 %collective-permute-start.24 = (bf16[256,1024]{1,0:T(8,128)(2,1)S(1)}, bf16[256,1024]{1,0:T(8,128)(2,1)S(1)}, u32[]{:S(2)}, u32[]{:S(2)}) collective-permute-start(bf16[256,1024]{1,0:T(8,128)(2,1)S(1)} %pad_maximum_fusion.1), channel_id=1, source_target_pairs={{0,1},{1,0},{2,3},{3,2},{4,5},{5,4},{6,7},{7,6},{8,9},{9,8},{10,11... | collective-permute-start | bytes 1572872 | tf_op jit(solution)/shard_map/ppermute | solution.py:31
  233.1 26.0 %collective-permute-start.29 = (bf16[256,1024]{1,0:T(8,128)(2,1)S(1)}, bf16[256,1024]{1,0:T(8,128)(2,1)S(1)}, u32[]{:S(2)}, u32[]{:S(2)}) collective-permute-start(bf16[256,1024]{1,0:T(8,128)(2,1)S(1)} %fusion), channel_id=1, source_target_pairs={{0,2},{1,3},{2,0},{3,1},{4,6},{5,7},{6,4},{7,5},{8,10},{9,11},{10,... | collective-permute-start | bytes 1572872 | tf_op jit(solution)/shard_map/ppermute | solution.py:31
  243.3 7.4 %collective-permute-start.25 = (bf16[1,128,1024]{2,1,0:T(8,128)(2,1)}, bf16[1,128,1024]{2,1,0:T(8,128)(2,1)S(1)}, u32[]{:S(2)}, u32[]{:S(2)}) collective-permute-start(bf16[1,128,1024]{2,1,0:T(8,128)(2,1)} %get-tuple-element.104), channel_id=1, source_target_pairs={{0,16},{4,20},{8,24},{12,28},{16,0},{20,4},{24,8},{28,12},{1,17},{... | collective-permute-start | bytes 786440 | tf_op jit(solution)/shard_map/ppermute | solution.py:31
  247.2 9.1 %collective-permute-start.26 = (bf16[1,128,1024]{2,1,0:T(8,128)(2,1)}, bf16[1,128,1024]{2,1,0:T(8,128)(2,1)S(1)}, u32[]{:S(2)}, u32[]{:S(2)}) collective-permute-start(bf16[1,128,1024]{2,1,0:T(8,128)(2,1)} %get-tuple-element.102), channel_id=1, source_target_pairs={{0,8},{4,12},{8,0},{12,4},{16,24},{20,28},{24,16},{28,20},{1,9},{5... | collective-permute-start | bytes 786440 | tf_op jit(solution)/shard_map/ppermute | solution.py:31
  248.6 8.8 %collective-permute-start.27 = (bf16[1,128,1024]{2,1,0:T(8,128)(2,1)}, bf16[1,128,1024]{2,1,0:T(8,128)(2,1)S(1)}, u32[]{:S(2)}, u32[]{:S(2)}) collective-permute-start(bf16[1,128,1024]{2,1,0:T(8,128)(2,1)} %get-tuple-element.103), channel_id=1, source_target_pairs={{0,16},{4,20},{8,24},{12,28},{16,0},{20,4},{24,8},{28,12},{1,17},{... | collective-permute-start | bytes 786440 | tf_op jit(solution)/shard_map/ppermute | solution.py:31
  249.4 9.7 %collective-permute-start.28 = (bf16[1,128,1024]{2,1,0:T(8,128)(2,1)}, bf16[1,128,1024]{2,1,0:T(8,128)(2,1)S(1)}, u32[]{:S(2)}, u32[]{:S(2)}) collective-permute-start(bf16[1,128,1024]{2,1,0:T(8,128)(2,1)} %get-tuple-element.101), channel_id=1, source_target_pairs={{0,8},{4,12},{8,0},{12,4},{16,24},{20,28},{24,16},{28,20},{1,9},{5... | collective-permute-start | bytes 786440 | tf_op jit(solution)/shard_map/ppermute | solution.py:31
  261.4 12.6 %collective-permute-start.30 = (bf16[256,1024]{1,0:T(8,128)(2,1)S(1)}, bf16[256,1024]{1,0:T(8,128)(2,1)S(1)}, u32[]{:S(2)}, u32[]{:S(2)}) collective-permute-start(bf16[256,1024]{1,0:T(8,128)(2,1)S(1)} %fusion.13), channel_id=1, source_target_pairs={{0,1},{1,0},{2,3},{3,2},{4,5},{5,4},{6,7},{7,6},{8,9},{9,8},{10,11... | collective-permute-start | bytes 1572872 | tf_op jit(solution)/shard_map/ppermute | solution.py:31
  264.2 7.7 %all-to-all-start = ((f32[8,1,96]{2,1,0:T(1,128)}), f32[8,1,96]{2,1,0:T(1,128)S(1)}, u32[]{:S(2)}, u32[]{:S(2)}) async-start(f32[8,1,96]{2,1,0:T(1,128)} %bitcast.16), calls=%async_computation | async-start | bytes 8192 | tf_op jit(solution)/shard_map/all_to_all | solution.py:438
  (49 other events, 657.9 us)
